TPU v7x, 512 devices: a whole 4x8x8 slice. The times are simulated.
512 devices in a mesh: ctx: 16 (over y, core), dp: 32 (over z, x).
Axes of the slice: x: 4, y: 8, z: 8, core: 2. Of those that a mesh axis runs over, the one named last changes fastest.
Arguments:
- queries: bfloat16 [131072, 256], P(('dp', 'ctx')), parts along dimension 0, may hold values from -6 to 6
- key_states: bfloat16 [131072, 128], P(('dp', 'ctx')), parts along dimension 0, may hold values from -6 to 6
- value_states: bfloat16 [131072, 128], P(('dp', 'ctx')), parts along dimension 0, may hold values from -6 to 6
- attn_out: bfloat16 [131072, 256], P(('dp', 'ctx')), parts along dimension 0, may hold values from -0.59765625 to 0.59765625
- grad_out: bfloat16 [131072, 256], P(('dp', 'ctx')), parts along dimension 0, may hold values from -6 to 6
- log_norm: float32 [2, 131072], P(None, ('dp', 'ctx')), parts along dimension 1, may hold values from 1 to 4
- doc_lengths: int32 [128], P('dp'), parts along dimension 0, may hold values from 1 to 2048, 4096 in all
Outputs:
- grad_query: bfloat16 [131072, 256], P(('dp', 'ctx')), parts along dimension 0
- grad_key: bfloat16 [131072, 128], P(('dp', 'ctx')), parts along dimension 0
- grad_value: bfloat16 [131072, 128], P(('dp', 'ctx')), parts along dimension 0
There are 32 independent parts, one for each index of `dp`. A program takes and returns all parts, laid end to end along the dimension named above; each array names one. Nothing has to cross between parts.
Inputs may be any that keep to these rules, and one draw needn't show every extreme that they name: `doc_lengths`: lengths of the documents packed in the sequence, in order of position; they sum to 4096 and the longest is exactly 2048.
All inputs are finite; a program needn't handle non-finite values.
Results may differ from a plain program's by a relative error of at most 0.0051.
Values may be sent and summed in bfloat16 or wider, within the bound.
No kernel may reach another device: no remote copies, remote signals or barrier semaphores. Data moves between devices by JAX's collectives and lax.ppermute only.
A program may use at most 64 MiB of HBM per device.

v0:
```python
import math

import jax
import jax.numpy as jnp
from jax import lax
from jax.sharding import PartitionSpec as P


def doc_index(doc_ends, positions):
    return jnp.sum((doc_ends[None, :] <= positions[:, None]).astype(jnp.int32), axis=1)


def doc_at(doc_ends, position):
    return doc_index(doc_ends, jnp.reshape(position, (1,)))[0]


def tile_grads(
    queries, grad_out, log_norm, row_delta, q_pos, key_states, value_states, k_pos, doc_ends
):
    q_count = queries.shape[0]
    head_count = log_norm.shape[0]
    head_dim = key_states.shape[1]
    scaling = head_dim ** (-0.5)
    query_heads = queries.reshape(q_count, head_count, head_dim)
    grad_heads = grad_out.reshape(q_count, head_count, head_dim)
    scores = (
        jnp.einsum("qhe,ke->hqk", query_heads, key_states, preferred_element_type=jnp.float32)
        * scaling
    )
    allowed = (doc_index(doc_ends, q_pos)[:, None] == doc_index(doc_ends, k_pos)[None, :]) & (
        k_pos[None, :] <= q_pos[:, None]
    )
    attn_prob = jnp.where(allowed[None], jnp.exp(scores - log_norm[:, :, None]), 0.0)
    grad_prob = jnp.einsum(
        "qhe,ke->hqk", grad_heads, value_states, preferred_element_type=jnp.float32
    )
    dscore = (attn_prob * (grad_prob - row_delta[:, :, None]) * scaling).astype(jnp.bfloat16)
    return (dscore, attn_prob.astype(jnp.bfloat16), query_heads, grad_heads)


def full_tile(
    queries, grad_out, log_norm, row_delta, own_pos, key_block, value_block, key_first, doc_ends
):
    key_len = key_block.shape[0]
    key_pos = key_first + jnp.arange(key_len, dtype=jnp.int32)
    dscore, prob_half, query_heads, grad_heads = tile_grads(
        queries, grad_out, log_norm, row_delta, own_pos, key_block, value_block, key_pos, doc_ends
    )
    update = jnp.einsum("hqk,ke->qhe", dscore, key_block, preferred_element_type=jnp.float32)
    grad_keys = jnp.einsum("hqk,qhe->ke", dscore, query_heads, preferred_element_type=jnp.float32)
    grad_values = jnp.einsum(
        "hqk,qhe->ke", prob_half, grad_heads, preferred_element_type=jnp.float32
    )
    return (update.reshape(queries.shape[0], -1), jnp.concatenate([grad_keys, grad_values], axis=1))


def body(queries, key_states, value_states, attn_out, grad_out, log_norm, doc_lengths):
    q_count = queries.shape[0]
    head_count = log_norm.shape[0]
    head_dim = key_states.shape[1]
    ctx_count = lax.axis_size("ctx")
    seq_len = q_count * ctx_count
    doc_ends = jnp.cumsum(doc_lengths)
    first_pos = lax.axis_index("ctx") * q_count
    last_pos = first_pos + q_count - 1
    own_pos = first_pos + jnp.arange(q_count, dtype=jnp.int32)
    first_doc = doc_at(doc_ends, first_pos)
    row_delta = jnp.sum(
        (grad_out.astype(jnp.float32) * attn_out.astype(jnp.float32)).reshape(
            q_count, head_count, head_dim
        ),
        axis=2,
    ).T
    zero_rows = jnp.zeros((q_count, head_count * head_dim), jnp.float32)
    key_all, value_all = (
        lax.all_gather(key_states, "ctx", axis=0, tiled=True),
        lax.all_gather(value_states, "ctx", axis=0, tiled=True),
    )
    block_len = math.gcd(seq_len, 512)

    def key_step(block_id, carry):
        key_first = block_id * block_len
        key_block = lax.dynamic_slice_in_dim(key_all, key_first, block_len, 0)
        value_block = lax.dynamic_slice_in_dim(value_all, key_first, block_len, 0)

        def compute(unused):
            return full_tile(
                queries,
                grad_out,
                log_norm,
                row_delta,
                own_pos,
                key_block,
                value_block,
                key_first,
                doc_ends,
            )

        def skipped(unused):
            return (zero_rows, jnp.zeros((block_len, 2 * head_dim), jnp.float32))

        needed = (key_first <= last_pos) & (
            doc_at(doc_ends, key_first + block_len - 1) >= first_doc
        )
        update, block_terms = lax.cond(needed, compute, skipped, key_first)
        return (
            carry[0] + update,
            lax.dynamic_update_slice_in_dim(carry[1], block_terms, key_first, 0),
        )

    start_terms = jnp.zeros((seq_len, 2 * head_dim), jnp.float32)
    grad_rows, terms_all = lax.fori_loop(
        0, seq_len // block_len, key_step, (zero_rows, start_terms)
    )
    grad_query = grad_rows.astype(jnp.bfloat16)
    summed = lax.psum_scatter(terms_all, "ctx", scatter_dimension=0, tiled=True)
    grad_key = summed[:, :head_dim].astype(jnp.bfloat16)
    grad_value = summed[:, head_dim:].astype(jnp.bfloat16)
    return (grad_query, grad_key, grad_value)


def solution(mesh):
    placed = (
        P(("dp", "ctx"), None),
        P(("dp", "ctx"), None),
        P(("dp", "ctx"), None),
        P(("dp", "ctx"), None),
        P(("dp", "ctx"), None),
        P(None, ("dp", "ctx")),
        P("dp"),
    )
    return jax.shard_map(
        body,
        mesh=mesh,
        in_specs=placed,
        out_specs=(P(("dp", "ctx"), None), P(("dp", "ctx"), None), P(("dp", "ctx"), None)),
        check_vma=False,
    )
```

profile of v0, /device:TPU:1, one launch (start us, length us, event | category | flops | bytes accessed | tf_op | source)
XLA Modules:
  0.0 217.9 jit_solution(10486175971852933666)
XLA Ops:
  7.2 0.7 all-gather.3.cloned.1.call-update
  8.0 0.7 all-gather.5.cloned.1.call-update
  8.7 0.8 reduce-window.4
  9.6 1.0 copy.37
  10.6 1.0 copy.38
  11.6 1.0 convert_multiply_fusion
  12.6 0.1 reshape.133
  12.7 0.3 reduce_sum.52
  13.1 0.7 fusion.22
  13.8 43.1 %all-gather.3.cloned.1.call-done = bf16[4096,128]{1,0:T(8,128)(2,1)} async-done(((bf16[256,128]{1,0:T(8,128)(2,1)}), bf16[4096,128]{1,0:T(8,128)(2,1)}) %all-gather.3.cloned.1.call-update) | async-done | bytes 1048592 | tf_op jit(solution)/shard_map/all_gather | solution.py:76
  56.9 42.0 %all-gather.5.cloned.1.call-done = bf16[4096,128]{1,0:T(8,128)(2,1)} async-done(((bf16[256,128]{1,0:T(8,128)(2,1)}), bf16[4096,128]{1,0:T(8,128)(2,1)}) %all-gather.5.cloned.1.call-update) | async-done | bytes 1048592 | tf_op jit(solution)/shard_map/all_gather | solution.py:77
  98.9 2.2 %broadcast_in_dim.42.clone = f32[4096,256]{1,0:T(8,128)} broadcast(f32[]{:T(128)} %constant.95.clone.1), dimensions={} | broadcast | bytes 4194308 | tf_op jit(solution)/shard_map/broadcast_in_dim | solution.py:111
  101.1 29.6 %while.20 = (s32[]{:T(128)}, f32[256,256]{0,1:T(8,128)S(1)}, f32[4096,256]{1,0:T(8,128)}, s32[]{:T(128)}, s32[4]{0:T(128)S(1)}, /*index=5*/s32[]{:T(128)}, bf16[...) while((s32[]{:T(128)}, f32[256,256]{0,1:T(8,128)S(1)}, ...), condition=%wide.region_9.10_spmd.clone, body=%wide.region_3.9_spmd.clone.sunk | while | flops 338306080 | bytes 10640819 | solution.py:112
  101.1 0.7 fusion.31
  103.0 4.7 %conditional.3 = (f32[256,256]{0,1:T(8,128)S(1)}, f32[512,256]{0,1:T(8,128)S(1)}) conditional(s32[]{:T(128)} %convert_element_type.94, () %tuple.77, (s32[4]{0:T(128)S(1)}, s32[]{:T(128)}, s32[]{:T(128)}, bf16[4096,128]{1,0:T(8,128)(2,1)}, s32[]{:T(128)}, /*index=5*/bf16[256,256]{0,1:T(8,128)(2,1)S(1)}, f32[2,256]{1,0:T(2,128)S(1)}, ...), branch_computations={%region_5.5_spmd, %region_6.8_spmd} | conditional | flops 338174976 | bytes 7755320 | solution.py:105
  103.2 0.2 compare_and_fusion
  103.4 1.3 fusion.6
  104.7 1.2 fusion.9
  105.9 0.3 convolution_bitcast_fusion.1
  106.2 1.2 fusion.12
  107.4 0.3 convolution_bitcast_fusion.2
  107.8 0.2 copy.53
  108.0 0.8 constant_dynamic-update-slice_fusion.2
  108.8 0.7 fusion.31
  110.9 0.2 copy.53
  111.1 0.9 constant_dynamic-update-slice_fusion.2
  112.0 0.7 fusion.31
  114.0 0.2 copy.53
  114.3 0.9 constant_dynamic-update-slice_fusion.2
  115.1 0.7 fusion.31
  117.2 0.2 copy.53
  117.4 0.9 constant_dynamic-update-slice_fusion.2
  118.2 0.7 fusion.31
  120.3 0.2 copy.53
  120.5 0.8 constant_dynamic-update-slice_fusion.2
  121.4 0.7 fusion.31
  123.4 0.2 copy.53
  123.6 0.9 constant_dynamic-update-slice_fusion.2
  124.5 0.7 fusion.31
  126.6 0.2 copy.53
  126.8 0.8 constant_dynamic-update-slice_fusion.2
  127.6 0.7 fusion.31
  129.7 0.2 copy.53
  129.9 0.9 constant_dynamic-update-slice_fusion.2
  130.7 0.8 copy.40
  131.5 78.3 %reduce-scatter.2.cloned.1.call-done = f32[256,256]{1,0:T(8,128)} async-done(((f32[4096,256]{1,0:T(8,128)}), f32[256,256]{1,0:T(8,128)}) %reduce-scatter.2.cloned.1.call-update) | async-done | bytes 262160 | tf_op jit(solution)/shard_map/reduce_scatter | solution.py:116
  209.8 1.0 convert.4
  210.7 0.7 fusion.23
  (50 shorter events, 2.2 us)
Async XLA Ops:
  7.2 93.9 %copy-start = (f32[2,256]{1,0:T(2,128)S(1)}, f32[2,256]{1,0:T(2,128)}, u32[]{:S(2)}) copy-start(f32[2,256]{1,0:T(2,128)} %param.16) | copy-start | bytes 6148
  7.2 49.7 %all-gather.3.cloned.1.call-start = ((), (), s32[]{:S(2)}) async-start(), calls=%async_computation.1 | async-start | bytes 1114112 | tf_op jit(solution)/shard_map/all_gather | solution.py:76
  7.9 91.0 %all-gather.5.cloned.1.call-start = ((), (), s32[]{:S(2)}) async-start(), calls=%async_computation.2 | async-start | bytes 1114112 | tf_op jit(solution)/shard_map/all_gather | solution.py:77
  8.7 201.1 %reduce-scatter.2.cloned.1.call-start = ((), (), s32[]{:S(2)}) async-start(), calls=%async_computation.3 | async-start | bytes 4456448 | tf_op jit(solution)/shard_map/reduce_scatter | solution.py:116
Sparse Core Ops, SparseCore 0:
  10.1 46.6 all-gather.2
  59.0 39.8 all-gather.4
  130.9 78.8 reduce-scatter.1
where the time goes:
time: 220 us; the launch traced here: 218 us
  waiting for transfers between devices  165 us (75%)
  local copies, waits for them, and re-layouts  14.7 us (7%)
  between operations  13.8 us (6%)
  loops' own time  10.3 us (5%)
  other arithmetic  10 us (5%)
  matrix products  4.24 us (2%)
    reduce_scatter x1, waiting for transfers between devices, body(): summed = lax.psum_scatter(terms_all, 'ctx', scatter_dimension=0, tiled=True)  78.3 us
    all_gather x1, waiting for transfers between devices, body(): lax.all_gather(key_states, 'ctx', axis=0, tiled=True)  43.1 us
    all_gather x1, waiting for transfers between devices, body(): lax.all_gather(value_states, 'ctx', axis=0, tiled=True)  42 us
    another operation x1, loops' own time, body(): lax.fori_loop(0, seq_len // block_len, key_step, (zero_rows, start_terms))  10 us
    dynamic_update_slice x16, local copies, waits for them, and re-layouts, key_step(): lax.dynamic_update_slice_in_dim(carry[1], block_terms, key_first, 0)  8.33 us
    reduce_sum x11, other arithmetic, doc_index(): jnp.sum((doc_ends[None, :] <= positions[:, None]).astype(jnp.int32), axis=1)  6.08 us
  transfers between devices with their start and end apart: 3, of which 3 were waited for; matrix products, arithmetic and copies ran while one was open for 3% of the time, Pallas kernels for 0%

commit v1 on v0

v1 whole, which is shorter than its diff:
```python
import functools
import math

import jax
import jax.numpy as jnp
from jax import lax
from jax.experimental import pallas as pl
from jax.experimental.pallas import tpu as pltpu
from jax.sharding import PartitionSpec as P

LOG2E = math.log2(math.e)
STAT_ROWS = 16


def split3(value):
    high = value.astype(jnp.bfloat16)
    rest = value - high.astype(jnp.float32)
    mid = rest.astype(jnp.bfloat16)
    low = (rest - mid.astype(jnp.float32)).astype(jnp.bfloat16)
    return high, mid, low


def prep_kernel(q_ref, go_ref, out_ref, norm_ref, k_ref, v_ref, pay_ref, kv_ref):
    rows, width = q_ref.shape
    heads = norm_ref.shape[0]
    head_dim = width // heads
    kv_ref[:, :head_dim] = k_ref[...]
    kv_ref[:, head_dim:] = v_ref[...]
    pay_ref[:rows, :width] = q_ref[...]
    pay_ref[:rows, width:] = go_ref[...]
    product = go_ref[...].astype(jnp.float32) * out_ref[...].astype(jnp.float32)
    product_t = product.T
    stats = []
    for h in range(heads):
        delta = jnp.sum(product_t[h * head_dim : (h + 1) * head_dim], axis=0, keepdims=True)
        stats += list(split3(norm_ref[h : h + 1, :] * LOG2E)) + list(split3(delta))
    stats += [jnp.zeros((1, rows), jnp.bfloat16)] * (STAT_ROWS - len(stats))
    table = jnp.concatenate([s.astype(jnp.float32) for s in stats], axis=0)
    pay_ref[rows:, :rows] = table.astype(jnp.bfloat16)
    pay_ref[rows:, rows:] = jnp.zeros((STAT_ROWS, pay_ref.shape[1] - rows), jnp.bfloat16)


class Query:
    def __init__(self, pay_ref, heads, first, lens_ref):
        rows = pay_ref.shape[0] - STAT_ROWS
        width = pay_ref.shape[1] // 2
        e = width // heads
        self.heads, self.rows, self.e = heads, rows, e
        self.q = [pay_ref[:rows, h * e : (h + 1) * e] for h in range(heads)]
        self.go = [pay_ref[:rows, width + h * e : width + (h + 1) * e] for h in range(heads)]
        table = pay_ref[rows:, :rows].astype(jnp.float32)
        row = lambda i: table[i : i + 1]
        self.norm = [row(6 * h) + row(6 * h + 1) + row(6 * h + 2) for h in range(heads)]
        self.delta = [row(6 * h + 3) + row(6 * h + 4) + row(6 * h + 5) for h in range(heads)]
        self.pos = first + lax.broadcasted_iota(jnp.int32, (1, rows), 1)
        self.start = jnp.zeros((1, rows), jnp.int32)
        end = jnp.int32(0)
        for d in range(lens_ref.shape[0]):
            end = end + lens_ref[d]
            self.start = jnp.where(end <= self.pos, end, self.start)


def tile(query, h, k_block, v_block, k_first, causal):
    contract = (((1,), (1,)), ((), ()))
    scaling = query.e ** (-0.5)
    scores = lax.dot_general(k_block, query.q[h], contract, preferred_element_type=jnp.float32)
    grads = lax.dot_general(v_block, query.go[h], contract, preferred_element_type=jnp.float32)
    k_pos = k_first + lax.broadcasted_iota(jnp.int32, (k_block.shape[0], 1), 0)
    allowed = k_pos >= query.start
    if causal:
        allowed = allowed & (k_pos <= query.pos)
    prob = jnp.where(allowed, jnp.exp2(scores * (scaling * LOG2E) - query.norm[h]), 0.0)
    dscore = (prob * (grads - query.delta[h]) * scaling).astype(jnp.bfloat16)
    return prob.astype(jnp.bfloat16), dscore


def key_terms(query, k_block, v_block, k_first, causal, dqt):
    dk = dv = None
    for h in range(query.heads):
        prob, dscore = tile(query, h, k_block, v_block, k_first, causal)
        dv_h = jnp.dot(prob, query.go[h], preferred_element_type=jnp.float32)
        dk_h = jnp.dot(dscore, query.q[h], preferred_element_type=jnp.float32)
        dv = dv_h if dv is None else dv + dv_h
        dk = dk_h if dk is None else dk + dk_h
        dq_h = lax.dot_general(
            k_block, dscore, (((0,), (0,)), ((), ())), preferred_element_type=jnp.float32
        )
        dqt[h] = dq_h if dqt[h] is None else dqt[h] + dq_h
    return dk, dv


def place():
    index = lax.axis_index("ctx")
    return index, index // 2, lax.rem(index, 2)


def block_start(chip, back, chips, rows):
    behind = chip - back
    return jnp.where(behind >= 0, behind, -2 * chips) * (2 * rows)


def own_kernel(heads, lens_ref, pay_ref, kv_ref, dqt_ref, keep_ref, give_ref):
    rows = pay_ref.shape[0] - STAT_ROWS
    e = kv_ref.shape[1] // 2
    index, chip, core = place()
    query = Query(pay_ref, heads, index * rows, lens_ref)
    dqt = [None] * heads
    for half in range(2):
        part = pl.ds(half * rows, rows)
        dk, dv = key_terms(
            query, kv_ref[part, :e], kv_ref[part, e:], (2 * chip + half) * rows, True, dqt
        )

        @pl.when(core == half)
        def _():
            keep_ref[:, :e] = dk
            keep_ref[:, e:] = dv

        @pl.when(core != half)
        def _():
            give_ref[:, :e] = dk
            give_ref[:, e:] = dv

    for h in range(heads):
        dqt_ref[h * e : (h + 1) * e, :] = dqt[h]


def near_kernel(heads, chips, lens_ref, pay_ref, kv_ref, dqt_in_ref, dqt_ref, terms_ref):
    rows = pay_ref.shape[0] - STAT_ROWS
    e = kv_ref.shape[1] // 2
    index, chip, core = place()
    query = Query(pay_ref, heads, index * rows, lens_ref)
    dqt = [dqt_in_ref[h * e : (h + 1) * e, :] for h in range(heads)]
    for half in range(2):
        for b in range(2):
            part = pl.ds((half * 2 + b) * rows, rows)
            first = block_start(chip, b + 1, chips, rows) + half * rows
            dk, dv = key_terms(query, kv_ref[part, :e], kv_ref[part, e:], first, False, dqt)
            terms_ref[part, :e] = dk
            terms_ref[part, e:] = dv
    for h in range(heads):
        dqt_ref[h * e : (h + 1) * e, :] = dqt[h]


def far_kernel(heads, chips, lens_ref, pay_ref, kv_ref, terms_ref, dqt_ref, keep_ref, give_ref):
    rows = pay_ref.shape[0] - STAT_ROWS
    e = kv_ref.shape[1] // 2
    index, chip, core = place()
    ahead = chip + 2
    query = Query(pay_ref, heads, (index + 4) * rows, lens_ref)
    query.start = jnp.where(ahead < chips, query.start, 4 * chips * rows)
    dqt = [None] * heads
    for half in range(2):
        for b in range(2):
            part = pl.ds((half * 2 + b) * rows, rows)
            first = block_start(chip, b + 1, chips, rows) + half * rows
            dk, dv = key_terms(query, kv_ref[part, :e], kv_ref[part, e:], first, False, dqt)
            dk = dk + terms_ref[part, :e]
            dv = dv + terms_ref[part, e:]
            out = pl.ds(b * rows, rows)

            @pl.when(core == half)
            def _():
                keep_ref[out, :e] = dk
                keep_ref[out, e:] = dv

            @pl.when(core != half)
            def _():
                give_ref[out, :e] = dk
                give_ref[out, e:] = dv

    for h in range(heads):
        dqt_ref[h * e : (h + 1) * e, :] = dqt[h].astype(jnp.bfloat16)


def pair_kernel(keep_ref, both_ref, near_ref, far_ref):
    count = keep_ref.shape[0]
    rows = count // 2
    _, _, core = place()
    other = both_ref[pl.ds(pl.multiple_of((1 - core) * count, count), count), :]
    total = (keep_ref[...] + other).astype(jnp.bfloat16)
    near_ref[...] = total[:rows]
    far_ref[...] = total[rows:]


def query_kernel(dqt_ref, back_ref, dq_ref):
    dq_ref[...] = (dqt_ref[...] + back_ref[...].astype(jnp.float32)).T.astype(jnp.bfloat16)


def key_kernel(keep_ref, both_ref, near_ref, far_ref, dk_ref, dv_ref):
    rows = keep_ref.shape[0]
    e = keep_ref.shape[1] // 2
    _, _, core = place()
    other = both_ref[pl.ds(pl.multiple_of((1 - core) * rows, rows), rows), :]
    total = keep_ref[...] + other
    total = total + near_ref[...].astype(jnp.float32) + far_ref[...].astype(jnp.float32)
    dk_ref[...] = total[:, :e].astype(jnp.bfloat16)
    dv_ref[...] = total[:, e:].astype(jnp.bfloat16)


def call(kernel, outs, name, flops=0, smem=0):
    def run(*args):
        specs = [pl.BlockSpec(memory_space=pltpu.SMEM)] * smem
        specs += [pl.BlockSpec(memory_space=pltpu.VMEM)] * (len(args) - smem)
        moved = sum(a.size * a.dtype.itemsize for a in args)
        return pl.pallas_call(
            kernel,
            out_shape=[jax.ShapeDtypeStruct(s, d) for s, d in outs],
            in_specs=specs,
            out_specs=[pl.BlockSpec(memory_space=pltpu.VMEM)] * len(outs),
            cost_estimate=pl.CostEstimate(flops=flops, bytes_accessed=moved, transcendentals=0),
            compiler_params=pltpu.CompilerParams(vmem_limit_bytes=32 * 1024 * 1024),
            name=name,
        )(*args)

    return run


def body(queries, key_states, value_states, attn_out, grad_out, log_norm, doc_lengths):
    rows, width = queries.shape
    heads = log_norm.shape[0]
    e = key_states.shape[1]
    count = lax.axis_size("ctx")
    chips = count // 2
    pairs = [[2 * i, 2 * i + 1] for i in range(chips)]
    bf16, f32 = jnp.bfloat16, jnp.float32

    def shift(x, by):
        return lax.ppermute(x, "ctx", [(i, (i + by) % count) for i in range(count)])

    def pair_gather(x):
        return lax.all_gather(x, "ctx", axis=0, tiled=True, axis_index_groups=pairs)

    pay, kv = call(
        prep_kernel, [((rows + STAT_ROWS, 2 * width), bf16), ((rows, 2 * e), bf16)], "prep"
    )(queries, grad_out, attn_out, log_norm, key_states, value_states)
    pay_far = shift(pay, -4)
    kv_far = shift(kv, 4)
    kv_near = shift(kv, 2)
    kv_own = pair_gather(kv)
    unit = 5 * 2 * heads * rows * 2 * rows * e
    dqt, keep_own, give_own = call(
        functools.partial(own_kernel, heads),
        [((width, rows), f32), ((rows, 2 * e), f32), ((rows, 2 * e), f32)],
        "own",
        unit,
        1,
    )(doc_lengths, pay, kv_own)
    kv_back = pair_gather(jnp.concatenate([kv_near, kv_far], axis=0))
    dqt, terms = call(
        functools.partial(near_kernel, heads, chips),
        [((width, rows), f32), ((4 * rows, 2 * e), f32)],
        "near",
        2 * unit,
        1,
    )(doc_lengths, pay, kv_back, dqt)
    dqt_far, keep, give = call(
        functools.partial(far_kernel, heads, chips),
        [((width, rows), bf16), ((2 * rows, 2 * e), f32), ((2 * rows, 2 * e), f32)],
        "far",
        2 * unit,
        1,
    )(doc_lengths, pay_far, kv_back, terms)
    dqt_back = shift(dqt_far, 4)
    both = pair_gather(give)
    to_near, to_far = call(
        pair_kernel, [((rows, 2 * e), bf16), ((rows, 2 * e), bf16)], "pair"
    )(keep, both)
    from_far = shift(to_far, -4)
    from_near = shift(to_near, -2)
    both_own = pair_gather(give_own)
    (grad_query,) = call(query_kernel, [((rows, width), bf16)], "grad_query")(dqt, dqt_back)
    grad_key, grad_value = call(
        key_kernel, [((rows, e), bf16), ((rows, e), bf16)], "grad_key"
    )(keep_own, both_own, from_near, from_far)
    return (grad_query, grad_key, grad_value)


def solution(mesh):
    rows = P(("dp", "ctx"), None)
    placed = (rows, rows, rows, rows, rows, P(None, ("dp", "ctx")), P("dp"))
    return jax.shard_map(
        body, mesh=mesh, in_specs=placed, out_specs=(rows, rows, rows), check_vma=False
    )
```

time: 220 us -> 87.1 us (0.40)
  waiting for transfers between devices: 165 us -> 23.3 us
  starting transfers between devices: 0.11 us -> 20.8 us
  blocking collectives: 0 us -> 11.7 us
  Pallas kernels: 0 us -> 10.4 us
  loops' own time: 10.3 us -> 0 us
  other arithmetic: 10 us -> 0.02 us
  local copies, waits for them, and re-layouts: 14.7 us -> 6.29 us
  matrix products: 4.24 us -> 0 us
    reduce_scatter x1 -> x0, waiting for transfers between devices: 78.3 us -> none  [body(): summed = lax.psum_scatter(terms_all, 'ctx', scatter_dimension=0, tiled=True)]
    all_gather x2 -> x1, waiting for transfers between devices: 85.1 us -> 19.9 us  [pair_gather(): return lax.all_gather(x, 'ctx', axis=0, tiled=True, axis_index_groups=pairs)]
    ppermute x0 -> x6, starting transfers between devices: none -> 20.8 us  [shift(): return lax.ppermute(x, 'ctx', [(i, (i + by) % count) for i in range(count)])]
    all_gather x0 -> x3, blocking collectives: none -> 11.7 us  [pair_gather(): return lax.all_gather(x, 'ctx', axis=0, tiled=True, axis_index_groups=pairs)]
    pallas_call x0 -> x7, Pallas kernels: none -> 10.4 us  [run(): pl.pallas_call(kernel, out_shape=[jax.ShapeDtypeStruct(s, d) for s, d in...]
    another operation x9 -> x0, loops' own time: 10.3 us -> none  [the longest x1 10 us: body(): lax.fori_loop(0, seq_len // block_len, key_step, (zero_rows, start_terms))]
    dynamic_update_slice x16 -> x0, local copies, waits for them, and re-layouts: 8.33 us -> none  [key_step(): lax.dynamic_update_slice_in_dim(carry[1], block_terms, key_first, 0)]
    reduce_sum x12 -> x0, other arithmetic: 6.42 us -> none  [the longest x11 6.08 us: doc_index(): jnp.sum((doc_ends[None, :] <= positions[:, None]).astype(jnp.int32), axis=1)]
  transfers between devices with their start and end apart: 3 -> 7, of which waited for: 3 -> 2; matrix products, arithmetic and copies ran while one was open for 3% -> 0% of each run, Pallas kernels for 0% -> 6%
where the time goes in v1:
time: 87.1 us; the launch traced here: 86.6 us
  waiting for transfers between devices  23.3 us (27%)
  starting transfers between devices  20.8 us (24%)
  between operations  14.2 us (16%)
  blocking collectives  11.7 us (13%)
  Pallas kernels  10.4 us (12%)
  local copies, waits for them, and re-layouts  6.29 us (7%)
    ppermute x6, starting transfers between devices, shift(): return lax.ppermute(x, 'ctx', [(i, (i + by) % count) for i in range(count)])  20.8 us
    all_gather x1, waiting for transfers between devices, pair_gather(): return lax.all_gather(x, 'ctx', axis=0, tiled=True, axis_index_groups=pairs)  19.9 us
    all_gather x3, blocking collectives, pair_gather(): return lax.all_gather(x, 'ctx', axis=0, tiled=True, axis_index_groups=pairs)  11.7 us
    pallas_call x7, Pallas kernels, run(): pl.pallas_call(kernel, out_shape=[jax.ShapeDtypeStruct(s, d) for s, d in...  10.4 us
    unnamed x16, local copies, waits for them, and re-layouts  6.29 us
    ppermute x6, waiting for transfers between devices, shift(): return lax.ppermute(x, 'ctx', [(i, (i + by) % count) for i in range(count)])  3.37 us
  transfers between devices with their start and end apart: 7, of which 2 were waited for; matrix products, arithmetic and copies ran while one was open for 0% of the time, Pallas kernels for 6%

profile of v1, /device:TPU:1, one launch (start us, length us, event | category | flops | bytes accessed | tf_op | source)
XLA Modules:
  0.0 86.6 jit_solution(5066372848984500975)
XLA Ops:
  7.2 0.0 all-gather.2.cloned.1.call-start
  7.2 0.0 copy-start.1
  7.2 0.9 %copy-done.1 = bf16[256,256]{1,0:T(8,128)(2,1)S(1)} copy-done((bf16[256,256]{1,0:T(8,128)(2,1)S(1)}, bf16[256,256]{1,0:T(8,128)(2,1)}, u32[]{:S(2)}) %copy-start.1) | copy-done | bytes 131096
  8.1 0.0 copy-start.2
  8.1 0.9 %copy-done.2 = bf16[256,256]{1,0:T(8,128)(2,1)S(1)} copy-done((bf16[256,256]{1,0:T(8,128)(2,1)S(1)}, bf16[256,256]{1,0:T(8,128)(2,1)}, u32[]{:S(2)}) %copy-start.2) | copy-done | bytes 131096
  9.0 0.0 copy-start.3
  9.0 0.9 %copy-done.3 = bf16[256,256]{1,0:T(8,128)(2,1)S(1)} copy-done((bf16[256,256]{1,0:T(8,128)(2,1)S(1)}, bf16[256,256]{1,0:T(8,128)(2,1)}, u32[]{:S(2)}) %copy-start.3) | copy-done | bytes 131096
  9.9 0.0 copy-start.4
  9.9 0.8 copy-done.4
  10.8 0.0 copy-start.5
  10.8 0.8 copy-done.5
  11.6 0.0 copy-start.6
  11.6 0.7 copy-done.6
  12.3 0.2 prep.1
  12.4 5.0 %collective-permute-start.1 = (bf16[256,256]{1,0:T(8,128)(2,1)S(1)}, bf16[256,256]{1,0:T(8,128)(2,1)S(1)}, u32[]{:S(2)}, u32[]{:S(2)}) collective-permute-start(bf16[256,256]{1,0:T(8,128)(2,1)S(1)} %get-tuple-element.18), channel_id=1, source_target_pairs={{0,128},{32,160},{64,192},{96,224},{128,256},{160,288},{192,320},{... | collective-permute-start | bytes 393224 | tf_op jit(solution)/shard_map/ppermute | solution.py:229
  17.5 3.2 %collective-permute-start = (bf16[256,256]{1,0:T(8,128)(2,1)S(1)}, bf16[256,256]{1,0:T(8,128)(2,1)S(1)}, u32[]{:S(2)}, u32[]{:S(2)}) collective-permute-start(bf16[256,256]{1,0:T(8,128)(2,1)S(1)} %get-tuple-element.18), channel_id=1, source_target_pairs={{0,64},{32,96},{64,128},{96,160},{128,192},{160,224},{192,256},{22... | collective-permute-start | bytes 393224 | tf_op jit(solution)/shard_map/ppermute | solution.py:229
  20.7 0.0 copy-start.7
  20.7 3.2 %collective-permute-start.2 = (bf16[272,512]{1,0:T(8,128)(2,1)S(1)}, bf16[272,512]{1,0:T(8,128)(2,1)S(1)}, u32[]{:S(2)}, u32[]{:S(2)}) collective-permute-start(bf16[272,512]{1,0:T(8,128)(2,1)S(1)} %get-tuple-element.17.pay_ref), channel_id=1, source_target_pairs={{0,384},{32,416},{64,448},{96,480},{128,0},{160,32},{192,64},{224,... | collective-permute-start | bytes 835592 | tf_op jit(solution)/shard_map/ppermute | solution.py:229
  23.9 7.0 %all_gather.13.kv_ref = bf16[512,256]{1,0:T(8,128)(2,1)S(1)} all-gather(bf16[256,256]{1,0:T(8,128)(2,1)S(1)} %get-tuple-element.18), channel_id=1, replica_groups={{0,32},{64,96},{128,160},{192,224},{256,288},{320,352},{384,416},{448,4..., dimensions={0}, use_global_device_ids=true | all-gather | bytes 393216 | tf_op jit(solution)/shard_map/all_gather | solution.py:232
  30.9 0.0 copy-done.7
  30.9 1.9 %own.1 = (f32[256,256]{1,0:T(8,128)S(1)}, f32[256,256]{1,0:T(8,128)S(1)}, f32[256,256]{1,0:T(8,128)S(1)}) custom-call(s32[4]{0:T(128)S(1)} %copy-done.7, bf16[272,512]{1,0:T(8,128)(2,1)S(1)} %get-tuple-element.17.pay_ref, bf16[512,256]{1,0:T(8,128)(2,1)S(1)} %all_gather.13.kv_ref), custom_call_target="tpu_custom_call" | custom-call | flops 335544320 | bytes 540688 | tf_op jit(solution)/shard_map/own/pallas_call | solution.py:206
  32.8 0.0 collective-permute-done.1
  32.8 0.0 collective-permute-done
  32.8 2.2 %all_gather.12.kv_ref = bf16[1024,256]{1,0:T(8,128)(2,1)S(1)} all-gather(bf16[512,256]{1,0:T(8,128)(2,1)S(1)} %pad_maximum_fusion), channel_id=1, replica_groups={{0,32},{64,96},{128,160},{192,224},{256,288},{320,352},{384,416},{448,4..., dimensions={0}, use_global_device_ids=true | all-gather | bytes 786432 | tf_op jit(solution)/shard_map/all_gather | solution.py:232
  35.0 2.8 %near.1 = (f32[256,256]{1,0:T(8,128)S(1)}, f32[1024,256]{1,0:T(8,128)S(1)}) custom-call(s32[4]{0:T(128)S(1)} %copy-done.7, bf16[272,512]{1,0:T(8,128)(2,1)S(1)} %get-tuple-element.17.pay_ref, bf16[1024,256]{1,0:T(8,128)(2,1)S(1)} %all_gather.12.kv_ref, f32[256,256]{1,0:T(8,128)S(1)} %get-tuple-element.19.dqt_in_ref), custom_call_target="tpu_custom_call" | custom-call | flops 671088640 | bytes 1064976 | tf_op jit(solution)/shard_map/near/pallas_call | solution.py:206
  37.8 0.0 collective-permute-done.2.pay_ref
  37.8 4.0 %far.1 = (bf16[256,256]{1,0:T(8,128)(2,1)S(1)}, f32[512,256]{1,0:T(8,128)S(1)}, f32[512,256]{1,0:T(8,128)}) custom-call(s32[4]{0:T(128)S(1)} %copy-done.7, bf16[272,512]{1,0:T(8,128)(2,1)S(1)} %collective-permute-done.2.pay_ref, bf16[1024,256]{1,0:T(8,128)(2,1)S(1)} %all_gather.12.kv_ref, f32[1024,256]{1,0:T(8,128)S(1)} %get-tuple-element.21.terms_ref), custom_call_target="tpu_custom_call" | custom-call | flops 671088640 | bytes 1851408 | tf_op jit(solution)/shard_map/far/pallas_call | solution.py:206
  41.8 0.0 all-gather.2.cloned.1.call-update
  41.9 1.9 %collective-permute-start.3 = (bf16[256,256]{1,0:T(8,128)(2,1)S(1)}, bf16[256,256]{1,0:T(8,128)(2,1)S(1)}, u32[]{:S(2)}, u32[]{:S(2)}) collective-permute-start(bf16[256,256]{1,0:T(8,128)(2,1)S(1)} %get-tuple-element.22), channel_id=1, source_target_pairs={{0,128},{32,160},{64,192},{96,224},{128,256},{160,288},{192,320},{... | collective-permute-start | bytes 393224 | tf_op jit(solution)/shard_map/ppermute | solution.py:229
  43.8 19.9 %all-gather.2.cloned.1.call-done.both_ref = f32[1024,256]{1,0:T(8,128)} async-done(((f32[512,256]{1,0:T(8,128)}), f32[1024,256]{1,0:T(8,128)}) %all-gather.2.cloned.1.call-update) | async-done | bytes 1048592 | tf_op jit(solution)/shard_map/all_gather | solution.py:232
  63.7 0.0 copy-start
  63.7 1.2 %copy-done = f32[1024,256]{1,0:T(8,128)S(1)} copy-done((f32[1024,256]{1,0:T(8,128)S(1)}, f32[1024,256]{1,0:T(8,128)}, u32[]{:S(2)}) %copy-start) | copy-done | bytes 1048600
  65.0 3.5 %collective-permute-start.4 = (bf16[256,256]{1,0:T(8,128)(2,1)S(1)}, bf16[256,256]{1,0:T(8,128)(2,1)S(1)}, u32[]{:S(2)}, u32[]{:S(2)}) collective-permute-start(bf16[256,256]{1,0:T(8,128)(2,1)S(1)} %get-tuple-element.27), channel_id=1, source_target_pairs={{0,448},{32,480},{64,0},{96,32},{128,64},{160,96},{192,128},{224,1... | collective-permute-start | bytes 393224 | tf_op jit(solution)/shard_map/ppermute | solution.py:229
  68.4 3.9 %collective-permute-start.5 = (bf16[256,256]{1,0:T(8,128)(2,1)S(1)}, bf16[256,256]{1,0:T(8,128)(2,1)S(1)}, u32[]{:S(2)}, u32[]{:S(2)}) collective-permute-start(bf16[256,256]{1,0:T(8,128)(2,1)S(1)} %get-tuple-element.28), channel_id=1, source_target_pairs={{0,384},{32,416},{64,448},{96,480},{128,0},{160,32},{192,64},{224,... | collective-permute-start | bytes 393224 | tf_op jit(solution)/shard_map/ppermute | solution.py:229
  72.4 2.6 %all_gather.14.both_ref = f32[512,256]{1,0:T(8,128)S(1)} all-gather(f32[256,256]{1,0:T(8,128)S(1)} %get-tuple-element.24), channel_id=1, replica_groups={{0,32},{64,96},{128,160},{192,224},{256,288},{320,352},{384,416},{448,4..., dimensions={0}, use_global_device_ids=true | all-gather | bytes 786432 | tf_op jit(solution)/shard_map/all_gather | solution.py:232
  75.0 0.0 collective-permute-done.3.back_ref
  75.0 0.8 grad_query.1
  75.7 0.0 collective-permute-done.4.near_ref
  75.7 3.4 %collective-permute-done.5.far_ref = bf16[256,256]{1,0:T(8,128)(2,1)S(1)} collective-permute-done((bf16[256,256]{1,0:T(8,128)(2,1)S(1)}, bf16[256,256]{1,0:T(8,128)(2,1)S(1)}, u32[]{:S(2)}, u32[]{:S(2)}) %collective-permute-start.5) | collective-permute-done | bytes 131104 | tf_op jit(solution)/shard_map/ppermute | solution.py:229
  79.1 0.7 grad_key.1
  (2 shorter events, 0.1 us)
Async XLA Ops:
  7.2 56.5 %all-gather.2.cloned.1.call-start = ((), (), s32[]{:S(2)}) async-start(), calls=%async_computation | async-start | bytes 1572864 | tf_op jit(solution)/shard_map/all_gather | solution.py:232
  7.2 0.9 %copy-start.1 = (bf16[256,256]{1,0:T(8,128)(2,1)S(1)}, bf16[256,256]{1,0:T(8,128)(2,1)}, u32[]{:S(2)}) copy-start(bf16[256,256]{1,0:T(8,128)(2,1)} %q_ref.1) | copy-start | bytes 393220
  8.1 0.9 %copy-start.2 = (bf16[256,256]{1,0:T(8,128)(2,1)S(1)}, bf16[256,256]{1,0:T(8,128)(2,1)}, u32[]{:S(2)}) copy-start(bf16[256,256]{1,0:T(8,128)(2,1)} %go_ref.1) | copy-start | bytes 393220
  9.0 0.9 %copy-start.3 = (bf16[256,256]{1,0:T(8,128)(2,1)S(1)}, bf16[256,256]{1,0:T(8,128)(2,1)}, u32[]{:S(2)}) copy-start(bf16[256,256]{1,0:T(8,128)(2,1)} %out_ref.1) | copy-start | bytes 393220
  9.9 0.8 copy-start.4
  10.8 0.8 copy-start.5
  11.6 0.7 copy-start.6
  12.4 20.3 %collective-permute-start.1 = (bf16[256,256]{1,0:T(8,128)(2,1)S(1)}, bf16[256,256]{1,0:T(8,128)(2,1)S(1)}, u32[]{:S(2)}, u32[]{:S(2)}) collective-permute-start(bf16[256,256]{1,0:T(8,128)(2,1)S(1)} %get-tuple-element.18), channel_id=1, source_target_pairs={{0,128},{32,160},{64,192},{96,224},{128,256},{160,288},{192,320},{... | collective-permute-start | bytes 393224 | tf_op jit(solution)/shard_map/ppermute | solution.py:229
  17.5 15.3 %collective-permute-start = (bf16[256,256]{1,0:T(8,128)(2,1)S(1)}, bf16[256,256]{1,0:T(8,128)(2,1)S(1)}, u32[]{:S(2)}, u32[]{:S(2)}) collective-permute-start(bf16[256,256]{1,0:T(8,128)(2,1)S(1)} %get-tuple-element.18), channel_id=1, source_target_pairs={{0,64},{32,96},{64,128},{96,160},{128,192},{160,224},{192,256},{22... | collective-permute-start | bytes 393224 | tf_op jit(solution)/shard_map/ppermute | solution.py:229
  20.7 10.2 %copy-start.7 = (s32[4]{0:T(128)S(1)}, s32[4]{0:T(128)}, u32[]{:S(2)}) copy-start(s32[4]{0:T(128)} %lens_ref.5) | copy-start | bytes 52
  20.7 17.1 %collective-permute-start.2 = (bf16[272,512]{1,0:T(8,128)(2,1)S(1)}, bf16[272,512]{1,0:T(8,128)(2,1)S(1)}, u32[]{:S(2)}, u32[]{:S(2)}) collective-permute-start(bf16[272,512]{1,0:T(8,128)(2,1)S(1)} %get-tuple-element.17.pay_ref), channel_id=1, source_target_pairs={{0,384},{32,416},{64,448},{96,480},{128,0},{160,32},{192,64},{224,... | collective-permute-start | bytes 835592 | tf_op jit(solution)/shard_map/ppermute | solution.py:229
  41.9 33.1 %collective-permute-start.3 = (bf16[256,256]{1,0:T(8,128)(2,1)S(1)}, bf16[256,256]{1,0:T(8,128)(2,1)S(1)}, u32[]{:S(2)}, u32[]{:S(2)}) collective-permute-start(bf16[256,256]{1,0:T(8,128)(2,1)S(1)} %get-tuple-element.22), channel_id=1, source_target_pairs={{0,128},{32,160},{64,192},{96,224},{128,256},{160,288},{192,320},{... | collective-permute-start | bytes 393224 | tf_op jit(solution)/shard_map/ppermute | solution.py:229
  63.7 1.2 %copy-start = (f32[1024,256]{1,0:T(8,128)S(1)}, f32[1024,256]{1,0:T(8,128)}, u32[]{:S(2)}) copy-start(f32[1024,256]{1,0:T(8,128)} %all-gather.2.cloned.1.call-done.both_ref) | copy-start | bytes 3145732
  65.0 10.8 %collective-permute-start.4 = (bf16[256,256]{1,0:T(8,128)(2,1)S(1)}, bf16[256,256]{1,0:T(8,128)(2,1)S(1)}, u32[]{:S(2)}, u32[]{:S(2)}) collective-permute-start(bf16[256,256]{1,0:T(8,128)(2,1)S(1)} %get-tuple-element.27), channel_id=1, source_target_pairs={{0,448},{32,480},{64,0},{96,32},{128,64},{160,96},{192,128},{224,1... | collective-permute-start | bytes 393224 | tf_op jit(solution)/shard_map/ppermute | solution.py:229
  68.4 10.6 %collective-permute-start.5 = (bf16[256,256]{1,0:T(8,128)(2,1)S(1)}, bf16[256,256]{1,0:T(8,128)(2,1)S(1)}, u32[]{:S(2)}, u32[]{:S(2)}) collective-permute-start(bf16[256,256]{1,0:T(8,128)(2,1)S(1)} %get-tuple-element.28), channel_id=1, source_target_pairs={{0,384},{32,416},{64,448},{96,480},{128,0},{160,32},{192,64},{224,... | collective-permute-start | bytes 393224 | tf_op jit(solution)/shard_map/ppermute | solution.py:229
Sparse Core Ops, SparseCore 0:
  42.0 21.6 all-gather.1

commit v2 on v1

--- a/solution.py
+++ b/solution.py
@@ -20,24 +20,36 @@
     return high, mid, low
 
 
-def prep_kernel(q_ref, go_ref, out_ref, norm_ref, k_ref, v_ref, pay_ref, kv_ref):
+def prep_kernel(q_ref, go_ref, out_ref, norm_ref, k_ref, v_ref, pay_ref, kv_ref, *scratch):
+    out_buf, norm_buf, sems = scratch
     rows, width = q_ref.shape
     heads = norm_ref.shape[0]
-    head_dim = width // heads
-    kv_ref[:, :head_dim] = k_ref[...]
-    kv_ref[:, head_dim:] = v_ref[...]
-    pay_ref[:rows, :width] = q_ref[...]
-    pay_ref[:rows, width:] = go_ref[...]
-    product = go_ref[...].astype(jnp.float32) * out_ref[...].astype(jnp.float32)
+    e = width // heads
+    moves = [
+        (go_ref, pay_ref.at[:rows, width:]),
+        (out_ref, out_buf),
+        (norm_ref, norm_buf),
+        (q_ref, pay_ref.at[:rows, :width]),
+        (k_ref, kv_ref.at[:, :e]),
+        (v_ref, kv_ref.at[:, e:]),
+    ]
+    copies = [pltpu.make_async_copy(s, d, sems.at[i]) for i, (s, d) in enumerate(moves)]
+    for copy in copies:
+        copy.start()
+    for copy in copies[:3]:
+        copy.wait()
+    product = pay_ref[:rows, width:].astype(jnp.float32) * out_buf[...].astype(jnp.float32)
     product_t = product.T
     stats = []
     for h in range(heads):
-        delta = jnp.sum(product_t[h * head_dim : (h + 1) * head_dim], axis=0, keepdims=True)
-        stats += list(split3(norm_ref[h : h + 1, :] * LOG2E)) + list(split3(delta))
+        delta = jnp.sum(product_t[h * e : (h + 1) * e], axis=0, keepdims=True)
+        stats += list(split3(norm_buf[h : h + 1, :] * LOG2E)) + list(split3(delta))
     stats += [jnp.zeros((1, rows), jnp.bfloat16)] * (STAT_ROWS - len(stats))
     table = jnp.concatenate([s.astype(jnp.float32) for s in stats], axis=0)
     pay_ref[rows:, :rows] = table.astype(jnp.bfloat16)
     pay_ref[rows:, rows:] = jnp.zeros((STAT_ROWS, pay_ref.shape[1] - rows), jnp.bfloat16)
+    for copy in copies[3:]:
+        copy.wait()
 
 
 class Query:
@@ -166,8 +178,8 @@
 
             @pl.when(core != half)
             def _():
-                give_ref[out, :e] = dk
-                give_ref[out, e:] = dv
+                give_ref[out, :e] = dk.astype(jnp.bfloat16)
+                give_ref[out, e:] = dv.astype(jnp.bfloat16)
 
     for h in range(heads):
         dqt_ref[h * e : (h + 1) * e, :] = dqt[h].astype(jnp.bfloat16)
@@ -178,7 +190,7 @@
     rows = count // 2
     _, _, core = place()
     other = both_ref[pl.ds(pl.multiple_of((1 - core) * count, count), count), :]
-    total = (keep_ref[...] + other).astype(jnp.bfloat16)
+    total = (keep_ref[...] + other.astype(jnp.float32)).astype(jnp.bfloat16)
     near_ref[...] = total[:rows]
     far_ref[...] = total[rows:]
 
@@ -198,16 +210,17 @@
     dv_ref[...] = total[:, e:].astype(jnp.bfloat16)
 
 
-def call(kernel, outs, name, flops=0, smem=0):
+def call(kernel, outs, name, flops=0, smem=0, space=pltpu.VMEM, scratch=()):
     def run(*args):
         specs = [pl.BlockSpec(memory_space=pltpu.SMEM)] * smem
-        specs += [pl.BlockSpec(memory_space=pltpu.VMEM)] * (len(args) - smem)
+        specs += [pl.BlockSpec(memory_space=space)] * (len(args) - smem)
         moved = sum(a.size * a.dtype.itemsize for a in args)
         return pl.pallas_call(
             kernel,
             out_shape=[jax.ShapeDtypeStruct(s, d) for s, d in outs],
             in_specs=specs,
             out_specs=[pl.BlockSpec(memory_space=pltpu.VMEM)] * len(outs),
+            scratch_shapes=list(scratch),
             cost_estimate=pl.CostEstimate(flops=flops, bytes_accessed=moved, transcendentals=0),
             compiler_params=pltpu.CompilerParams(vmem_limit_bytes=32 * 1024 * 1024),
             name=name,
@@ -232,8 +245,21 @@
         return lax.all_gather(x, "ctx", axis=0, tiled=True, axis_index_groups=pairs)
 
     pay, kv = call(
-        prep_kernel, [((rows + STAT_ROWS, 2 * width), bf16), ((rows, 2 * e), bf16)], "prep"
-    )(queries, grad_out, attn_out, log_norm, key_states, value_states)
+        prep_kernel,
+        [((rows + STAT_ROWS, 2 * width), bf16), ((rows, 2 * e), bf16)],
+        "prep",
+        space=pltpu.HBM,
+        scratch=[
+            pltpu.VMEM((rows, width), bf16),
+            pltpu.VMEM((heads, rows), f32),
+            pltpu.SemaphoreType.DMA((6,)),
+        ],
+    )(
+        *[
+            pltpu.with_memory_space_constraint(x, pltpu.HBM)
+            for x in (queries, grad_out, attn_out, log_norm, key_states, value_states)
+        ]
+    )
     pay_far = shift(pay, -4)
     kv_far = shift(kv, 4)
     kv_near = shift(kv, 2)
@@ -256,7 +282,7 @@
     )(doc_lengths, pay, kv_back, dqt)
     dqt_far, keep, give = call(
         functools.partial(far_kernel, heads, chips),
-        [((width, rows), bf16), ((2 * rows, 2 * e), f32), ((2 * rows, 2 * e), f32)],
+        [((width, rows), bf16), ((2 * rows, 2 * e), f32), ((2 * rows, 2 * e), bf16)],
         "far",
         2 * unit,
         1,

time: 87.1 us -> 53.1 us (0.61)
  waiting for transfers between devices: 23.3 us -> 4.5 us
  between operations: 14.2 us -> 0.75 us
  local copies, waits for them, and re-layouts: 6.29 us -> 0.01 us
  blocking collectives: 11.7 us -> 15.2 us
    all_gather x1 -> x0, waiting for transfers between devices: 19.9 us -> none  [pair_gather(): return lax.all_gather(x, 'ctx', axis=0, tiled=True, axis_index_groups=pairs)]
    unnamed x16 -> x2, local copies, waits for them, and re-layouts: 6.29 us -> 0.01 us
    all_gather x3 -> x4, blocking collectives: 11.7 us -> 15.2 us  [pair_gather(): return lax.all_gather(x, 'ctx', axis=0, tiled=True, axis_index_groups=pairs)]
    ppermute x6, waiting for transfers between devices: 3.37 us -> 4.5 us  [shift(): return lax.ppermute(x, 'ctx', [(i, (i + by) % count) for i in range(count)])]
    ppermute x6, starting transfers between devices: 20.8 us -> 21.6 us  [shift(): return lax.ppermute(x, 'ctx', [(i, (i + by) % count) for i in range(count)])]
  transfers between devices with their start and end apart: 7 -> 6, of which waited for: 2 -> 1; matrix products, arithmetic and copies ran while one was open for 0% -> 0% of each run, Pallas kernels for 6% -> 11%
where the time goes in v2:
time: 53.1 us; the launch traced here: 52.8 us
  starting transfers between devices  21.6 us (41%)
  blocking collectives  15.2 us (29%)
  Pallas kernels  10.7 us (20%)
  waiting for transfers between devices  4.5 us (8%)
  between operations  0.75 us (1%)
    ppermute x6, starting transfers between devices, shift(): return lax.ppermute(x, 'ctx', [(i, (i + by) % count) for i in range(count)])  21.6 us
    all_gather x4, blocking collectives, pair_gather(): return lax.all_gather(x, 'ctx', axis=0, tiled=True, axis_index_groups=pairs)  15.2 us
    pallas_call x7, Pallas kernels, run(): pl.pallas_call(kernel, out_shape=[jax.ShapeDtypeStruct(s, d) for s, d in...  10.7 us
    ppermute x6, waiting for transfers between devices, shift(): return lax.ppermute(x, 'ctx', [(i, (i + by) % count) for i in range(count)])  4.5 us
  transfers between devices with their start and end apart: 6, of which 1 were waited for; matrix products, arithmetic and copies ran while one was open for 0% of the time, Pallas kernels for 11%

profile of v2, /device:TPU:1, one launch (start us, length us, event | category | flops | bytes accessed | tf_op | source)
XLA Modules:
  0.0 52.8 jit_solution(13408002064019451611)
XLA Ops:
  0.6 1.2 %prep.1 = (bf16[272,512]{1,0:T(8,128)(2,1)S(1)}, bf16[256,256]{1,0:T(8,128)(2,1)S(1)}) custom-call(bf16[256,256]{1,0:T(8,128)(2,1)} %q_ref.1, bf16[256,256]{1,0:T(8,128)(2,1)} %go_ref.1, bf16[256,256]{1,0:T(8,128)(2,1)} %out_ref.1, f32[2,256]{1,0:T(2,128)} %norm_ref.1, bf16[256,128]{1,0:T(8,128)(2,1)} %k_ref.1, bf16[256,128]{1,0:T(8,128)(2,1)} %v_ref.1), custom_call_target="tpu_custom_call" | custom-call | bytes 526336 | tf_op jit(solution)/shard_map/prep/pallas_call | solution.py:218
  1.8 5.0 %collective-permute-start.1 = (bf16[256,256]{1,0:T(8,128)(2,1)S(1)}, bf16[256,256]{1,0:T(8,128)(2,1)S(1)}, u32[]{:S(2)}, u32[]{:S(2)}) collective-permute-start(bf16[256,256]{1,0:T(8,128)(2,1)S(1)} %get-tuple-element.18), channel_id=1, source_target_pairs={{0,128},{32,160},{64,192},{96,224},{128,256},{160,288},{192,320},{... | collective-permute-start | bytes 393224 | tf_op jit(solution)/shard_map/ppermute | solution.py:242
  6.9 3.2 %collective-permute-start = (bf16[256,256]{1,0:T(8,128)(2,1)S(1)}, bf16[256,256]{1,0:T(8,128)(2,1)S(1)}, u32[]{:S(2)}, u32[]{:S(2)}) collective-permute-start(bf16[256,256]{1,0:T(8,128)(2,1)S(1)} %get-tuple-element.18), channel_id=1, source_target_pairs={{0,64},{32,96},{64,128},{96,160},{128,192},{160,224},{192,256},{22... | collective-permute-start | bytes 393224 | tf_op jit(solution)/shard_map/ppermute | solution.py:242
  10.1 0.0 copy-start
  10.1 3.2 %collective-permute-start.2 = (bf16[272,512]{1,0:T(8,128)(2,1)S(1)}, bf16[272,512]{1,0:T(8,128)(2,1)S(1)}, u32[]{:S(2)}, u32[]{:S(2)}) collective-permute-start(bf16[272,512]{1,0:T(8,128)(2,1)S(1)} %get-tuple-element.17.pay_ref), channel_id=1, source_target_pairs={{0,384},{32,416},{64,448},{96,480},{128,0},{160,32},{192,64},{224,... | collective-permute-start | bytes 835592 | tf_op jit(solution)/shard_map/ppermute | solution.py:242
  13.3 7.0 %all_gather.13.kv_ref = bf16[512,256]{1,0:T(8,128)(2,1)S(1)} all-gather(bf16[256,256]{1,0:T(8,128)(2,1)S(1)} %get-tuple-element.18), channel_id=1, replica_groups={{0,32},{64,96},{128,160},{192,224},{256,288},{320,352},{384,416},{448,4..., dimensions={0}, use_global_device_ids=true | all-gather | bytes 393216 | tf_op jit(solution)/shard_map/all_gather | solution.py:245
  20.2 0.0 copy-done
  20.2 1.9 %own.1 = (f32[256,256]{1,0:T(8,128)S(1)}, f32[256,256]{1,0:T(8,128)S(1)}, f32[256,256]{1,0:T(8,128)S(1)}) custom-call(s32[4]{0:T(128)S(1)} %copy-done, bf16[272,512]{1,0:T(8,128)(2,1)S(1)} %get-tuple-element.17.pay_ref, bf16[512,256]{1,0:T(8,128)(2,1)S(1)} %all_gather.13.kv_ref), custom_call_target="tpu_custom_call" | custom-call | flops 335544320 | bytes 540688 | tf_op jit(solution)/shard_map/own/pallas_call | solution.py:218
  22.1 0.0 collective-permute-done.1
  22.1 0.0 collective-permute-done
  22.2 2.2 %all_gather.12.kv_ref = bf16[1024,256]{1,0:T(8,128)(2,1)S(1)} all-gather(bf16[512,256]{1,0:T(8,128)(2,1)S(1)} %pad_maximum_fusion), channel_id=1, replica_groups={{0,32},{64,96},{128,160},{192,224},{256,288},{320,352},{384,416},{448,4..., dimensions={0}, use_global_device_ids=true | all-gather | bytes 786432 | tf_op jit(solution)/shard_map/all_gather | solution.py:245
  24.4 2.8 %near.1 = (f32[256,256]{1,0:T(8,128)S(1)}, f32[1024,256]{1,0:T(8,128)S(1)}) custom-call(s32[4]{0:T(128)S(1)} %copy-done, bf16[272,512]{1,0:T(8,128)(2,1)S(1)} %get-tuple-element.17.pay_ref, bf16[1024,256]{1,0:T(8,128)(2,1)S(1)} %all_gather.12.kv_ref, f32[256,256]{1,0:T(8,128)S(1)} %get-tuple-element.19.dqt_in_ref), custom_call_target="tpu_custom_call" | custom-call | flops 671088640 | bytes 1064976 | tf_op jit(solution)/shard_map/near/pallas_call | solution.py:218
  27.2 0.0 collective-permute-done.2.pay_ref
  27.2 3.2 %far.1 = (bf16[256,256]{1,0:T(8,128)(2,1)S(1)}, f32[512,256]{1,0:T(8,128)S(1)}, bf16[512,256]{1,0:T(8,128)(2,1)S(1)}) custom-call(s32[4]{0:T(128)S(1)} %copy-done, bf16[272,512]{1,0:T(8,128)(2,1)S(1)} %collective-permute-done.2.pay_ref, bf16[1024,256]{1,0:T(8,128)(2,1)S(1)} %all_gather.12.kv_ref, f32[1024,256]{1,0:T(8,128)S(1)} %get-tuple-element.21.terms_ref), custom_call_target="tpu_custom_call" | custom-call | flops 671088640 | bytes 1851408 | tf_op jit(solution)/shard_map/far/pallas_call | solution.py:218
  30.5 1.9 %collective-permute-start.3 = (bf16[256,256]{1,0:T(8,128)(2,1)S(1)}, bf16[256,256]{1,0:T(8,128)(2,1)S(1)}, u32[]{:S(2)}, u32[]{:S(2)}) collective-permute-start(bf16[256,256]{1,0:T(8,128)(2,1)S(1)} %get-tuple-element.22), channel_id=1, source_target_pairs={{0,128},{32,160},{64,192},{96,224},{128,256},{160,288},{192,320},{... | collective-permute-start | bytes 393224 | tf_op jit(solution)/shard_map/ppermute | solution.py:242
  32.4 3.3 %all_gather.15.both_ref = bf16[1024,256]{1,0:T(8,128)(2,1)S(1)} all-gather(bf16[512,256]{1,0:T(8,128)(2,1)S(1)} %get-tuple-element.26), channel_id=1, replica_groups={{0,32},{64,96},{128,160},{192,224},{256,288},{320,352},{384,416},{448,4..., dimensions={0}, use_global_device_ids=true | all-gather | bytes 786432 | tf_op jit(solution)/shard_map/all_gather | solution.py:245
  35.7 0.1 pair.1
  35.8 6.4 %collective-permute-start.4 = (bf16[256,256]{1,0:T(8,128)(2,1)S(1)}, bf16[256,256]{1,0:T(8,128)(2,1)S(1)}, u32[]{:S(2)}, u32[]{:S(2)}) collective-permute-start(bf16[256,256]{1,0:T(8,128)(2,1)S(1)} %get-tuple-element.27), channel_id=1, source_target_pairs={{0,448},{32,480},{64,0},{96,32},{128,64},{160,96},{192,128},{224,1... | collective-permute-start | bytes 393224 | tf_op jit(solution)/shard_map/ppermute | solution.py:242
  42.2 1.9 %collective-permute-start.5 = (bf16[256,256]{1,0:T(8,128)(2,1)S(1)}, bf16[256,256]{1,0:T(8,128)(2,1)S(1)}, u32[]{:S(2)}, u32[]{:S(2)}) collective-permute-start(bf16[256,256]{1,0:T(8,128)(2,1)S(1)} %get-tuple-element.28), channel_id=1, source_target_pairs={{0,384},{32,416},{64,448},{96,480},{128,0},{160,32},{192,64},{224,... | collective-permute-start | bytes 393224 | tf_op jit(solution)/shard_map/ppermute | solution.py:242
  44.1 2.7 %all_gather.14.both_ref = f32[512,256]{1,0:T(8,128)S(1)} all-gather(f32[256,256]{1,0:T(8,128)S(1)} %get-tuple-element.24), channel_id=1, replica_groups={{0,32},{64,96},{128,160},{192,224},{256,288},{320,352},{384,416},{448,4..., dimensions={0}, use_global_device_ids=true | all-gather | bytes 786432 | tf_op jit(solution)/shard_map/all_gather | solution.py:245
  46.8 0.0 collective-permute-done.3.back_ref
  46.8 0.8 %grad_query.1 = bf16[256,256]{1,0:T(8,128)(2,1)} custom-call(f32[256,256]{1,0:T(8,128)S(1)} %get-tuple-element.20.dqt_ref, bf16[256,256]{1,0:T(8,128)(2,1)S(1)} %collective-permute-done.3.back_ref), custom_call_target="tpu_custom_call" | custom-call | bytes 393216 | tf_op jit(solution)/shard_map/grad_query/pallas_call | solution.py:218
  47.6 0.0 collective-permute-done.4.near_ref
  47.6 4.5 %collective-permute-done.5.far_ref = bf16[256,256]{1,0:T(8,128)(2,1)S(1)} collective-permute-done((bf16[256,256]{1,0:T(8,128)(2,1)S(1)}, bf16[256,256]{1,0:T(8,128)(2,1)S(1)}, u32[]{:S(2)}, u32[]{:S(2)}) %collective-permute-start.5) | collective-permute-done | bytes 131104 | tf_op jit(solution)/shard_map/ppermute | solution.py:242
  52.1 0.7 %grad_key.1 = (bf16[256,128]{1,0:T(8,128)(2,1)}, bf16[256,128]{1,0:T(8,128)(2,1)}) custom-call(f32[256,256]{1,0:T(8,128)S(1)} %get-tuple-element.23.keep_ref, f32[512,256]{1,0:T(8,128)S(1)} %all_gather.14.both_ref, bf16[256,256]{1,0:T(8,128)(2,1)S(1)} %collective-permute-done.4.near_ref, bf16[256,256]{1,0:T(8,128)(2,1)S(1)} %collective-permute-done.5.far_ref), custom_call_target="tpu_custom_call" | custom-call | bytes 1048576 | tf_op jit(solution)/shard_map/grad_key/pallas_call | solution.py:218
  (1 shorter events, 0.0 us)
Async XLA Ops:
  1.8 20.3 %collective-permute-start.1 = (bf16[256,256]{1,0:T(8,128)(2,1)S(1)}, bf16[256,256]{1,0:T(8,128)(2,1)S(1)}, u32[]{:S(2)}, u32[]{:S(2)}) collective-permute-start(bf16[256,256]{1,0:T(8,128)(2,1)S(1)} %get-tuple-element.18), channel_id=1, source_target_pairs={{0,128},{32,160},{64,192},{96,224},{128,256},{160,288},{192,320},{... | collective-permute-start | bytes 393224 | tf_op jit(solution)/shard_map/ppermute | solution.py:242
  6.9 15.3 %collective-permute-start = (bf16[256,256]{1,0:T(8,128)(2,1)S(1)}, bf16[256,256]{1,0:T(8,128)(2,1)S(1)}, u32[]{:S(2)}, u32[]{:S(2)}) collective-permute-start(bf16[256,256]{1,0:T(8,128)(2,1)S(1)} %get-tuple-element.18), channel_id=1, source_target_pairs={{0,64},{32,96},{64,128},{96,160},{128,192},{160,224},{192,256},{22... | collective-permute-start | bytes 393224 | tf_op jit(solution)/shard_map/ppermute | solution.py:242
  10.1 10.2 %copy-start = (s32[4]{0:T(128)S(1)}, s32[4]{0:T(128)}, u32[]{:S(2)}) copy-start(s32[4]{0:T(128)} %lens_ref.5) | copy-start | bytes 52
  10.1 17.1 %collective-permute-start.2 = (bf16[272,512]{1,0:T(8,128)(2,1)S(1)}, bf16[272,512]{1,0:T(8,128)(2,1)S(1)}, u32[]{:S(2)}, u32[]{:S(2)}) collective-permute-start(bf16[272,512]{1,0:T(8,128)(2,1)S(1)} %get-tuple-element.17.pay_ref), channel_id=1, source_target_pairs={{0,384},{32,416},{64,448},{96,480},{128,0},{160,32},{192,64},{224,... | collective-permute-start | bytes 835592 | tf_op jit(solution)/shard_map/ppermute | solution.py:242
  30.5 16.3 %collective-permute-start.3 = (bf16[256,256]{1,0:T(8,128)(2,1)S(1)}, bf16[256,256]{1,0:T(8,128)(2,1)S(1)}, u32[]{:S(2)}, u32[]{:S(2)}) collective-permute-start(bf16[256,256]{1,0:T(8,128)(2,1)S(1)} %get-tuple-element.22), channel_id=1, source_target_pairs={{0,128},{32,160},{64,192},{96,224},{128,256},{160,288},{192,320},{... | collective-permute-start | bytes 393224 | tf_op jit(solution)/shard_map/ppermute | solution.py:242
  35.8 11.8 %collective-permute-start.4 = (bf16[256,256]{1,0:T(8,128)(2,1)S(1)}, bf16[256,256]{1,0:T(8,128)(2,1)S(1)}, u32[]{:S(2)}, u32[]{:S(2)}) collective-permute-start(bf16[256,256]{1,0:T(8,128)(2,1)S(1)} %get-tuple-element.27), channel_id=1, source_target_pairs={{0,448},{32,480},{64,0},{96,32},{128,64},{160,96},{192,128},{224,1... | collective-permute-start | bytes 393224 | tf_op jit(solution)/shard_map/ppermute | solution.py:242
  42.2 9.9 %collective-permute-start.5 = (bf16[256,256]{1,0:T(8,128)(2,1)S(1)}, bf16[256,256]{1,0:T(8,128)(2,1)S(1)}, u32[]{:S(2)}, u32[]{:S(2)}) collective-permute-start(bf16[256,256]{1,0:T(8,128)(2,1)S(1)} %get-tuple-element.28), channel_id=1, source_target_pairs={{0,384},{32,416},{64,448},{96,480},{128,0},{160,32},{192,64},{224,... | collective-permute-start | bytes 393224 | tf_op jit(solution)/shard_map/ppermute | solution.py:242

commit v3 on v2

--- a/solution.py
+++ b/solution.py
@@ -72,7 +72,7 @@
             self.start = jnp.where(end <= self.pos, end, self.start)
 
 
-def tile(query, h, k_block, v_block, k_first, causal):
+def scores_block(query, h, k_block, v_block, k_first, causal):
     contract = (((1,), (1,)), ((), ()))
     scaling = query.e ** (-0.5)
     scores = lax.dot_general(k_block, query.q[h], contract, preferred_element_type=jnp.float32)
@@ -82,23 +82,38 @@
     if causal:
         allowed = allowed & (k_pos <= query.pos)
     prob = jnp.where(allowed, jnp.exp2(scores * (scaling * LOG2E) - query.norm[h]), 0.0)
-    dscore = (prob * (grads - query.delta[h]) * scaling).astype(jnp.bfloat16)
-    return prob.astype(jnp.bfloat16), dscore
-
-
-def key_terms(query, k_block, v_block, k_first, causal, dqt):
-    dk = dv = None
-    for h in range(query.heads):
-        prob, dscore = tile(query, h, k_block, v_block, k_first, causal)
-        dv_h = jnp.dot(prob, query.go[h], preferred_element_type=jnp.float32)
-        dk_h = jnp.dot(dscore, query.q[h], preferred_element_type=jnp.float32)
-        dv = dv_h if dv is None else dv + dv_h
-        dk = dk_h if dk is None else dk + dk_h
-        dq_h = lax.dot_general(
-            k_block, dscore, (((0,), (0,)), ((), ())), preferred_element_type=jnp.float32
-        )
-        dqt[h] = dq_h if dqt[h] is None else dqt[h] + dq_h
-    return dk, dv
+    dscore = prob * (grads - query.delta[h]) * scaling
+    return prob.astype(jnp.bfloat16), dscore.astype(jnp.bfloat16)
+
+
+def fill(queries, kv_ref, firsts, causal, prob_ref, dscore_ref):
+    e = kv_ref.shape[1] // 2
+    rows = kv_ref.shape[0] // len(firsts)
+    for block, first in enumerate(firsts):
+        part = pl.ds(block * rows, rows)
+        k_block, v_block = kv_ref[part, :e], kv_ref[part, e:]
+        column = 0
+        for query in queries:
+            for h in range(query.heads):
+                prob, dscore = scores_block(query, h, k_block, v_block, first, causal)
+                prob_ref[part, column : column + query.rows] = prob
+                dscore_ref[part, column : column + query.rows] = dscore
+                column += query.rows
+
+
+def key_terms(queries, part, prob_ref, dscore_ref):
+    go = jnp.concatenate([g for query in queries for g in query.go], axis=0)
+    q = jnp.concatenate([g for query in queries for g in query.q], axis=0)
+    dk = jnp.dot(dscore_ref[part, :], q, preferred_element_type=jnp.float32)
+    dv = jnp.dot(prob_ref[part, :], go, preferred_element_type=jnp.float32)
+    return jnp.concatenate([dk, dv], axis=1)
+
+
+def query_terms(kv_ref, dscore_ref):
+    e = kv_ref.shape[1] // 2
+    return lax.dot_general(
+        kv_ref[:, :e], dscore_ref[...], (((0,), (0,)), ((), ())), preferred_element_type=jnp.float32
+    )
 
 
 def place():
@@ -111,81 +126,48 @@
     return jnp.where(behind >= 0, behind, -2 * chips) * (2 * rows)
 
 
-def own_kernel(heads, lens_ref, pay_ref, kv_ref, dqt_ref, keep_ref, give_ref):
+def own_kernel(heads, lens_ref, pay_ref, kv_ref, dqt_ref, keep_ref, give_ref, prob_ref, dscore_ref):
     rows = pay_ref.shape[0] - STAT_ROWS
     e = kv_ref.shape[1] // 2
     index, chip, core = place()
     query = Query(pay_ref, heads, index * rows, lens_ref)
-    dqt = [None] * heads
-    for half in range(2):
-        part = pl.ds(half * rows, rows)
-        dk, dv = key_terms(
-            query, kv_ref[part, :e], kv_ref[part, e:], (2 * chip + half) * rows, True, dqt
-        )
-
-        @pl.when(core == half)
-        def _():
-            keep_ref[:, :e] = dk
-            keep_ref[:, e:] = dv
-
-        @pl.when(core != half)
-        def _():
-            give_ref[:, :e] = dk
-            give_ref[:, e:] = dv
-
+    firsts = [(2 * chip + half) * rows for half in range(2)]
+    fill([query], kv_ref, firsts, True, prob_ref, dscore_ref)
+    for out_ref, half in ((give_ref, 1 - core), (keep_ref, core)):
+        part = pl.ds(pl.multiple_of(half * rows, rows), rows)
+        out_ref[...] = key_terms([query], part, prob_ref, dscore_ref)
+    dqt = query_terms(kv_ref, dscore_ref)
     for h in range(heads):
-        dqt_ref[h * e : (h + 1) * e, :] = dqt[h]
-
-
-def near_kernel(heads, chips, lens_ref, pay_ref, kv_ref, dqt_in_ref, dqt_ref, terms_ref):
+        dqt_ref[h * e : (h + 1) * e, :] = dqt[:, h * rows : (h + 1) * rows]
+
+
+def cross_kernel(
+    heads, chips, lens_ref, pay_ref, far_ref, kv_ref, dqt_in_ref, dqt_ref, back_ref, keep_ref, give_ref,
+    prob_ref, dscore_ref
+):
     rows = pay_ref.shape[0] - STAT_ROWS
     e = kv_ref.shape[1] // 2
     index, chip, core = place()
-    query = Query(pay_ref, heads, index * rows, lens_ref)
-    dqt = [dqt_in_ref[h * e : (h + 1) * e, :] for h in range(heads)]
-    for half in range(2):
-        for b in range(2):
-            part = pl.ds((half * 2 + b) * rows, rows)
-            first = block_start(chip, b + 1, chips, rows) + half * rows
-            dk, dv = key_terms(query, kv_ref[part, :e], kv_ref[part, e:], first, False, dqt)
-            terms_ref[part, :e] = dk
-            terms_ref[part, e:] = dv
+    own = Query(pay_ref, heads, index * rows, lens_ref)
+    far = Query(far_ref, heads, (index + 4) * rows, lens_ref)
+    far.start = jnp.where(chip + 2 < chips, far.start, 4 * chips * rows)
+    firsts = [
+        block_start(chip, b + 1, chips, rows) + half * rows for half in range(2) for b in range(2)
+    ]
+    fill([own, far], kv_ref, firsts, False, prob_ref, dscore_ref)
+    for out_ref, half in ((give_ref, 1 - core), (keep_ref, core)):
+        part = pl.ds(pl.multiple_of(half * 2 * rows, rows), 2 * rows)
+        out_ref[...] = key_terms([own, far], part, prob_ref, dscore_ref).astype(out_ref.dtype)
+    dqt = query_terms(kv_ref, dscore_ref)
     for h in range(heads):
-        dqt_ref[h * e : (h + 1) * e, :] = dqt[h]
-
-
-def far_kernel(heads, chips, lens_ref, pay_ref, kv_ref, terms_ref, dqt_ref, keep_ref, give_ref):
-    rows = pay_ref.shape[0] - STAT_ROWS
-    e = kv_ref.shape[1] // 2
-    index, chip, core = place()
-    ahead = chip + 2
-    query = Query(pay_ref, heads, (index + 4) * rows, lens_ref)
-    query.start = jnp.where(ahead < chips, query.start, 4 * chips * rows)
-    dqt = [None] * heads
-    for half in range(2):
-        for b in range(2):
-            part = pl.ds((half * 2 + b) * rows, rows)
-            first = block_start(chip, b + 1, chips, rows) + half * rows
-            dk, dv = key_terms(query, kv_ref[part, :e], kv_ref[part, e:], first, False, dqt)
-            dk = dk + terms_ref[part, :e]
-            dv = dv + terms_ref[part, e:]
-            out = pl.ds(b * rows, rows)
-
-            @pl.when(core == half)
-            def _():
-                keep_ref[out, :e] = dk
-                keep_ref[out, e:] = dv
-
-            @pl.when(core != half)
-            def _():
-                give_ref[out, :e] = dk.astype(jnp.bfloat16)
-                give_ref[out, e:] = dv.astype(jnp.bfloat16)
-
-    for h in range(heads):
-        dqt_ref[h * e : (h + 1) * e, :] = dqt[h].astype(jnp.bfloat16)
-
-
-def pair_kernel(keep_ref, both_ref, near_ref, far_ref):
+        block = pl.ds(h * e, e)
+        dqt_ref[block, :] = dqt_in_ref[block, :] + dqt[:, h * rows : (h + 1) * rows]
+        far_part = dqt[:, (heads + h) * rows : (heads + h + 1) * rows]
+        back_ref[block, :] = far_part.astype(jnp.bfloat16)
+
+
+def pair_kernel(keep_ref, both_ref, back_ref, near_ref, far_ref, send_ref):
+    send_ref[...] = back_ref[...]
     count = keep_ref.shape[0]
     rows = count // 2
     _, _, core = place()
@@ -195,14 +177,11 @@
     far_ref[...] = total[rows:]
 
 
-def query_kernel(dqt_ref, back_ref, dq_ref):
-    dq_ref[...] = (dqt_ref[...] + back_ref[...].astype(jnp.float32)).T.astype(jnp.bfloat16)
-
-
-def key_kernel(keep_ref, both_ref, near_ref, far_ref, dk_ref, dv_ref):
+def final_kernel(dqt_ref, keep_ref, both_ref, far_ref, back_ref, near_ref, dq_ref, dk_ref, dv_ref):
     rows = keep_ref.shape[0]
     e = keep_ref.shape[1] // 2
     _, _, core = place()
+    dq_ref[...] = (dqt_ref[...] + back_ref[...].astype(jnp.float32)).T.astype(jnp.bfloat16)
     other = both_ref[pl.ds(pl.multiple_of((1 - core) * rows, rows), rows), :]
     total = keep_ref[...] + other
     total = total + near_ref[...].astype(jnp.float32) + far_ref[...].astype(jnp.float32)
@@ -271,34 +250,36 @@
         "own",
         unit,
         1,
+        scratch=[pltpu.VMEM((2 * rows, heads * rows), bf16)] * 2,
     )(doc_lengths, pay, kv_own)
+    kv_near, kv_far, pay_far = lax.optimization_barrier((kv_near, kv_far, pay_far))
     kv_back = pair_gather(jnp.concatenate([kv_near, kv_far], axis=0))
-    dqt, terms = call(
-        functools.partial(near_kernel, heads, chips),
-        [((width, rows), f32), ((4 * rows, 2 * e), f32)],
-        "near",
-        2 * unit,
+    dqt, dqt_far, keep, give = call(
+        functools.partial(cross_kernel, heads, chips),
+        [
+            ((width, rows), f32),
+            ((width, rows), bf16),
+            ((2 * rows, 2 * e), f32),
+            ((2 * rows, 2 * e), bf16),
+        ],
+        "cross",
+        4 * unit,
         1,
-    )(doc_lengths, pay, kv_back, dqt)
-    dqt_far, keep, give = call(
-        functools.partial(far_kernel, heads, chips),
-        [((width, rows), bf16), ((2 * rows, 2 * e), f32), ((2 * rows, 2 * e), bf16)],
-        "far",
-        2 * unit,
-        1,
-    )(doc_lengths, pay_far, kv_back, terms)
-    dqt_back = shift(dqt_far, 4)
+        scratch=[pltpu.VMEM((4 * rows, 2 * heads * rows), bf16)] * 2,
+    )(doc_lengths, pay, pay_far, kv_back, dqt)
     both = pair_gather(give)
-    to_near, to_far = call(
-        pair_kernel, [((rows, 2 * e), bf16), ((rows, 2 * e), bf16)], "pair"
-    )(keep, both)
+    to_near, to_far, to_query = call(
+        pair_kernel,
+        [((rows, 2 * e), bf16), ((rows, 2 * e), bf16), ((width, rows), bf16)],
+        "pair",
+    )(keep, both, dqt_far)
+    dqt_back = shift(to_query, 4)
     from_far = shift(to_far, -4)
     from_near = shift(to_near, -2)
     both_own = pair_gather(give_own)
-    (grad_query,) = call(query_kernel, [((rows, width), bf16)], "grad_query")(dqt, dqt_back)
-    grad_key, grad_value = call(
-        key_kernel, [((rows, e), bf16), ((rows, e), bf16)], "grad_key"
-    )(keep_own, both_own, from_near, from_far)
+    grad_query, grad_key, grad_value = call(
+        final_kernel, [((rows, width), bf16), ((rows, e), bf16), ((rows, e), bf16)], "final"
+    )(dqt, keep_own, both_own, from_far, dqt_back, from_near)
     return (grad_query, grad_key, grad_value)
 
 

time: 53.1 us -> 46.9 us (0.88)
  Pallas kernels: 10.7 us -> 7.05 us
  waiting for transfers between devices: 4.5 us -> 1.92 us
  blocking collectives: 15.2 us -> 16.3 us
  starting transfers between devices: 21.6 us -> 20.6 us
    pallas_call x7 -> x5, Pallas kernels: 10.7 us -> 7.05 us  [run(): pl.pallas_call(kernel, out_shape=[jax.ShapeDtypeStruct(s, d) for s, d in...]
    ppermute x6, waiting for transfers between devices: 4.5 us -> 1.92 us  [shift(): return lax.ppermute(x, 'ctx', [(i, (i + by) % count) for i in range(count)])]
    all_gather x4, blocking collectives: 15.2 us -> 16.3 us  [pair_gather(): return lax.all_gather(x, 'ctx', axis=0, tiled=True, axis_index_groups=pairs)]
    ppermute x6, starting transfers between devices: 21.6 us -> 20.6 us  [shift(): return lax.ppermute(x, 'ctx', [(i, (i + by) % count) for i in range(count)])]
  transfers between devices with their start and end apart: 6 -> 6, of which waited for: 1 -> 2; matrix products, arithmetic and copies ran while one was open for 0% -> 0% of each run, Pallas kernels for 11% -> 3%
where the time goes in v3:
time: 46.9 us; the launch traced here: 46.6 us
  starting transfers between devices  20.6 us (44%)
  blocking collectives  16.3 us (35%)
  Pallas kernels  7.05 us (15%)
  waiting for transfers between devices  1.92 us (4%)
  between operations  0.73 us (2%)
    ppermute x6, starting transfers between devices, shift(): return lax.ppermute(x, 'ctx', [(i, (i + by) % count) for i in range(count)])  20.6 us
    all_gather x4, blocking collectives, pair_gather(): return lax.all_gather(x, 'ctx', axis=0, tiled=True, axis_index_groups=pairs)  16.3 us
    pallas_call x5, Pallas kernels, run(): pl.pallas_call(kernel, out_shape=[jax.ShapeDtypeStruct(s, d) for s, d in...  7.05 us
    ppermute x6, waiting for transfers between devices, shift(): return lax.ppermute(x, 'ctx', [(i, (i + by) % count) for i in range(count)])  1.92 us
  transfers between devices with their start and end apart: 6, of which 2 were waited for; matrix products, arithmetic and copies ran while one was open for 0% of the time, Pallas kernels for 3%

profile of v3, /device:TPU:1, one launch (start us, length us, event | category | flops | bytes accessed | tf_op | source)
XLA Modules:
  0.0 46.6 jit_solution(16848907777159598722)
XLA Ops:
  0.6 1.2 %prep.1 = (bf16[272,512]{1,0:T(8,128)(2,1)S(1)}, bf16[256,256]{1,0:T(8,128)(2,1)S(1)}) custom-call(bf16[256,256]{1,0:T(8,128)(2,1)} %q_ref.1, bf16[256,256]{1,0:T(8,128)(2,1)} %go_ref.1, bf16[256,256]{1,0:T(8,128)(2,1)} %out_ref.1, f32[2,256]{1,0:T(2,128)} %norm_ref.1, bf16[256,128]{1,0:T(8,128)(2,1)} %k_ref.1, bf16[256,128]{1,0:T(8,128)(2,1)} %v_ref.1), custom_call_target="tpu_custom_call" | custom-call | bytes 526336 | tf_op jit(solution)/shard_map/prep/pallas_call | solution.py:197
  1.8 6.7 %collective-permute-start.2 = (bf16[272,512]{1,0:T(8,128)(2,1)S(1)}, bf16[272,512]{1,0:T(8,128)(2,1)S(1)}, u32[]{:S(2)}, u32[]{:S(2)}) collective-permute-start(bf16[272,512]{1,0:T(8,128)(2,1)S(1)} %get-tuple-element.18.pay_ref), channel_id=1, source_target_pairs={{0,384},{32,416},{64,448},{96,480},{128,0},{160,32},{192,64},{224,... | collective-permute-start | bytes 835592 | tf_op jit(solution)/shard_map/ppermute | solution.py:221
  8.5 0.0 copy-start
  8.6 1.9 %collective-permute-start.1 = (bf16[256,256]{1,0:T(8,128)(2,1)S(1)}, bf16[256,256]{1,0:T(8,128)(2,1)S(1)}, u32[]{:S(2)}, u32[]{:S(2)}) collective-permute-start(bf16[256,256]{1,0:T(8,128)(2,1)S(1)} %get-tuple-element.19), channel_id=1, source_target_pairs={{0,128},{32,160},{64,192},{96,224},{128,256},{160,288},{192,320},{... | collective-permute-start | bytes 393224 | tf_op jit(solution)/shard_map/ppermute | solution.py:221
  10.5 2.3 %collective-permute-start = (bf16[256,256]{1,0:T(8,128)(2,1)S(1)}, bf16[256,256]{1,0:T(8,128)(2,1)S(1)}, u32[]{:S(2)}, u32[]{:S(2)}) collective-permute-start(bf16[256,256]{1,0:T(8,128)(2,1)S(1)} %get-tuple-element.19), channel_id=1, source_target_pairs={{0,64},{32,96},{64,128},{96,160},{128,192},{160,224},{192,256},{22... | collective-permute-start | bytes 393224 | tf_op jit(solution)/shard_map/ppermute | solution.py:221
  12.8 6.2 %all_gather.13.kv_ref = bf16[512,256]{1,0:T(8,128)(2,1)S(1)} all-gather(bf16[256,256]{1,0:T(8,128)(2,1)S(1)} %get-tuple-element.19), channel_id=1, replica_groups={{0,32},{64,96},{128,160},{192,224},{256,288},{320,352},{384,416},{448,4..., dimensions={0}, use_global_device_ids=true | all-gather | bytes 393216 | tf_op jit(solution)/shard_map/all_gather | solution.py:224
  19.0 0.0 copy-done
  19.0 1.5 %own.1 = (f32[256,256]{1,0:T(8,128)S(1)}, f32[256,256]{1,0:T(8,128)S(1)}, f32[256,256]{1,0:T(8,128)S(1)}) custom-call(s32[4]{0:T(128)S(1)} %copy-done, bf16[272,512]{1,0:T(8,128)(2,1)S(1)} %get-tuple-element.18.pay_ref, bf16[512,256]{1,0:T(8,128)(2,1)S(1)} %all_gather.13.kv_ref), custom_call_target="tpu_custom_call" | custom-call | flops 335544320 | bytes 540688 | tf_op jit(solution)/shard_map/own/pallas_call | solution.py:197
  20.5 0.0 collective-permute-done.1
  20.5 0.2 collective-permute-done
  20.8 0.0 collective-permute-done.2.far_ref
  20.8 4.9 %all_gather.12.kv_ref = bf16[1024,256]{1,0:T(8,128)(2,1)S(1)} all-gather(bf16[512,256]{1,0:T(8,128)(2,1)S(1)} %pad_maximum_fusion), channel_id=1, replica_groups={{0,32},{64,96},{128,160},{192,224},{256,288},{320,352},{384,416},{448,4..., dimensions={0}, use_global_device_ids=true | all-gather | bytes 786432 | tf_op jit(solution)/shard_map/all_gather | solution.py:224
  25.7 3.5 %cross.1 = (f32[256,256]{1,0:T(8,128)S(1)}, bf16[256,256]{1,0:T(8,128)(2,1)S(1)}, f32[512,256]{1,0:T(8,128)S(1)}, bf16[512,256]{1,0:T(8,128)(2,1)S(1)}) custom-call(s32[4]{0:T(128)S(1)} %copy-done, bf16[272,512]{1,0:T(8,128)(2,1)S(1)} %get-tuple-element.18.pay_ref, bf16[272,512]{1,0:T(8,128)(2,1)S(1)} %collective-permute-done.2.far_ref, ...), custom_call_target="tpu_custom_call" | custom-call | flops 1342177280 | bytes 1343504 | tf_op jit(solution)/shard_map/cross/pallas_call | solution.py:197
  29.2 2.2 %all_gather.15.both_ref = bf16[1024,256]{1,0:T(8,128)(2,1)S(1)} all-gather(bf16[512,256]{1,0:T(8,128)(2,1)S(1)} %get-tuple-element.28), channel_id=1, replica_groups={{0,32},{64,96},{128,160},{192,224},{256,288},{320,352},{384,416},{448,4..., dimensions={0}, use_global_device_ids=true | all-gather | bytes 786432 | tf_op jit(solution)/shard_map/all_gather | solution.py:224
  31.3 0.1 pair.1
  31.4 3.7 %collective-permute-start.3 = (bf16[256,256]{1,0:T(8,128)(2,1)S(1)}, bf16[256,256]{1,0:T(8,128)(2,1)S(1)}, u32[]{:S(2)}, u32[]{:S(2)}) collective-permute-start(bf16[256,256]{1,0:T(8,128)(2,1)S(1)} %get-tuple-element.30), channel_id=1, source_target_pairs={{0,384},{32,416},{64,448},{96,480},{128,0},{160,32},{192,64},{224,... | collective-permute-start | bytes 393224 | tf_op jit(solution)/shard_map/ppermute | solution.py:221
  35.2 2.4 %collective-permute-start.4 = (bf16[256,256]{1,0:T(8,128)(2,1)S(1)}, bf16[256,256]{1,0:T(8,128)(2,1)S(1)}, u32[]{:S(2)}, u32[]{:S(2)}) collective-permute-start(bf16[256,256]{1,0:T(8,128)(2,1)S(1)} %get-tuple-element.31), channel_id=1, source_target_pairs={{0,128},{32,160},{64,192},{96,224},{128,256},{160,288},{192,320},{... | collective-permute-start | bytes 393224 | tf_op jit(solution)/shard_map/ppermute | solution.py:221
  37.6 3.5 %collective-permute-start.5 = (bf16[256,256]{1,0:T(8,128)(2,1)S(1)}, bf16[256,256]{1,0:T(8,128)(2,1)S(1)}, u32[]{:S(2)}, u32[]{:S(2)}) collective-permute-start(bf16[256,256]{1,0:T(8,128)(2,1)S(1)} %get-tuple-element.32), channel_id=1, source_target_pairs={{0,448},{32,480},{64,0},{96,32},{128,64},{160,96},{192,128},{224,1... | collective-permute-start | bytes 393224 | tf_op jit(solution)/shard_map/ppermute | solution.py:221
  41.1 3.0 %all_gather.14.both_ref = f32[512,256]{1,0:T(8,128)S(1)} all-gather(f32[256,256]{1,0:T(8,128)S(1)} %get-tuple-element.26), channel_id=1, replica_groups={{0,32},{64,96},{128,160},{192,224},{256,288},{320,352},{384,416},{448,4..., dimensions={0}, use_global_device_ids=true | all-gather | bytes 786432 | tf_op jit(solution)/shard_map/all_gather | solution.py:224
  44.1 0.0 collective-permute-done.3.far_ref
  44.1 1.7 %collective-permute-done.4.back_ref = bf16[256,256]{1,0:T(8,128)(2,1)S(1)} collective-permute-done((bf16[256,256]{1,0:T(8,128)(2,1)S(1)}, bf16[256,256]{1,0:T(8,128)(2,1)S(1)}, u32[]{:S(2)}, u32[]{:S(2)}) %collective-permute-start.4) | collective-permute-done | bytes 131104 | tf_op jit(solution)/shard_map/ppermute | solution.py:221
  45.8 0.0 collective-permute-done.5.near_ref
  45.8 0.8 %final.1 = (bf16[256,256]{1,0:T(8,128)(2,1)}, bf16[256,128]{1,0:T(8,128)(2,1)}, bf16[256,128]{1,0:T(8,128)(2,1)}) custom-call(f32[256,256]{1,0:T(8,128)S(1)} %get-tuple-element.24.dqt_ref, f32[256,256]{1,0:T(8,128)S(1)} %get-tuple-element.25.keep_ref, f32[512,256]{1,0:T(8,128)S(1)} %all_gather.14.both_ref, ...), custom_call_target="tpu_custom_call" | custom-call | bytes 1441792 | tf_op jit(solution)/shard_map/final/pallas_call | solution.py:197
  (1 shorter events, 0.0 us)
Async XLA Ops:
  1.8 18.9 %collective-permute-start.2 = (bf16[272,512]{1,0:T(8,128)(2,1)S(1)}, bf16[272,512]{1,0:T(8,128)(2,1)S(1)}, u32[]{:S(2)}, u32[]{:S(2)}) collective-permute-start(bf16[272,512]{1,0:T(8,128)(2,1)S(1)} %get-tuple-element.18.pay_ref), channel_id=1, source_target_pairs={{0,384},{32,416},{64,448},{96,480},{128,0},{160,32},{192,64},{224,... | collective-permute-start | bytes 835592 | tf_op jit(solution)/shard_map/ppermute | solution.py:221
  8.5 10.5 %copy-start = (s32[4]{0:T(128)S(1)}, s32[4]{0:T(128)}, u32[]{:S(2)}) copy-start(s32[4]{0:T(128)} %lens_ref.3) | copy-start | bytes 52
  8.6 12.0 %collective-permute-start.1 = (bf16[256,256]{1,0:T(8,128)(2,1)S(1)}, bf16[256,256]{1,0:T(8,128)(2,1)S(1)}, u32[]{:S(2)}, u32[]{:S(2)}) collective-permute-start(bf16[256,256]{1,0:T(8,128)(2,1)S(1)} %get-tuple-element.19), channel_id=1, source_target_pairs={{0,128},{32,160},{64,192},{96,224},{128,256},{160,288},{192,320},{... | collective-permute-start | bytes 393224 | tf_op jit(solution)/shard_map/ppermute | solution.py:221
  10.5 10.3 %collective-permute-start = (bf16[256,256]{1,0:T(8,128)(2,1)S(1)}, bf16[256,256]{1,0:T(8,128)(2,1)S(1)}, u32[]{:S(2)}, u32[]{:S(2)}) collective-permute-start(bf16[256,256]{1,0:T(8,128)(2,1)S(1)} %get-tuple-element.19), channel_id=1, source_target_pairs={{0,64},{32,96},{64,128},{96,160},{128,192},{160,224},{192,256},{22... | collective-permute-start | bytes 393224 | tf_op jit(solution)/shard_map/ppermute | solution.py:221
  31.4 12.7 %collective-permute-start.3 = (bf16[256,256]{1,0:T(8,128)(2,1)S(1)}, bf16[256,256]{1,0:T(8,128)(2,1)S(1)}, u32[]{:S(2)}, u32[]{:S(2)}) collective-permute-start(bf16[256,256]{1,0:T(8,128)(2,1)S(1)} %get-tuple-element.30), channel_id=1, source_target_pairs={{0,384},{32,416},{64,448},{96,480},{128,0},{160,32},{192,64},{224,... | collective-permute-start | bytes 393224 | tf_op jit(solution)/shard_map/ppermute | solution.py:221
  35.2 10.6 %collective-permute-start.4 = (bf16[256,256]{1,0:T(8,128)(2,1)S(1)}, bf16[256,256]{1,0:T(8,128)(2,1)S(1)}, u32[]{:S(2)}, u32[]{:S(2)}) collective-permute-start(bf16[256,256]{1,0:T(8,128)(2,1)S(1)} %get-tuple-element.31), channel_id=1, source_target_pairs={{0,128},{32,160},{64,192},{96,224},{128,256},{160,288},{192,320},{... | collective-permute-start | bytes 393224 | tf_op jit(solution)/shard_map/ppermute | solution.py:221
  37.6 8.2 %collective-permute-start.5 = (bf16[256,256]{1,0:T(8,128)(2,1)S(1)}, bf16[256,256]{1,0:T(8,128)(2,1)S(1)}, u32[]{:S(2)}, u32[]{:S(2)}) collective-permute-start(bf16[256,256]{1,0:T(8,128)(2,1)S(1)} %get-tuple-element.32), channel_id=1, source_target_pairs={{0,448},{32,480},{64,0},{96,32},{128,64},{160,96},{192,128},{224,1... | collective-permute-start | bytes 393224 | tf_op jit(solution)/shard_map/ppermute | solution.py:221

commit v4 on v3

v4 whole, which is shorter than its diff:
```python
import functools
import math

import jax
import jax.numpy as jnp
from jax import lax
from jax.experimental import pallas as pl
from jax.experimental.pallas import tpu as pltpu
from jax.sharding import PartitionSpec as P

LOG2E = math.log2(math.e)
STAT_ROWS = 16


def split3(value):
    high = value.astype(jnp.bfloat16)
    rest = value - high.astype(jnp.float32)
    mid = rest.astype(jnp.bfloat16)
    low = (rest - mid.astype(jnp.float32)).astype(jnp.bfloat16)
    return high, mid, low


def prep_kernel(q_ref, go_ref, out_ref, norm_ref, k_ref, v_ref, pay_ref, kv_ref, *scratch):
    out_buf, norm_buf, sems = scratch
    rows, width = q_ref.shape
    heads = norm_ref.shape[0]
    e = width // heads
    moves = [
        (go_ref, pay_ref.at[rows : 2 * rows]),
        (out_ref, out_buf),
        (norm_ref, norm_buf),
        (q_ref, pay_ref.at[:rows]),
        (k_ref, kv_ref.at[:, :e]),
        (v_ref, kv_ref.at[:, e:]),
    ]
    copies = [pltpu.make_async_copy(s, d, sems.at[i]) for i, (s, d) in enumerate(moves)]
    for copy in copies:
        copy.start()
    for copy in copies[:3]:
        copy.wait()
    product = pay_ref[rows : 2 * rows].astype(jnp.float32) * out_buf[...].astype(jnp.float32)
    product_t = product.T
    stats = []
    for h in range(heads):
        delta = jnp.sum(product_t[h * e : (h + 1) * e], axis=0, keepdims=True)
        stats += list(split3(norm_buf[h : h + 1, :] * LOG2E)) + list(split3(delta))
    stats += [jnp.zeros((1, rows), jnp.bfloat16)] * (STAT_ROWS - len(stats))
    table = jnp.concatenate([s.astype(jnp.float32) for s in stats], axis=0)
    pay_ref[2 * rows :, :rows] = table.astype(jnp.bfloat16)
    for copy in copies[3:]:
        copy.wait()


class Query:
    def __init__(self, pay_ref, block, heads, first, lens_ref):
        rows, width = (pay_ref.shape[0] // 2 - STAT_ROWS) // 2, pay_ref.shape[1]
        e = width // heads
        base = block * (2 * rows + STAT_ROWS)
        self.heads, self.rows, self.e = heads, rows, e
        self.q = [pay_ref[base : base + rows, h * e : (h + 1) * e] for h in range(heads)]
        self.go = [
            pay_ref[base + rows : base + 2 * rows, h * e : (h + 1) * e] for h in range(heads)
        ]
        table = pay_ref[base + 2 * rows : base + 2 * rows + STAT_ROWS, :rows].astype(jnp.float32)
        row = lambda i: table[i : i + 1]
        self.norm = [row(6 * h) + row(6 * h + 1) + row(6 * h + 2) for h in range(heads)]
        self.delta = [row(6 * h + 3) + row(6 * h + 4) + row(6 * h + 5) for h in range(heads)]
        self.pos = first + lax.broadcasted_iota(jnp.int32, (1, rows), 1)
        self.start = jnp.zeros((1, rows), jnp.int32)
        end = jnp.int32(0)
        for d in range(lens_ref.shape[0]):
            end = end + lens_ref[d]
            self.start = jnp.where(end <= self.pos, end, self.start)


def scores_block(query, h, k_block, v_block, k_first, causal):
    contract = (((1,), (1,)), ((), ()))
    scaling = query.e ** (-0.5)
    scores = lax.dot_general(k_block, query.q[h], contract, preferred_element_type=jnp.float32)
    grads = lax.dot_general(v_block, query.go[h], contract, preferred_element_type=jnp.float32)
    k_pos = k_first + lax.broadcasted_iota(jnp.int32, (k_block.shape[0], 1), 0)
    allowed = k_pos >= query.start
    if causal:
        allowed = allowed & (k_pos <= query.pos)
    prob = jnp.where(allowed, jnp.exp2(scores * (scaling * LOG2E) - query.norm[h]), 0.0)
    dscore = prob * (grads - query.delta[h]) * scaling
    return prob.astype(jnp.bfloat16), dscore.astype(jnp.bfloat16)


def fill(queries, blocks, firsts, causal, prob_ref, dscore_ref):
    for i, (block, first) in enumerate(zip(blocks, firsts)):
        rows, e = block.shape[0], block.shape[1] // 2
        part = pl.ds(i * rows, rows)
        k_block, v_block = block[:, :e], block[:, e:]
        column = 0
        for query in queries:
            for h in range(query.heads):
                prob, dscore = scores_block(query, h, k_block, v_block, first, causal)
                prob_ref[part, column : column + query.rows] = prob
                dscore_ref[part, column : column + query.rows] = dscore
                column += query.rows


def key_terms(queries, part, prob_ref, dscore_ref):
    go = jnp.concatenate([g for query in queries for g in query.go], axis=0)
    q = jnp.concatenate([g for query in queries for g in query.q], axis=0)
    dk = jnp.dot(dscore_ref[part, :], q, preferred_element_type=jnp.float32)
    dv = jnp.dot(prob_ref[part, :], go, preferred_element_type=jnp.float32)
    return jnp.concatenate([dk, dv], axis=1)


def query_terms(keys, dscore):
    return lax.dot_general(
        keys, dscore, (((0,), (0,)), ((), ())), preferred_element_type=jnp.float32
    )


def place():
    index = lax.axis_index("ctx")
    return index, index // 2, lax.rem(index, 2)


def block_start(chip, back, chips, rows):
    behind = chip - back
    return jnp.where(behind >= 0, behind, -2 * chips) * (2 * rows)


def own_kernel(heads, lens_ref, pay_ref, kv_ref, dqt_ref, dkv_ref, prob_ref, dscore_ref):
    rows, e = kv_ref.shape[0], kv_ref.shape[1] // 2
    index, chip, core = place()
    queries = [Query(pay_ref, i, heads, (2 * chip + i) * rows, lens_ref) for i in range(2)]
    fill(queries, [kv_ref[...]], [index * rows], True, prob_ref, dscore_ref)
    dkv_ref[...] = key_terms(queries, pl.ds(0, rows), prob_ref, dscore_ref)
    dqt = query_terms(kv_ref[:, :e], dscore_ref[...])
    for i in range(2):
        for h in range(heads):
            column = (i * heads + h) * rows
            dqt_ref[(i * heads + h) * e : (i * heads + h + 1) * e, :] = dqt[:, column : column + rows]


def cross_kernel(
    heads, chips, lens_ref, own_ref, far_ref, same_ref, other_ref, dqt_in_ref,
    dkv_ref, give_ref, keep_far_ref, keep_own_ref, prob_ref, dscore_ref, dqt_ref
):
    rows, e = same_ref.shape[0], same_ref.shape[1] // 2
    width = heads * e
    index, chip, core = place()
    own = [Query(own_ref, i, heads, (2 * chip + i) * rows, lens_ref) for i in range(2)]
    far = [Query(far_ref, i, heads, (2 * chip + 4 + i) * rows, lens_ref) for i in range(2)]
    for query in far:
        query.start = jnp.where(chip + 2 < chips, query.start, 4 * chips * rows)
    first = block_start(chip, 1 + core, chips, rows)
    firsts = [first + core * rows, first + (1 - core) * rows]
    fill(own + far, [same_ref[...], other_ref[...]], firsts, False, prob_ref, dscore_ref)
    for i, half in enumerate((core, 1 - core)):
        out = pl.ds(pl.multiple_of(half * rows, rows), rows)
        terms = key_terms(own + far, pl.ds(i * rows, rows), prob_ref, dscore_ref)
        dkv_ref[out, :] = terms.astype(jnp.bfloat16)
    dqt = query_terms(same_ref[:, :e], dscore_ref[:rows, :])
    dqt = dqt + query_terms(other_ref[:, :e], dscore_ref[rows:, :])
    for i in range(4 * heads):
        dqt_ref[i * e : (i + 1) * e, :] = dqt[:, i * rows : (i + 1) * rows]
    mine = lambda ref, i: ref[pl.ds(pl.multiple_of(i * width, width), width), :]
    keep_own_ref[...] = mine(dqt_ref, core) + mine(dqt_in_ref, core)
    keep_far_ref[...] = mine(dqt_ref, 2 + core)
    give_ref[:width, :] = mine(dqt_ref, 3 - core).astype(jnp.bfloat16)
    given = mine(dqt_ref, 1 - core) + mine(dqt_in_ref, 1 - core)
    give_ref[width:, :] = given.astype(jnp.bfloat16)


def pair_kernel(keep_ref, both_ref, send_ref):
    width = keep_ref.shape[0]
    _, _, core = place()
    other = both_ref[pl.ds(pl.multiple_of((1 - core) * 2 * width, width), width), :]
    send_ref[...] = (keep_ref[...] + other.astype(jnp.float32)).astype(jnp.bfloat16)


def final_kernel(keep_ref, both_ref, dkv_ref, back_ref, dqt_back_ref, dq_ref, dk_ref, dv_ref):
    width = keep_ref.shape[0]
    rows, e = dkv_ref.shape[0], dkv_ref.shape[1] // 2
    _, _, core = place()
    take = lambda ref, i, size: ref[pl.ds(pl.multiple_of(i * size, size), size), :].astype(jnp.float32)
    dqt = keep_ref[...] + take(both_ref, 2 * (1 - core) + 1, width)
    dq_ref[...] = (dqt + dqt_back_ref[...].astype(jnp.float32)).T.astype(jnp.bfloat16)
    total = dkv_ref[...] + take(back_ref, core, rows) + take(back_ref, 2 + core, rows)
    dk_ref[...] = total[:, :e].astype(jnp.bfloat16)
    dv_ref[...] = total[:, e:].astype(jnp.bfloat16)


def call(kernel, outs, name, flops=0, smem=0, space=pltpu.VMEM, scratch=()):
    def run(*args):
        specs = [pl.BlockSpec(memory_space=pltpu.SMEM)] * smem
        specs += [pl.BlockSpec(memory_space=space)] * (len(args) - smem)
        moved = sum(a.size * a.dtype.itemsize for a in args)
        return pl.pallas_call(
            kernel,
            out_shape=[jax.ShapeDtypeStruct(s, d) for s, d in outs],
            in_specs=specs,
            out_specs=[pl.BlockSpec(memory_space=pltpu.VMEM)] * len(outs),
            scratch_shapes=list(scratch),
            cost_estimate=pl.CostEstimate(flops=flops, bytes_accessed=moved, transcendentals=0),
            compiler_params=pltpu.CompilerParams(vmem_limit_bytes=32 * 1024 * 1024),
            name=name,
        )(*args)

    return run


def body(queries, key_states, value_states, attn_out, grad_out, log_norm, doc_lengths):
    rows, width = queries.shape
    heads = log_norm.shape[0]
    e = key_states.shape[1]
    count = lax.axis_size("ctx")
    chips = count // 2
    pairs = [[2 * i, 2 * i + 1] for i in range(chips)]
    bf16, f32 = jnp.bfloat16, jnp.float32

    def shift(x, by_even, by_odd):
        moves = [(i, i + (by_odd if i % 2 else by_even)) for i in range(count)]
        return lax.ppermute(x, "ctx", [(i, j) for i, j in moves if 0 <= j < count])

    def pair_gather(x):
        return lax.all_gather(x, "ctx", axis=0, tiled=True, axis_index_groups=pairs)

    pay, kv = call(
        prep_kernel,
        [((2 * rows + STAT_ROWS, width), bf16), ((rows, 2 * e), bf16)],
        "prep",
        space=pltpu.HBM,
        scratch=[
            pltpu.VMEM((rows, width), bf16),
            pltpu.VMEM((heads, rows), f32),
            pltpu.SemaphoreType.DMA((6,)),
        ],
    )(
        *[
            pltpu.with_memory_space_constraint(x, pltpu.HBM)
            for x in (queries, grad_out, attn_out, log_norm, key_states, value_states)
        ]
    )
    pay_far = shift(pay, -4, -4)
    kv_same = shift(kv, 2, 4)
    kv_other = shift(kv, 5, 1)
    pay_own = pair_gather(pay)
    unit = 5 * 2 * heads * rows * 2 * rows * e
    dqt, dkv_own = call(
        functools.partial(own_kernel, heads),
        [((2 * width, rows), f32), ((rows, 2 * e), f32)],
        "own",
        unit,
        1,
        scratch=[pltpu.VMEM((rows, 2 * heads * rows), bf16)] * 2,
    )(doc_lengths, pay_own, kv)
    pay_ahead = pair_gather(pay_far)
    dkv, give, keep_far, keep_own = call(
        functools.partial(cross_kernel, heads, chips),
        [((2 * rows, 2 * e), bf16), ((2 * width, rows), bf16), ((width, rows), f32), ((width, rows), f32)],
        "cross",
        4 * unit,
        1,
        scratch=[pltpu.VMEM((2 * rows, 4 * heads * rows), bf16)] * 2
        + [pltpu.VMEM((4 * width, rows), f32)],
    )(doc_lengths, pay_own, pay_ahead, kv_same, kv_other, dqt)
    dkv_back = shift(dkv, -2, -4)
    both = pair_gather(give)
    (to_query,) = call(pair_kernel, [((width, rows), bf16)], "pair")(keep_far, both)
    dqt_back = shift(to_query, 4, 4)
    back = pair_gather(dkv_back)
    grad_query, grad_key, grad_value = call(
        final_kernel, [((rows, width), bf16), ((rows, e), bf16), ((rows, e), bf16)], "final"
    )(keep_own, both, dkv_own, back, dqt_back)
    return (grad_query, grad_key, grad_value)


def solution(mesh):
    rows = P(("dp", "ctx"), None)
    placed = (rows, rows, rows, rows, rows, P(None, ("dp", "ctx")), P("dp"))
    return jax.shard_map(
        body, mesh=mesh, in_specs=placed, out_specs=(rows, rows, rows), check_vma=False
    )
```

time: 46.9 us -> 43.2 us (0.921)
  blocking collectives: 16.3 us -> 11.2 us
  waiting for transfers between devices: 1.92 us -> 5.62 us
  starting transfers between devices: 20.6 us -> 18.5 us
    all_gather x4, blocking collectives: 16.3 us -> 11.2 us  [pair_gather(): return lax.all_gather(x, 'ctx', axis=0, tiled=True, axis_index_groups=pairs)]
    ppermute x6 -> x5, waiting for transfers between devices: 1.92 us -> 5.62 us  [shift(): return lax.ppermute(x, 'ctx', [(i, j) for i, j in moves if 0 <= j < count])]
    ppermute x6 -> x5, starting transfers between devices: 20.6 us -> 18.5 us  [shift(): return lax.ppermute(x, 'ctx', [(i, j) for i, j in moves if 0 <= j < count])]
  transfers between devices with their start and end apart: 6 -> 5, of which waited for: 2 -> 2; matrix products, arithmetic and copies ran while one was open for 0% -> 0% of each run, Pallas kernels for 3% -> 3%
where the time goes in v4:
time: 43.2 us; the launch traced here: 42.9 us
  starting transfers between devices  18.5 us (43%)
  blocking collectives  11.2 us (26%)
  Pallas kernels  6.97 us (16%)
  waiting for transfers between devices  5.62 us (13%)
  between operations  0.71 us (2%)
    ppermute x5, starting transfers between devices, shift(): return lax.ppermute(x, 'ctx', [(i, j) for i, j in moves if 0 <= j < count])  18.5 us
    all_gather x4, blocking collectives, pair_gather(): return lax.all_gather(x, 'ctx', axis=0, tiled=True, axis_index_groups=pairs)  11.2 us
    pallas_call x5, Pallas kernels, run(): pl.pallas_call(kernel, out_shape=[jax.ShapeDtypeStruct(s, d) for s, d in...  6.97 us
    ppermute x5, waiting for transfers between devices, shift(): return lax.ppermute(x, 'ctx', [(i, j) for i, j in moves if 0 <= j < count])  5.62 us
  transfers between devices with their start and end apart: 5, of which 2 were waited for; matrix products, arithmetic and copies ran while one was open for 0% of the time, Pallas kernels for 3%

profile of v4, /device:TPU:1, one launch (start us, length us, event | category | flops | bytes accessed | tf_op | source)
XLA Modules:
  0.0 42.9 jit_solution(6346471205331888948)
XLA Ops:
  0.6 1.2 %prep.1 = (bf16[528,256]{1,0:T(8,128)(2,1)S(1)}, bf16[256,256]{1,0:T(8,128)(2,1)S(1)}) custom-call(bf16[256,256]{1,0:T(8,128)(2,1)} %q_ref.1, bf16[256,256]{1,0:T(8,128)(2,1)} %go_ref.1, bf16[256,256]{1,0:T(8,128)(2,1)} %out_ref.1, f32[2,256]{1,0:T(2,128)} %norm_ref.1, bf16[256,128]{1,0:T(8,128)(2,1)} %k_ref.1, bf16[256,128]{1,0:T(8,128)(2,1)} %v_ref.1), custom_call_target="tpu_custom_call" | custom-call | bytes 526336 | tf_op jit(solution)/shard_map/prep/pallas_call | solution.py:195
  1.8 1.3 %collective-permute-start = (bf16[528,256]{1,0:T(8,128)(2,1)S(1)}, bf16[528,256]{1,0:T(8,128)(2,1)S(1)}, u32[]{:S(2)}, u32[]{:S(2)}) collective-permute-start(bf16[528,256]{1,0:T(8,128)(2,1)S(1)} %get-tuple-element.11), channel_id=1, source_target_pairs={{128,0},{160,32},{192,64},{224,96},{256,128},{288,160},{320,192},{... | collective-permute-start | bytes 811016 | tf_op jit(solution)/shard_map/ppermute | solution.py:220
  3.1 0.0 copy-start
  3.1 4.6 %collective-permute-start.2 = (bf16[256,256]{1,0:T(8,128)(2,1)S(1)}, bf16[256,256]{1,0:T(8,128)(2,1)S(1)}, u32[]{:S(2)}, u32[]{:S(2)}) collective-permute-start(bf16[256,256]{1,0:T(8,128)(2,1)S(1)} %get-tuple-element.12.kv_ref), channel_id=1, source_target_pairs={{0,160},{32,64},{64,224},{96,128},{128,288},{160,192},{192,352},{2... | collective-permute-start | bytes 393224 | tf_op jit(solution)/shard_map/ppermute | solution.py:220
  7.7 5.2 %collective-permute-start.1 = (bf16[256,256]{1,0:T(8,128)(2,1)S(1)}, bf16[256,256]{1,0:T(8,128)(2,1)S(1)}, u32[]{:S(2)}, u32[]{:S(2)}) collective-permute-start(bf16[256,256]{1,0:T(8,128)(2,1)S(1)} %get-tuple-element.12.kv_ref), channel_id=1, source_target_pairs={{0,64},{32,160},{64,128},{96,224},{128,192},{160,288},{192,256},{2... | collective-permute-start | bytes 393224 | tf_op jit(solution)/shard_map/ppermute | solution.py:220
  12.9 2.2 %all_gather.12.pay_ref.own_ref = bf16[1056,256]{1,0:T(8,128)(2,1)S(1)} all-gather(bf16[528,256]{1,0:T(8,128)(2,1)S(1)} %get-tuple-element.11), channel_id=1, replica_groups={{0,32},{64,96},{128,160},{192,224},{256,288},{320,352},{384,416},{448,4..., dimensions={0}, use_global_device_ids=true | all-gather | bytes 811008 | tf_op jit(solution)/shard_map/all_gather | solution.py:223
  15.1 0.0 copy-done
  15.1 1.4 %own.1 = (f32[512,256]{1,0:T(8,128)S(1)}, f32[256,256]{1,0:T(8,128)S(1)}) custom-call(s32[4]{0:T(128)S(1)} %copy-done, bf16[1056,256]{1,0:T(8,128)(2,1)S(1)} %all_gather.12.pay_ref.own_ref, bf16[256,256]{1,0:T(8,128)(2,1)S(1)} %get-tuple-element.12.kv_ref), custom_call_target="tpu_custom_call" | custom-call | flops 335544320 | bytes 671760 | tf_op jit(solution)/shard_map/own/pallas_call | solution.py:195
  16.5 0.7 %collective-permute-done = bf16[528,256]{1,0:T(8,128)(2,1)S(1)} collective-permute-done((bf16[528,256]{1,0:T(8,128)(2,1)S(1)}, bf16[528,256]{1,0:T(8,128)(2,1)S(1)}, u32[]{:S(2)}, u32[]{:S(2)}) %collective-permute-start) | collective-permute-done | bytes 270368 | tf_op jit(solution)/shard_map/ppermute | solution.py:220
  17.3 4.6 %all_gather.13.far_ref = bf16[1056,256]{1,0:T(8,128)(2,1)S(1)} all-gather(bf16[528,256]{1,0:T(8,128)(2,1)S(1)} %collective-permute-done), channel_id=1, replica_groups={{0,32},{64,96},{128,160},{192,224},{256,288},{320,352},{384,416},{448,4..., dimensions={0}, use_global_device_ids=true | all-gather | bytes 811008 | tf_op jit(solution)/shard_map/all_gather | solution.py:223
  21.9 0.0 collective-permute-done.2.other_ref
  21.9 0.0 collective-permute-done.1.same_ref
  21.9 3.5 %cross.1 = (bf16[512,256]{1,0:T(8,128)(2,1)S(1)}, bf16[512,256]{1,0:T(8,128)(2,1)S(1)}, f32[256,256]{1,0:T(8,128)S(1)}, f32[256,256]{1,0:T(8,128)S(1)}) custom-call(s32[4]{0:T(128)S(1)} %copy-done, bf16[1056,256]{1,0:T(8,128)(2,1)S(1)} %all_gather.12.pay_ref.own_ref, bf16[1056,256]{1,0:T(8,128)(2,1)S(1)} %all_gather.13.far_ref, ...), custom_call_target="tpu_custom_call" | custom-call | flops 1342177280 | bytes 1867792 | tf_op jit(solution)/shard_map/cross/pallas_call | solution.py:195
  25.5 1.3 %collective-permute-start.3 = (bf16[512,256]{1,0:T(8,128)(2,1)S(1)}, bf16[512,256]{1,0:T(8,128)(2,1)S(1)}, u32[]{:S(2)}, u32[]{:S(2)}) collective-permute-start(bf16[512,256]{1,0:T(8,128)(2,1)S(1)} %get-tuple-element.17), channel_id=1, source_target_pairs={{64,0},{128,64},{160,32},{192,128},{224,96},{256,192},{288,160},{3... | collective-permute-start | bytes 786440 | tf_op jit(solution)/shard_map/ppermute | solution.py:220
  26.8 2.2 %all_gather.14.both_ref = bf16[1024,256]{1,0:T(8,128)(2,1)S(1)} all-gather(bf16[512,256]{1,0:T(8,128)(2,1)S(1)} %get-tuple-element.15), channel_id=1, replica_groups={{0,32},{64,96},{128,160},{192,224},{256,288},{320,352},{384,416},{448,4..., dimensions={0}, use_global_device_ids=true | all-gather | bytes 786432 | tf_op jit(solution)/shard_map/all_gather | solution.py:223
  29.0 6.1 %collective-permute-start.4 = (bf16[256,256]{1,0:T(8,128)(2,1)S(1)}, bf16[256,256]{1,0:T(8,128)(2,1)S(1)}, u32[]{:S(2)}, u32[]{:S(2)}) collective-permute-start(bf16[256,256]{1,0:T(8,128)(2,1)S(1)} %pair.1), channel_id=1, source_target_pairs={{0,128},{32,160},{64,192},{96,224},{128,256},{160,288},{192,320},{... | collective-permute-start | bytes 393224 | tf_op jit(solution)/shard_map/ppermute | solution.py:220
  35.1 4.9 %collective-permute-done.3 = bf16[512,256]{1,0:T(8,128)(2,1)S(1)} collective-permute-done((bf16[512,256]{1,0:T(8,128)(2,1)S(1)}, bf16[512,256]{1,0:T(8,128)(2,1)S(1)}, u32[]{:S(2)}, u32[]{:S(2)}) %collective-permute-start.3) | collective-permute-done | bytes 262176 | tf_op jit(solution)/shard_map/ppermute | solution.py:220
  40.0 2.2 %all_gather.15.back_ref = bf16[1024,256]{1,0:T(8,128)(2,1)S(1)} all-gather(bf16[512,256]{1,0:T(8,128)(2,1)S(1)} %collective-permute-done.3), channel_id=1, replica_groups={{0,32},{64,96},{128,160},{192,224},{256,288},{320,352},{384,416},{448,4..., dimensions={0}, use_global_device_ids=true | all-gather | bytes 786432 | tf_op jit(solution)/shard_map/all_gather | solution.py:223
  42.1 0.0 collective-permute-done.4.dqt_back_ref
  42.2 0.8 %final.1 = (bf16[256,256]{1,0:T(8,128)(2,1)}, bf16[256,128]{1,0:T(8,128)(2,1)}, bf16[256,128]{1,0:T(8,128)(2,1)}) custom-call(f32[256,256]{1,0:T(8,128)S(1)} %get-tuple-element.14.keep_ref, bf16[1024,256]{1,0:T(8,128)(2,1)S(1)} %all_gather.14.both_ref, f32[256,256]{1,0:T(8,128)S(1)} %get-tuple-element.16.dkv_ref, bf16[1024,256]{1,0:T(8,128)(2,1)S(1)} %all_gather.15.back_ref, ...), custom_call_target="tpu_custom_call" | custom-call | bytes 1703936 | tf_op jit(solution)/shard_map/final/pallas_call | solution.py:195
  (1 shorter events, 0.0 us)
Async XLA Ops:
  1.8 15.4 %collective-permute-start = (bf16[528,256]{1,0:T(8,128)(2,1)S(1)}, bf16[528,256]{1,0:T(8,128)(2,1)S(1)}, u32[]{:S(2)}, u32[]{:S(2)}) collective-permute-start(bf16[528,256]{1,0:T(8,128)(2,1)S(1)} %get-tuple-element.11), channel_id=1, source_target_pairs={{128,0},{160,32},{192,64},{224,96},{256,128},{288,160},{320,192},{... | collective-permute-start | bytes 811016 | tf_op jit(solution)/shard_map/ppermute | solution.py:220
  3.1 12.0 %copy-start = (s32[4]{0:T(128)S(1)}, s32[4]{0:T(128)}, u32[]{:S(2)}) copy-start(s32[4]{0:T(128)} %lens_ref.3) | copy-start | bytes 52
  3.1 18.8 %collective-permute-start.2 = (bf16[256,256]{1,0:T(8,128)(2,1)S(1)}, bf16[256,256]{1,0:T(8,128)(2,1)S(1)}, u32[]{:S(2)}, u32[]{:S(2)}) collective-permute-start(bf16[256,256]{1,0:T(8,128)(2,1)S(1)} %get-tuple-element.12.kv_ref), channel_id=1, source_target_pairs={{0,160},{32,64},{64,224},{96,128},{128,288},{160,192},{192,352},{2... | collective-permute-start | bytes 393224 | tf_op jit(solution)/shard_map/ppermute | solution.py:220
  7.7 14.2 %collective-permute-start.1 = (bf16[256,256]{1,0:T(8,128)(2,1)S(1)}, bf16[256,256]{1,0:T(8,128)(2,1)S(1)}, u32[]{:S(2)}, u32[]{:S(2)}) collective-permute-start(bf16[256,256]{1,0:T(8,128)(2,1)S(1)} %get-tuple-element.12.kv_ref), channel_id=1, source_target_pairs={{0,64},{32,160},{64,128},{96,224},{128,192},{160,288},{192,256},{2... | collective-permute-start | bytes 393224 | tf_op jit(solution)/shard_map/ppermute | solution.py:220
  25.5 14.5 %collective-permute-start.3 = (bf16[512,256]{1,0:T(8,128)(2,1)S(1)}, bf16[512,256]{1,0:T(8,128)(2,1)S(1)}, u32[]{:S(2)}, u32[]{:S(2)}) collective-permute-start(bf16[512,256]{1,0:T(8,128)(2,1)S(1)} %get-tuple-element.17), channel_id=1, source_target_pairs={{64,0},{128,64},{160,32},{192,128},{224,96},{256,192},{288,160},{3... | collective-permute-start | bytes 786440 | tf_op jit(solution)/shard_map/ppermute | solution.py:220
  29.0 13.2 %collective-permute-start.4 = (bf16[256,256]{1,0:T(8,128)(2,1)S(1)}, bf16[256,256]{1,0:T(8,128)(2,1)S(1)}, u32[]{:S(2)}, u32[]{:S(2)}) collective-permute-start(bf16[256,256]{1,0:T(8,128)(2,1)S(1)} %pair.1), channel_id=1, source_target_pairs={{0,128},{32,160},{64,192},{96,224},{128,256},{160,288},{192,320},{... | collective-permute-start | bytes 393224 | tf_op jit(solution)/shard_map/ppermute | solution.py:220

commit v5 on v4

--- a/solution.py
+++ b/solution.py
@@ -138,8 +138,23 @@
             dqt_ref[(i * heads + h) * e : (i * heads + h + 1) * e, :] = dqt[:, column : column + rows]
 
 
+def near_kernel(
+    heads, chips, lens_ref, own_ref, same_ref, dqt_in_ref, dqt_ref, dkv_ref, prob_ref, dscore_ref
+):
+    rows, e = same_ref.shape[0], same_ref.shape[1] // 2
+    index, chip, core = place()
+    own = [Query(own_ref, i, heads, (2 * chip + i) * rows, lens_ref) for i in range(2)]
+    first = block_start(chip, 1 + core, chips, rows) + core * rows
+    fill(own, [same_ref[...]], [first], False, prob_ref, dscore_ref)
+    dkv_ref[...] = key_terms(own, pl.ds(0, rows), prob_ref, dscore_ref)
+    dqt = query_terms(same_ref[:, :e], dscore_ref[...])
+    for i in range(2 * heads):
+        block = pl.ds(i * e, e)
+        dqt_ref[block, :] = dqt_in_ref[block, :] + dqt[:, i * rows : (i + 1) * rows]
+
+
 def cross_kernel(
-    heads, chips, lens_ref, own_ref, far_ref, same_ref, other_ref, dqt_in_ref,
+    heads, chips, lens_ref, own_ref, far_ref, same_ref, other_ref, dqt_in_ref, dkv_in_ref,
     dkv_ref, give_ref, keep_far_ref, keep_own_ref, prob_ref, dscore_ref, dqt_ref
 ):
     rows, e = same_ref.shape[0], same_ref.shape[1] // 2
@@ -150,22 +165,27 @@
     for query in far:
         query.start = jnp.where(chip + 2 < chips, query.start, 4 * chips * rows)
     first = block_start(chip, 1 + core, chips, rows)
-    firsts = [first + core * rows, first + (1 - core) * rows]
-    fill(own + far, [same_ref[...], other_ref[...]], firsts, False, prob_ref, dscore_ref)
-    for i, half in enumerate((core, 1 - core)):
-        out = pl.ds(pl.multiple_of(half * rows, rows), rows)
-        terms = key_terms(own + far, pl.ds(i * rows, rows), prob_ref, dscore_ref)
-        dkv_ref[out, :] = terms.astype(jnp.bfloat16)
-    dqt = query_terms(same_ref[:, :e], dscore_ref[:rows, :])
-    dqt = dqt + query_terms(other_ref[:, :e], dscore_ref[rows:, :])
-    for i in range(4 * heads):
-        dqt_ref[i * e : (i + 1) * e, :] = dqt[:, i * rows : (i + 1) * rows]
-    mine = lambda ref, i: ref[pl.ds(pl.multiple_of(i * width, width), width), :]
-    keep_own_ref[...] = mine(dqt_ref, core) + mine(dqt_in_ref, core)
-    keep_far_ref[...] = mine(dqt_ref, 2 + core)
-    give_ref[:width, :] = mine(dqt_ref, 3 - core).astype(jnp.bfloat16)
-    given = mine(dqt_ref, 1 - core) + mine(dqt_in_ref, 1 - core)
-    give_ref[width:, :] = given.astype(jnp.bfloat16)
+    half = 2 * heads * rows
+    probs = [prob_ref.at[:rows, half:], prob_ref.at[rows:, :]]
+    dscores = [dscore_ref.at[:rows, half:], dscore_ref.at[rows:, :]]
+    fill(far, [same_ref[...]], [first + core * rows], False, probs[0], dscores[0])
+    fill(own + far, [other_ref[...]], [first + (1 - core) * rows], False, probs[1], dscores[1])
+    same = dkv_in_ref[...] + key_terms(far, pl.ds(0, rows), probs[0], dscores[0])
+    other = key_terms(own + far, pl.ds(0, rows), probs[1], dscores[1])
+    dkv_ref[pl.ds(pl.multiple_of(core * rows, rows), rows), :] = same.astype(jnp.bfloat16)
+    dkv_ref[pl.ds(pl.multiple_of((1 - core) * rows, rows), rows), :] = other.astype(jnp.bfloat16)
+    dqt = query_terms(other_ref[:, :e], dscores[1][...])
+    dqt_far = query_terms(same_ref[:, :e], dscores[0][...])
+    for i in range(2 * heads):
+        block = pl.ds(i * e, e)
+        columns = slice(i * rows, (i + 1) * rows)
+        dqt_ref[block, :] = dqt_in_ref[block, :] + dqt[:, columns]
+        dqt_ref[pl.ds(2 * width + i * e, e), :] = dqt[:, half:][:, columns] + dqt_far[:, columns]
+    mine = lambda i: dqt_ref[pl.ds(pl.multiple_of(i * width, width), width), :]
+    keep_own_ref[...] = mine(core)
+    keep_far_ref[...] = mine(2 + core)
+    give_ref[:width, :] = mine(3 - core).astype(jnp.bfloat16)
+    give_ref[width:, :] = mine(1 - core).astype(jnp.bfloat16)
 
 
 def pair_kernel(keep_ref, both_ref, send_ref):
@@ -215,9 +235,9 @@
     pairs = [[2 * i, 2 * i + 1] for i in range(chips)]
     bf16, f32 = jnp.bfloat16, jnp.float32
 
-    def shift(x, by_even, by_odd):
+    def shift(x, by_even, by_odd, least=0):
         moves = [(i, i + (by_odd if i % 2 else by_even)) for i in range(count)]
-        return lax.ppermute(x, "ctx", [(i, j) for i, j in moves if 0 <= j < count])
+        return lax.ppermute(x, "ctx", [(i, j) for i, j in moves if least <= i and least <= j < count])
 
     def pair_gather(x):
         return lax.all_gather(x, "ctx", axis=0, tiled=True, axis_index_groups=pairs)
@@ -238,7 +258,7 @@
             for x in (queries, grad_out, attn_out, log_norm, key_states, value_states)
         ]
     )
-    pay_far = shift(pay, -4, -4)
+    pay_far = shift(pay, -4, -4, 2)
     kv_same = shift(kv, 2, 4)
     kv_other = shift(kv, 5, 1)
     pay_own = pair_gather(pay)
@@ -251,20 +271,29 @@
         1,
         scratch=[pltpu.VMEM((rows, 2 * heads * rows), bf16)] * 2,
     )(doc_lengths, pay_own, kv)
+    dqt, dkv_same = call(
+        functools.partial(near_kernel, heads, chips),
+        [((2 * width, rows), f32), ((rows, 2 * e), f32)],
+        "near",
+        unit,
+        1,
+        scratch=[pltpu.VMEM((rows, 2 * heads * rows), bf16)] * 2,
+    )(doc_lengths, pay_own, kv_same, dqt)
+    pay_far, kv_other = lax.optimization_barrier((pay_far, kv_other))
     pay_ahead = pair_gather(pay_far)
     dkv, give, keep_far, keep_own = call(
         functools.partial(cross_kernel, heads, chips),
         [((2 * rows, 2 * e), bf16), ((2 * width, rows), bf16), ((width, rows), f32), ((width, rows), f32)],
         "cross",
-        4 * unit,
+        3 * unit,
         1,
         scratch=[pltpu.VMEM((2 * rows, 4 * heads * rows), bf16)] * 2
         + [pltpu.VMEM((4 * width, rows), f32)],
-    )(doc_lengths, pay_own, pay_ahead, kv_same, kv_other, dqt)
+    )(doc_lengths, pay_own, pay_ahead, kv_same, kv_other, dqt, dkv_same)
     dkv_back = shift(dkv, -2, -4)
     both = pair_gather(give)
     (to_query,) = call(pair_kernel, [((width, rows), bf16)], "pair")(keep_far, both)
-    dqt_back = shift(to_query, 4, 4)
+    dqt_back = shift(to_query, 4, 4, 2)
     back = pair_gather(dkv_back)
     grad_query, grad_key, grad_value = call(
         final_kernel, [((rows, width), bf16), ((rows, e), bf16), ((rows, e), bf16)], "final"

time: 43.2 us -> 42.6 us (0.986)
  starting transfers between devices: 18.5 us -> 11.3 us
  waiting for transfers between devices: 5.62 us -> 10.4 us
  Pallas kernels: 6.97 us -> 7.66 us
  blocking collectives: 11.2 us -> 11.8 us
    ppermute x5, starting transfers between devices: 18.5 us -> 11.3 us  [shift(): lax.ppermute(x, 'ctx', [(i, j) for i, j in moves if least <= i and least...]
    ppermute x5, waiting for transfers between devices: 5.62 us -> 10.4 us  [shift(): lax.ppermute(x, 'ctx', [(i, j) for i, j in moves if least <= i and least...]
    pallas_call x5 -> x6, Pallas kernels: 6.97 us -> 7.66 us  [run(): pl.pallas_call(kernel, out_shape=[jax.ShapeDtypeStruct(s, d) for s, d in...]
    all_gather x4, blocking collectives: 11.2 us -> 11.8 us  [pair_gather(): return lax.all_gather(x, 'ctx', axis=0, tiled=True, axis_index_groups=pairs)]
  transfers between devices with their start and end apart: 5 -> 5, of which waited for: 2 -> 1; matrix products, arithmetic and copies ran while one was open for 0% -> 0% of each run, Pallas kernels for 3% -> 7%
where the time goes in v5:
time: 42.6 us; the launch traced here: 42 us
  blocking collectives  11.8 us (28%)
  starting transfers between devices  11.3 us (27%)
  waiting for transfers between devices  10.4 us (24%)
  Pallas kernels  7.66 us (18%)
  between operations  0.74 us (2%)
    all_gather x4, blocking collectives, pair_gather(): return lax.all_gather(x, 'ctx', axis=0, tiled=True, axis_index_groups=pairs)  11.8 us
    ppermute x5, starting transfers between devices, shift(): lax.ppermute(x, 'ctx', [(i, j) for i, j in moves if least <= i and least...  11.3 us
    ppermute x5, waiting for transfers between devices, shift(): lax.ppermute(x, 'ctx', [(i, j) for i, j in moves if least <= i and least...  10.4 us
    pallas_call x6, Pallas kernels, run(): pl.pallas_call(kernel, out_shape=[jax.ShapeDtypeStruct(s, d) for s, d in...  7.66 us
  transfers between devices with their start and end apart: 5, of which 1 were waited for; matrix products, arithmetic and copies ran while one was open for 0% of the time, Pallas kernels for 7%

profile of v5, /device:TPU:1, one launch (start us, length us, event | category | flops | bytes accessed | tf_op | source)
XLA Modules:
  0.0 42.0 jit_solution(4776275944462743292)
XLA Ops:
  0.6 1.2 %prep.1 = (bf16[528,256]{1,0:T(8,128)(2,1)S(1)}, bf16[256,256]{1,0:T(8,128)(2,1)S(1)}) custom-call(bf16[256,256]{1,0:T(8,128)(2,1)} %q_ref.1, bf16[256,256]{1,0:T(8,128)(2,1)} %go_ref.1, bf16[256,256]{1,0:T(8,128)(2,1)} %out_ref.1, f32[2,256]{1,0:T(2,128)} %norm_ref.1, bf16[256,128]{1,0:T(8,128)(2,1)} %k_ref.1, bf16[256,128]{1,0:T(8,128)(2,1)} %v_ref.1), custom_call_target="tpu_custom_call" | custom-call | bytes 526336 | tf_op jit(solution)/shard_map/prep/pallas_call | solution.py:215
  1.8 0.7 %collective-permute-start = (bf16[528,256]{1,0:T(8,128)(2,1)S(1)}, bf16[528,256]{1,0:T(8,128)(2,1)S(1)}, u32[]{:S(2)}, u32[]{:S(2)}) collective-permute-start(bf16[528,256]{1,0:T(8,128)(2,1)S(1)} %get-tuple-element.15), channel_id=1, source_target_pairs={{192,64},{224,96},{256,128},{288,160},{320,192},{352,224},{384,256... | collective-permute-start | bytes 811016 | tf_op jit(solution)/shard_map/ppermute | solution.py:240
  2.5 0.0 copy-start
  2.5 5.7 %collective-permute-start.2 = (bf16[256,256]{1,0:T(8,128)(2,1)S(1)}, bf16[256,256]{1,0:T(8,128)(2,1)S(1)}, u32[]{:S(2)}, u32[]{:S(2)}) collective-permute-start(bf16[256,256]{1,0:T(8,128)(2,1)S(1)} %get-tuple-element.16.kv_ref), channel_id=1, source_target_pairs={{0,64},{32,160},{64,128},{96,224},{128,192},{160,288},{192,256},{2... | collective-permute-start | bytes 393224 | tf_op jit(solution)/shard_map/ppermute | solution.py:240
  8.2 3.0 %collective-permute-start.1 = (bf16[256,256]{1,0:T(8,128)(2,1)S(1)}, bf16[256,256]{1,0:T(8,128)(2,1)S(1)}, u32[]{:S(2)}, u32[]{:S(2)}) collective-permute-start(bf16[256,256]{1,0:T(8,128)(2,1)S(1)} %get-tuple-element.16.kv_ref), channel_id=1, source_target_pairs={{0,160},{32,64},{64,224},{96,128},{128,288},{160,192},{192,352},{2... | collective-permute-start | bytes 393224 | tf_op jit(solution)/shard_map/ppermute | solution.py:240
  11.2 5.3 %all_gather.12.pay_ref.own_ref = bf16[1056,256]{1,0:T(8,128)(2,1)S(1)} all-gather(bf16[528,256]{1,0:T(8,128)(2,1)S(1)} %get-tuple-element.15), channel_id=1, replica_groups={{0,32},{64,96},{128,160},{192,224},{256,288},{320,352},{384,416},{448,4..., dimensions={0}, use_global_device_ids=true | all-gather | bytes 811008 | tf_op jit(solution)/shard_map/all_gather | solution.py:243
  16.5 0.0 copy-done
  16.5 1.4 %own.1 = (f32[512,256]{1,0:T(8,128)S(1)}, f32[256,256]{1,0:T(8,128)S(1)}) custom-call(s32[4]{0:T(128)S(1)} %copy-done, bf16[1056,256]{1,0:T(8,128)(2,1)S(1)} %all_gather.12.pay_ref.own_ref, bf16[256,256]{1,0:T(8,128)(2,1)S(1)} %get-tuple-element.16.kv_ref), custom_call_target="tpu_custom_call" | custom-call | flops 335544320 | bytes 671760 | tf_op jit(solution)/shard_map/own/pallas_call | solution.py:215
  17.9 0.0 collective-permute-done.2.same_ref
  17.9 1.4 %near.1 = (f32[512,256]{1,0:T(8,128)S(1)}, f32[256,256]{1,0:T(8,128)S(1)}) custom-call(s32[4]{0:T(128)S(1)} %copy-done, bf16[1056,256]{1,0:T(8,128)(2,1)S(1)} %all_gather.12.pay_ref.own_ref, bf16[256,256]{1,0:T(8,128)(2,1)S(1)} %collective-permute-done.2.same_ref, f32[512,256]{1,0:T(8,128)S(1)} %get-tuple-element.19.dqt_in_ref), custom_call_target="tpu_custom_call" | custom-call | flops 335544320 | bytes 1196048 | tf_op jit(solution)/shard_map/near/pallas_call | solution.py:215
  19.3 0.0 collective-permute-done.1.other_ref
  19.3 0.0 collective-permute-done
  19.3 2.2 %all_gather.13.far_ref = bf16[1056,256]{1,0:T(8,128)(2,1)S(1)} all-gather(bf16[528,256]{1,0:T(8,128)(2,1)S(1)} %collective-permute-done), channel_id=1, replica_groups={{0,32},{64,96},{128,160},{192,224},{256,288},{320,352},{384,416},{448,4..., dimensions={0}, use_global_device_ids=true | all-gather | bytes 811008 | tf_op jit(solution)/shard_map/all_gather | solution.py:243
  21.5 2.9 %cross.1 = (bf16[512,256]{1,0:T(8,128)(2,1)S(1)}, bf16[512,256]{1,0:T(8,128)(2,1)S(1)}, f32[256,256]{1,0:T(8,128)S(1)}, f32[256,256]{1,0:T(8,128)S(1)}) custom-call(s32[4]{0:T(128)S(1)} %copy-done, bf16[1056,256]{1,0:T(8,128)(2,1)S(1)} %all_gather.12.pay_ref.own_ref, bf16[1056,256]{1,0:T(8,128)(2,1)S(1)} %all_gather.13.far_ref, ...), custom_call_target="tpu_custom_call" | custom-call | flops 1006632960 | bytes 2129936 | tf_op jit(solution)/shard_map/cross/pallas_call | solution.py:215
  24.4 1.3 %collective-permute-start.3 = (bf16[512,256]{1,0:T(8,128)(2,1)S(1)}, bf16[512,256]{1,0:T(8,128)(2,1)S(1)}, u32[]{:S(2)}, u32[]{:S(2)}) collective-permute-start(bf16[512,256]{1,0:T(8,128)(2,1)S(1)} %get-tuple-element.25), channel_id=1, source_target_pairs={{64,0},{128,64},{160,32},{192,128},{224,96},{256,192},{288,160},{3... | collective-permute-start | bytes 786440 | tf_op jit(solution)/shard_map/ppermute | solution.py:240
  25.7 2.2 %all_gather.14.both_ref = bf16[1024,256]{1,0:T(8,128)(2,1)S(1)} all-gather(bf16[512,256]{1,0:T(8,128)(2,1)S(1)} %get-tuple-element.23), channel_id=1, replica_groups={{0,32},{64,96},{128,160},{192,224},{256,288},{320,352},{384,416},{448,4..., dimensions={0}, use_global_device_ids=true | all-gather | bytes 786432 | tf_op jit(solution)/shard_map/all_gather | solution.py:243
  27.9 0.7 %collective-permute-start.4 = (bf16[256,256]{1,0:T(8,128)(2,1)S(1)}, bf16[256,256]{1,0:T(8,128)(2,1)S(1)}, u32[]{:S(2)}, u32[]{:S(2)}) collective-permute-start(bf16[256,256]{1,0:T(8,128)(2,1)S(1)} %pair.1), channel_id=1, source_target_pairs={{64,192},{96,224},{128,256},{160,288},{192,320},{224,352},{256,384... | collective-permute-start | bytes 393224 | tf_op jit(solution)/shard_map/ppermute | solution.py:240
  28.6 10.4 %collective-permute-done.3 = bf16[512,256]{1,0:T(8,128)(2,1)S(1)} collective-permute-done((bf16[512,256]{1,0:T(8,128)(2,1)S(1)}, bf16[512,256]{1,0:T(8,128)(2,1)S(1)}, u32[]{:S(2)}, u32[]{:S(2)}) %collective-permute-start.3) | collective-permute-done | bytes 262176 | tf_op jit(solution)/shard_map/ppermute | solution.py:240
  39.0 2.2 %all_gather.15.back_ref = bf16[1024,256]{1,0:T(8,128)(2,1)S(1)} all-gather(bf16[512,256]{1,0:T(8,128)(2,1)S(1)} %collective-permute-done.3), channel_id=1, replica_groups={{0,32},{64,96},{128,160},{192,224},{256,288},{320,352},{384,416},{448,4..., dimensions={0}, use_global_device_ids=true | all-gather | bytes 786432 | tf_op jit(solution)/shard_map/all_gather | solution.py:243
  41.2 0.0 collective-permute-done.4.dqt_back_ref
  41.2 0.8 %final.1 = (bf16[256,256]{1,0:T(8,128)(2,1)}, bf16[256,128]{1,0:T(8,128)(2,1)}, bf16[256,128]{1,0:T(8,128)(2,1)}) custom-call(f32[256,256]{1,0:T(8,128)S(1)} %get-tuple-element.22.keep_ref, bf16[1024,256]{1,0:T(8,128)(2,1)S(1)} %all_gather.14.both_ref, f32[256,256]{1,0:T(8,128)S(1)} %get-tuple-element.24.dkv_ref, bf16[1024,256]{1,0:T(8,128)(2,1)S(1)} %all_gather.15.back_ref, ...), custom_call_target="tpu_custom_call" | custom-call | bytes 1703936 | tf_op jit(solution)/shard_map/final/pallas_call | solution.py:215
  (1 shorter events, 0.0 us)
Async XLA Ops:
  1.8 17.5 %collective-permute-start = (bf16[528,256]{1,0:T(8,128)(2,1)S(1)}, bf16[528,256]{1,0:T(8,128)(2,1)S(1)}, u32[]{:S(2)}, u32[]{:S(2)}) collective-permute-start(bf16[528,256]{1,0:T(8,128)(2,1)S(1)} %get-tuple-element.15), channel_id=1, source_target_pairs={{192,64},{224,96},{256,128},{288,160},{320,192},{352,224},{384,256... | collective-permute-start | bytes 811016 | tf_op jit(solution)/shard_map/ppermute | solution.py:240
  2.5 14.0 %copy-start = (s32[4]{0:T(128)S(1)}, s32[4]{0:T(128)}, u32[]{:S(2)}) copy-start(s32[4]{0:T(128)} %lens_ref.5) | copy-start | bytes 52
  2.5 15.4 %collective-permute-start.2 = (bf16[256,256]{1,0:T(8,128)(2,1)S(1)}, bf16[256,256]{1,0:T(8,128)(2,1)S(1)}, u32[]{:S(2)}, u32[]{:S(2)}) collective-permute-start(bf16[256,256]{1,0:T(8,128)(2,1)S(1)} %get-tuple-element.16.kv_ref), channel_id=1, source_target_pairs={{0,64},{32,160},{64,128},{96,224},{128,192},{160,288},{192,256},{2... | collective-permute-start | bytes 393224 | tf_op jit(solution)/shard_map/ppermute | solution.py:240
  8.2 11.1 %collective-permute-start.1 = (bf16[256,256]{1,0:T(8,128)(2,1)S(1)}, bf16[256,256]{1,0:T(8,128)(2,1)S(1)}, u32[]{:S(2)}, u32[]{:S(2)}) collective-permute-start(bf16[256,256]{1,0:T(8,128)(2,1)S(1)} %get-tuple-element.16.kv_ref), channel_id=1, source_target_pairs={{0,160},{32,64},{64,224},{96,128},{128,288},{160,192},{192,352},{2... | collective-permute-start | bytes 393224 | tf_op jit(solution)/shard_map/ppermute | solution.py:240
  24.4 14.6 %collective-permute-start.3 = (bf16[512,256]{1,0:T(8,128)(2,1)S(1)}, bf16[512,256]{1,0:T(8,128)(2,1)S(1)}, u32[]{:S(2)}, u32[]{:S(2)}) collective-permute-start(bf16[512,256]{1,0:T(8,128)(2,1)S(1)} %get-tuple-element.25), channel_id=1, source_target_pairs={{64,0},{128,64},{160,32},{192,128},{224,96},{256,192},{288,160},{3... | collective-permute-start | bytes 786440 | tf_op jit(solution)/shard_map/ppermute | solution.py:240
  27.9 13.2 %collective-permute-start.4 = (bf16[256,256]{1,0:T(8,128)(2,1)S(1)}, bf16[256,256]{1,0:T(8,128)(2,1)S(1)}, u32[]{:S(2)}, u32[]{:S(2)}) collective-permute-start(bf16[256,256]{1,0:T(8,128)(2,1)S(1)} %pair.1), channel_id=1, source_target_pairs={{64,192},{96,224},{128,256},{160,288},{192,320},{224,352},{256,384... | collective-permute-start | bytes 393224 | tf_op jit(solution)/shard_map/ppermute | solution.py:240

commit v6 on v5

--- a/solution.py
+++ b/solution.py
@@ -57,11 +57,10 @@
         e = width // heads
         base = block * (2 * rows + STAT_ROWS)
         self.heads, self.rows, self.e = heads, rows, e
-        self.q = [pay_ref[base : base + rows, h * e : (h + 1) * e] for h in range(heads)]
-        self.go = [
-            pay_ref[base + rows : base + 2 * rows, h * e : (h + 1) * e] for h in range(heads)
-        ]
-        table = pay_ref[base + 2 * rows : base + 2 * rows + STAT_ROWS, :rows].astype(jnp.float32)
+        part = lambda at, size: pl.ds(pl.multiple_of(base + at, STAT_ROWS), size)
+        self.q = [pay_ref[part(0, rows), h * e : (h + 1) * e] for h in range(heads)]
+        self.go = [pay_ref[part(rows, rows), h * e : (h + 1) * e] for h in range(heads)]
+        table = pay_ref[part(2 * rows, STAT_ROWS), :rows].astype(jnp.float32)
         row = lambda i: table[i : i + 1]
         self.norm = [row(6 * h) + row(6 * h + 1) + row(6 * h + 2) for h in range(heads)]
         self.delta = [row(6 * h + 3) + row(6 * h + 4) + row(6 * h + 5) for h in range(heads)]
@@ -125,10 +124,16 @@
     return jnp.where(behind >= 0, behind, -2 * chips) * (2 * rows)
 
 
+def both_halves(pay_ref, heads, chip, core, rows, lens_ref):
+    return [
+        Query(pay_ref, half, heads, (2 * chip + half) * rows, lens_ref) for half in (core, 1 - core)
+    ]
+
+
 def own_kernel(heads, lens_ref, pay_ref, kv_ref, dqt_ref, dkv_ref, prob_ref, dscore_ref):
     rows, e = kv_ref.shape[0], kv_ref.shape[1] // 2
     index, chip, core = place()
-    queries = [Query(pay_ref, i, heads, (2 * chip + i) * rows, lens_ref) for i in range(2)]
+    queries = both_halves(pay_ref, heads, chip, core, rows, lens_ref)
     fill(queries, [kv_ref[...]], [index * rows], True, prob_ref, dscore_ref)
     dkv_ref[...] = key_terms(queries, pl.ds(0, rows), prob_ref, dscore_ref)
     dqt = query_terms(kv_ref[:, :e], dscore_ref[...])
@@ -143,7 +148,7 @@
 ):
     rows, e = same_ref.shape[0], same_ref.shape[1] // 2
     index, chip, core = place()
-    own = [Query(own_ref, i, heads, (2 * chip + i) * rows, lens_ref) for i in range(2)]
+    own = both_halves(own_ref, heads, chip, core, rows, lens_ref)
     first = block_start(chip, 1 + core, chips, rows) + core * rows
     fill(own, [same_ref[...]], [first], False, prob_ref, dscore_ref)
     dkv_ref[...] = key_terms(own, pl.ds(0, rows), prob_ref, dscore_ref)
@@ -155,37 +160,40 @@
 
 def cross_kernel(
     heads, chips, lens_ref, own_ref, far_ref, same_ref, other_ref, dqt_in_ref, dkv_in_ref,
-    dkv_ref, give_ref, keep_far_ref, keep_own_ref, prob_ref, dscore_ref, dqt_ref
+    dkv_ref, give_ref, keep_far_ref, keep_own_ref, prob_ref, dscore_ref
 ):
     rows, e = same_ref.shape[0], same_ref.shape[1] // 2
-    width = heads * e
     index, chip, core = place()
-    own = [Query(own_ref, i, heads, (2 * chip + i) * rows, lens_ref) for i in range(2)]
-    far = [Query(far_ref, i, heads, (2 * chip + 4 + i) * rows, lens_ref) for i in range(2)]
+    own = both_halves(own_ref, heads, chip, core, rows, lens_ref)
+    far = both_halves(far_ref, heads, chip + 2, core, rows, lens_ref)
     for query in far:
         query.start = jnp.where(chip + 2 < chips, query.start, 4 * chips * rows)
     first = block_start(chip, 1 + core, chips, rows)
     half = 2 * heads * rows
-    probs = [prob_ref.at[:rows, half:], prob_ref.at[rows:, :]]
-    dscores = [dscore_ref.at[:rows, half:], dscore_ref.at[rows:, :]]
-    fill(far, [same_ref[...]], [first + core * rows], False, probs[0], dscores[0])
-    fill(own + far, [other_ref[...]], [first + (1 - core) * rows], False, probs[1], dscores[1])
-    same = dkv_in_ref[...] + key_terms(far, pl.ds(0, rows), probs[0], dscores[0])
-    other = key_terms(own + far, pl.ds(0, rows), probs[1], dscores[1])
+    far_prob, far_dscore = prob_ref.at[:, half:], dscore_ref.at[:, half:]
+    own_prob, own_dscore = prob_ref.at[rows:, :half], dscore_ref.at[rows:, :half]
+    firsts = [first + core * rows, first + (1 - core) * rows]
+    fill(far, [same_ref[...], other_ref[...]], firsts, False, far_prob, far_dscore)
+    fill(own, [other_ref[...]], firsts[1:], False, own_prob, own_dscore)
+    terms = key_terms(far, pl.ds(0, 2 * rows), far_prob, far_dscore)
+    same = terms[:rows] + dkv_in_ref[...]
+    other = terms[rows:] + key_terms(own, pl.ds(0, rows), own_prob, own_dscore)
     dkv_ref[pl.ds(pl.multiple_of(core * rows, rows), rows), :] = same.astype(jnp.bfloat16)
     dkv_ref[pl.ds(pl.multiple_of((1 - core) * rows, rows), rows), :] = other.astype(jnp.bfloat16)
-    dqt = query_terms(other_ref[:, :e], dscores[1][...])
-    dqt_far = query_terms(same_ref[:, :e], dscores[0][...])
+    keys = jnp.concatenate([same_ref[:, :e], other_ref[:, :e]], axis=0)
+    dqt = query_terms(other_ref[:, :e], own_dscore[...])
+    dqt_far = query_terms(keys, far_dscore[...])
     for i in range(2 * heads):
-        block = pl.ds(i * e, e)
         columns = slice(i * rows, (i + 1) * rows)
-        dqt_ref[block, :] = dqt_in_ref[block, :] + dqt[:, columns]
-        dqt_ref[pl.ds(2 * width + i * e, e), :] = dqt[:, half:][:, columns] + dqt_far[:, columns]
-    mine = lambda i: dqt_ref[pl.ds(pl.multiple_of(i * width, width), width), :]
-    keep_own_ref[...] = mine(core)
-    keep_far_ref[...] = mine(2 + core)
-    give_ref[:width, :] = mine(3 - core).astype(jnp.bfloat16)
-    give_ref[width:, :] = mine(1 - core).astype(jnp.bfloat16)
+        own_part = dqt_in_ref[i * e : (i + 1) * e, :] + dqt[:, columns]
+        far_part = dqt_far[:, columns]
+        if i < heads:
+            block = pl.ds(i * e, e)
+            keep_own_ref[block, :] = own_part
+            keep_far_ref[block, :] = far_part
+        else:
+            give_ref[pl.ds((i - heads) * e, e), :] = far_part.astype(jnp.bfloat16)
+            give_ref[pl.ds(i * e, e), :] = own_part.astype(jnp.bfloat16)
 
 
 def pair_kernel(keep_ref, both_ref, send_ref):
@@ -287,8 +295,7 @@
         "cross",
         3 * unit,
         1,
-        scratch=[pltpu.VMEM((2 * rows, 4 * heads * rows), bf16)] * 2
-        + [pltpu.VMEM((4 * width, rows), f32)],
+        scratch=[pltpu.VMEM((2 * rows, 4 * heads * rows), bf16)] * 2,
     )(doc_lengths, pay_own, pay_ahead, kv_same, kv_other, dqt, dkv_same)
     dkv_back = shift(dkv, -2, -4)
     both = pair_gather(give)

time: 42.6 us -> 42.4 us (level)
  no operation moved by 1% of the time
where the time goes in v6:
time: 42.4 us; the launch traced here: 41.8 us
  blocking collectives  11.8 us (28%)
  starting transfers between devices  11.3 us (27%)
  waiting for transfers between devices  10.4 us (25%)
  Pallas kernels  7.52 us (18%)
  between operations  0.74 us (2%)
    all_gather x4, blocking collectives, pair_gather(): return lax.all_gather(x, 'ctx', axis=0, tiled=True, axis_index_groups=pairs)  11.8 us
    ppermute x5, starting transfers between devices, shift(): lax.ppermute(x, 'ctx', [(i, j) for i, j in moves if least <= i and least...  11.3 us
    ppermute x5, waiting for transfers between devices, shift(): lax.ppermute(x, 'ctx', [(i, j) for i, j in moves if least <= i and least...  10.4 us
    pallas_call x6, Pallas kernels, run(): pl.pallas_call(kernel, out_shape=[jax.ShapeDtypeStruct(s, d) for s, d in...  7.52 us
  transfers between devices with their start and end apart: 5, of which 1 were waited for; matrix products, arithmetic and copies ran while one was open for 0% of the time, Pallas kernels for 7%

profile of v6, /device:TPU:1, one launch (start us, length us, event | category | flops | bytes accessed | tf_op | source)
XLA Modules:
  0.0 41.8 jit_solution(7767125164393218521)
XLA Ops:
  0.6 1.2 %prep.1 = (bf16[528,256]{1,0:T(8,128)(2,1)S(1)}, bf16[256,256]{1,0:T(8,128)(2,1)S(1)}) custom-call(bf16[256,256]{1,0:T(8,128)(2,1)} %q_ref.1, bf16[256,256]{1,0:T(8,128)(2,1)} %go_ref.1, bf16[256,256]{1,0:T(8,128)(2,1)} %out_ref.1, f32[2,256]{1,0:T(2,128)} %norm_ref.1, bf16[256,128]{1,0:T(8,128)(2,1)} %k_ref.1, bf16[256,128]{1,0:T(8,128)(2,1)} %v_ref.1), custom_call_target="tpu_custom_call" | custom-call | bytes 526336 | tf_op jit(solution)/shard_map/prep/pallas_call | solution.py:223
  1.8 0.7 %collective-permute-start = (bf16[528,256]{1,0:T(8,128)(2,1)S(1)}, bf16[528,256]{1,0:T(8,128)(2,1)S(1)}, u32[]{:S(2)}, u32[]{:S(2)}) collective-permute-start(bf16[528,256]{1,0:T(8,128)(2,1)S(1)} %get-tuple-element.15), channel_id=1, source_target_pairs={{192,64},{224,96},{256,128},{288,160},{320,192},{352,224},{384,256... | collective-permute-start | bytes 811016 | tf_op jit(solution)/shard_map/ppermute | solution.py:248
  2.5 0.0 copy-start
  2.5 5.7 %collective-permute-start.2 = (bf16[256,256]{1,0:T(8,128)(2,1)S(1)}, bf16[256,256]{1,0:T(8,128)(2,1)S(1)}, u32[]{:S(2)}, u32[]{:S(2)}) collective-permute-start(bf16[256,256]{1,0:T(8,128)(2,1)S(1)} %get-tuple-element.16.kv_ref), channel_id=1, source_target_pairs={{0,64},{32,160},{64,128},{96,224},{128,192},{160,288},{192,256},{2... | collective-permute-start | bytes 393224 | tf_op jit(solution)/shard_map/ppermute | solution.py:248
  8.2 3.0 %collective-permute-start.1 = (bf16[256,256]{1,0:T(8,128)(2,1)S(1)}, bf16[256,256]{1,0:T(8,128)(2,1)S(1)}, u32[]{:S(2)}, u32[]{:S(2)}) collective-permute-start(bf16[256,256]{1,0:T(8,128)(2,1)S(1)} %get-tuple-element.16.kv_ref), channel_id=1, source_target_pairs={{0,160},{32,64},{64,224},{96,128},{128,288},{160,192},{192,352},{2... | collective-permute-start | bytes 393224 | tf_op jit(solution)/shard_map/ppermute | solution.py:248
  11.2 5.3 %all_gather.12.pay_ref.own_ref = bf16[1056,256]{1,0:T(8,128)(2,1)S(1)} all-gather(bf16[528,256]{1,0:T(8,128)(2,1)S(1)} %get-tuple-element.15), channel_id=1, replica_groups={{0,32},{64,96},{128,160},{192,224},{256,288},{320,352},{384,416},{448,4..., dimensions={0}, use_global_device_ids=true | all-gather | bytes 811008 | tf_op jit(solution)/shard_map/all_gather | solution.py:251
  16.5 0.0 copy-done
  16.5 1.4 %own.1 = (f32[512,256]{1,0:T(8,128)S(1)}, f32[256,256]{1,0:T(8,128)S(1)}) custom-call(s32[4]{0:T(128)S(1)} %copy-done, bf16[1056,256]{1,0:T(8,128)(2,1)S(1)} %all_gather.12.pay_ref.own_ref, bf16[256,256]{1,0:T(8,128)(2,1)S(1)} %get-tuple-element.16.kv_ref), custom_call_target="tpu_custom_call" | custom-call | flops 335544320 | bytes 671760 | tf_op jit(solution)/shard_map/own/pallas_call | solution.py:223
  18.0 0.0 collective-permute-done.2.same_ref
  18.0 1.4 %near.1 = (f32[512,256]{1,0:T(8,128)S(1)}, f32[256,256]{1,0:T(8,128)S(1)}) custom-call(s32[4]{0:T(128)S(1)} %copy-done, bf16[1056,256]{1,0:T(8,128)(2,1)S(1)} %all_gather.12.pay_ref.own_ref, bf16[256,256]{1,0:T(8,128)(2,1)S(1)} %collective-permute-done.2.same_ref, f32[512,256]{1,0:T(8,128)S(1)} %get-tuple-element.19.dqt_in_ref), custom_call_target="tpu_custom_call" | custom-call | flops 335544320 | bytes 1196048 | tf_op jit(solution)/shard_map/near/pallas_call | solution.py:223
  19.3 0.0 collective-permute-done.1.other_ref
  19.3 0.0 collective-permute-done
  19.4 2.2 %all_gather.13.far_ref = bf16[1056,256]{1,0:T(8,128)(2,1)S(1)} all-gather(bf16[528,256]{1,0:T(8,128)(2,1)S(1)} %collective-permute-done), channel_id=1, replica_groups={{0,32},{64,96},{128,160},{192,224},{256,288},{320,352},{384,416},{448,4..., dimensions={0}, use_global_device_ids=true | all-gather | bytes 811008 | tf_op jit(solution)/shard_map/all_gather | solution.py:251
  21.6 2.7 %cross.1 = (bf16[512,256]{1,0:T(8,128)(2,1)S(1)}, bf16[512,256]{1,0:T(8,128)(2,1)S(1)}, f32[256,256]{1,0:T(8,128)S(1)}, f32[256,256]{1,0:T(8,128)S(1)}) custom-call(s32[4]{0:T(128)S(1)} %copy-done, bf16[1056,256]{1,0:T(8,128)(2,1)S(1)} %all_gather.12.pay_ref.own_ref, bf16[1056,256]{1,0:T(8,128)(2,1)S(1)} %all_gather.13.far_ref, ...), custom_call_target="tpu_custom_call" | custom-call | flops 1006632960 | bytes 2129936 | tf_op jit(solution)/shard_map/cross/pallas_call | solution.py:223
  24.3 1.3 %collective-permute-start.3 = (bf16[512,256]{1,0:T(8,128)(2,1)S(1)}, bf16[512,256]{1,0:T(8,128)(2,1)S(1)}, u32[]{:S(2)}, u32[]{:S(2)}) collective-permute-start(bf16[512,256]{1,0:T(8,128)(2,1)S(1)} %get-tuple-element.25), channel_id=1, source_target_pairs={{64,0},{128,64},{160,32},{192,128},{224,96},{256,192},{288,160},{3... | collective-permute-start | bytes 786440 | tf_op jit(solution)/shard_map/ppermute | solution.py:248
  25.6 2.2 %all_gather.14.both_ref = bf16[1024,256]{1,0:T(8,128)(2,1)S(1)} all-gather(bf16[512,256]{1,0:T(8,128)(2,1)S(1)} %get-tuple-element.23), channel_id=1, replica_groups={{0,32},{64,96},{128,160},{192,224},{256,288},{320,352},{384,416},{448,4..., dimensions={0}, use_global_device_ids=true | all-gather | bytes 786432 | tf_op jit(solution)/shard_map/all_gather | solution.py:251
  27.8 0.7 %collective-permute-start.4 = (bf16[256,256]{1,0:T(8,128)(2,1)S(1)}, bf16[256,256]{1,0:T(8,128)(2,1)S(1)}, u32[]{:S(2)}, u32[]{:S(2)}) collective-permute-start(bf16[256,256]{1,0:T(8,128)(2,1)S(1)} %pair.1), channel_id=1, source_target_pairs={{64,192},{96,224},{128,256},{160,288},{192,320},{224,352},{256,384... | collective-permute-start | bytes 393224 | tf_op jit(solution)/shard_map/ppermute | solution.py:248
  28.5 10.4 %collective-permute-done.3 = bf16[512,256]{1,0:T(8,128)(2,1)S(1)} collective-permute-done((bf16[512,256]{1,0:T(8,128)(2,1)S(1)}, bf16[512,256]{1,0:T(8,128)(2,1)S(1)}, u32[]{:S(2)}, u32[]{:S(2)}) %collective-permute-start.3) | collective-permute-done | bytes 262176 | tf_op jit(solution)/shard_map/ppermute | solution.py:248
  38.9 2.2 %all_gather.15.back_ref = bf16[1024,256]{1,0:T(8,128)(2,1)S(1)} all-gather(bf16[512,256]{1,0:T(8,128)(2,1)S(1)} %collective-permute-done.3), channel_id=1, replica_groups={{0,32},{64,96},{128,160},{192,224},{256,288},{320,352},{384,416},{448,4..., dimensions={0}, use_global_device_ids=true | all-gather | bytes 786432 | tf_op jit(solution)/shard_map/all_gather | solution.py:251
  41.0 0.0 collective-permute-done.4.dqt_back_ref
  41.0 0.8 %final.1 = (bf16[256,256]{1,0:T(8,128)(2,1)}, bf16[256,128]{1,0:T(8,128)(2,1)}, bf16[256,128]{1,0:T(8,128)(2,1)}) custom-call(f32[256,256]{1,0:T(8,128)S(1)} %get-tuple-element.22.keep_ref, bf16[1024,256]{1,0:T(8,128)(2,1)S(1)} %all_gather.14.both_ref, f32[256,256]{1,0:T(8,128)S(1)} %get-tuple-element.24.dkv_ref, bf16[1024,256]{1,0:T(8,128)(2,1)S(1)} %all_gather.15.back_ref, ...), custom_call_target="tpu_custom_call" | custom-call | bytes 1703936 | tf_op jit(solution)/shard_map/final/pallas_call | solution.py:223
  (1 shorter events, 0.0 us)
Async XLA Ops:
  1.8 17.5 %collective-permute-start = (bf16[528,256]{1,0:T(8,128)(2,1)S(1)}, bf16[528,256]{1,0:T(8,128)(2,1)S(1)}, u32[]{:S(2)}, u32[]{:S(2)}) collective-permute-start(bf16[528,256]{1,0:T(8,128)(2,1)S(1)} %get-tuple-element.15), channel_id=1, source_target_pairs={{192,64},{224,96},{256,128},{288,160},{320,192},{352,224},{384,256... | collective-permute-start | bytes 811016 | tf_op jit(solution)/shard_map/ppermute | solution.py:248
  2.5 14.0 %copy-start = (s32[4]{0:T(128)S(1)}, s32[4]{0:T(128)}, u32[]{:S(2)}) copy-start(s32[4]{0:T(128)} %lens_ref.5) | copy-start | bytes 52
  2.5 15.4 %collective-permute-start.2 = (bf16[256,256]{1,0:T(8,128)(2,1)S(1)}, bf16[256,256]{1,0:T(8,128)(2,1)S(1)}, u32[]{:S(2)}, u32[]{:S(2)}) collective-permute-start(bf16[256,256]{1,0:T(8,128)(2,1)S(1)} %get-tuple-element.16.kv_ref), channel_id=1, source_target_pairs={{0,64},{32,160},{64,128},{96,224},{128,192},{160,288},{192,256},{2... | collective-permute-start | bytes 393224 | tf_op jit(solution)/shard_map/ppermute | solution.py:248
  8.2 11.1 %collective-permute-start.1 = (bf16[256,256]{1,0:T(8,128)(2,1)S(1)}, bf16[256,256]{1,0:T(8,128)(2,1)S(1)}, u32[]{:S(2)}, u32[]{:S(2)}) collective-permute-start(bf16[256,256]{1,0:T(8,128)(2,1)S(1)} %get-tuple-element.16.kv_ref), channel_id=1, source_target_pairs={{0,160},{32,64},{64,224},{96,128},{128,288},{160,192},{192,352},{2... | collective-permute-start | bytes 393224 | tf_op jit(solution)/shard_map/ppermute | solution.py:248
  24.3 14.6 %collective-permute-start.3 = (bf16[512,256]{1,0:T(8,128)(2,1)S(1)}, bf16[512,256]{1,0:T(8,128)(2,1)S(1)}, u32[]{:S(2)}, u32[]{:S(2)}) collective-permute-start(bf16[512,256]{1,0:T(8,128)(2,1)S(1)} %get-tuple-element.25), channel_id=1, source_target_pairs={{64,0},{128,64},{160,32},{192,128},{224,96},{256,192},{288,160},{3... | collective-permute-start | bytes 786440 | tf_op jit(solution)/shard_map/ppermute | solution.py:248
  27.8 13.2 %collective-permute-start.4 = (bf16[256,256]{1,0:T(8,128)(2,1)S(1)}, bf16[256,256]{1,0:T(8,128)(2,1)S(1)}, u32[]{:S(2)}, u32[]{:S(2)}) collective-permute-start(bf16[256,256]{1,0:T(8,128)(2,1)S(1)} %pair.1), channel_id=1, source_target_pairs={{64,192},{96,224},{128,256},{160,288},{192,320},{224,352},{256,384... | collective-permute-start | bytes 393224 | tf_op jit(solution)/shard_map/ppermute | solution.py:248

commit v7 on v6

--- a/solution.py
+++ b/solution.py
@@ -119,9 +119,17 @@
     return index, index // 2, lax.rem(index, 2)
 
 
+def near_core(chip):
+    return (chip + 1) % 2
+
+
+def behind(chip, core):
+    return jnp.where(core == near_core(chip), 1, 2)
+
+
 def block_start(chip, back, chips, rows):
-    behind = chip - back
-    return jnp.where(behind >= 0, behind, -2 * chips) * (2 * rows)
+    there = chip - back
+    return jnp.where(there >= 0, there, -2 * chips) * (2 * rows)
 
 
 def both_halves(pay_ref, heads, chip, core, rows, lens_ref):
@@ -149,7 +157,8 @@
     rows, e = same_ref.shape[0], same_ref.shape[1] // 2
     index, chip, core = place()
     own = both_halves(own_ref, heads, chip, core, rows, lens_ref)
-    first = block_start(chip, 1 + core, chips, rows) + core * rows
+    back = behind(chip, core)
+    first = block_start(chip, back, chips, rows) + (back - 1) * rows
     fill(own, [same_ref[...]], [first], False, prob_ref, dscore_ref)
     dkv_ref[...] = key_terms(own, pl.ds(0, rows), prob_ref, dscore_ref)
     dqt = query_terms(same_ref[:, :e], dscore_ref[...])
@@ -168,18 +177,19 @@
     far = both_halves(far_ref, heads, chip + 2, core, rows, lens_ref)
     for query in far:
         query.start = jnp.where(chip + 2 < chips, query.start, 4 * chips * rows)
-    first = block_start(chip, 1 + core, chips, rows)
+    back = behind(chip, core)
+    first = block_start(chip, back, chips, rows)
     half = 2 * heads * rows
     far_prob, far_dscore = prob_ref.at[:, half:], dscore_ref.at[:, half:]
     own_prob, own_dscore = prob_ref.at[rows:, :half], dscore_ref.at[rows:, :half]
-    firsts = [first + core * rows, first + (1 - core) * rows]
+    firsts = [first + (back - 1) * rows, first + (2 - back) * rows]
     fill(far, [same_ref[...], other_ref[...]], firsts, False, far_prob, far_dscore)
     fill(own, [other_ref[...]], firsts[1:], False, own_prob, own_dscore)
     terms = key_terms(far, pl.ds(0, 2 * rows), far_prob, far_dscore)
     same = terms[:rows] + dkv_in_ref[...]
     other = terms[rows:] + key_terms(own, pl.ds(0, rows), own_prob, own_dscore)
-    dkv_ref[pl.ds(pl.multiple_of(core * rows, rows), rows), :] = same.astype(jnp.bfloat16)
-    dkv_ref[pl.ds(pl.multiple_of((1 - core) * rows, rows), rows), :] = other.astype(jnp.bfloat16)
+    dkv_ref[pl.ds(pl.multiple_of((back - 1) * rows, rows), rows), :] = same.astype(jnp.bfloat16)
+    dkv_ref[pl.ds(pl.multiple_of((2 - back) * rows, rows), rows), :] = other.astype(jnp.bfloat16)
     keys = jnp.concatenate([same_ref[:, :e], other_ref[:, :e]], axis=0)
     dqt = query_terms(other_ref[:, :e], own_dscore[...])
     dqt_far = query_terms(keys, far_dscore[...])
@@ -242,6 +252,17 @@
     chips = count // 2
     pairs = [[2 * i, 2 * i + 1] for i in range(chips)]
     bf16, f32 = jnp.bfloat16, jnp.float32
+
+    def send(x, target):
+        moves = [(i, target(i // 2, i % 2)) for i in range(count)]
+        moves = [(i, 2 * chip + core) for i, (chip, core) in moves if 0 <= chip < chips]
+        return lax.ppermute(x, "ctx", moves)
+
+    def near(m):
+        return (m + 1, near_core(m + 1))
+
+    def far(m):
+        return (m + 2, 1 - near_core(m + 2))
 
     def shift(x, by_even, by_odd, least=0):
         moves = [(i, i + (by_odd if i % 2 else by_even)) for i in range(count)]
@@ -267,8 +288,8 @@
         ]
     )
     pay_far = shift(pay, -4, -4, 2)
-    kv_same = shift(kv, 2, 4)
-    kv_other = shift(kv, 5, 1)
+    kv_same = send(kv, lambda m, c: near(m) if c == 0 else far(m))
+    kv_other = send(kv, lambda m, c: far(m) if c == 0 else near(m))
     pay_own = pair_gather(pay)
     unit = 5 * 2 * heads * rows * 2 * rows * e
     dqt, dkv_own = call(
@@ -297,7 +318,10 @@
         1,
         scratch=[pltpu.VMEM((2 * rows, 4 * heads * rows), bf16)] * 2,
     )(doc_lengths, pay_own, pay_ahead, kv_same, kv_other, dqt, dkv_same)
-    dkv_back = shift(dkv, -2, -4)
+    dkv_back = send(
+        dkv,
+        lambda m, c: (m - 1, near_core(m - 1)) if c == near_core(m) else (m - 2, 1 - near_core(m - 2)),
+    )
     both = pair_gather(give)
     (to_query,) = call(pair_kernel, [((width, rows), bf16)], "pair")(keep_far, both)
     dqt_back = shift(to_query, 4, 4, 2)

time: 42.4 us -> 42.5 us (level)
  blocking collectives: 11.8 us -> 18.4 us
  waiting for transfers between devices: 10.4 us -> 4.73 us
  starting transfers between devices: 11.3 us -> 10.8 us
    ppermute x5 -> x2, waiting for transfers between devices: 10.4 us -> 0.01 us  [shift(): lax.ppermute(x, 'ctx', [(i, j) for i, j in moves if least <= i and least...]
    ppermute x5 -> x2, starting transfers between devices: 11.3 us -> 1.35 us  [shift(): lax.ppermute(x, 'ctx', [(i, j) for i, j in moves if least <= i and least...]
    ppermute x0 -> x3, starting transfers between devices: none -> 9.43 us  [send(): return lax.ppermute(x, 'ctx', moves)]
    all_gather x4, blocking collectives: 11.8 us -> 18.4 us  [pair_gather(): return lax.all_gather(x, 'ctx', axis=0, tiled=True, axis_index_groups=pairs)]
    ppermute x0 -> x3, waiting for transfers between devices: none -> 4.73 us  [send(): return lax.ppermute(x, 'ctx', moves)]
where the time goes in v7:
time: 42.5 us; the launch traced here: 42.2 us
  blocking collectives  18.4 us (43%)
  starting transfers between devices  10.8 us (25%)
  Pallas kernels  7.52 us (18%)
  waiting for transfers between devices  4.73 us (11%)
  between operations  0.74 us (2%)
    all_gather x4, blocking collectives, pair_gather(): return lax.all_gather(x, 'ctx', axis=0, tiled=True, axis_index_groups=pairs)  18.4 us
    ppermute x3, starting transfers between devices, send(): return lax.ppermute(x, 'ctx', moves)  9.43 us
    pallas_call x6, Pallas kernels, run(): pl.pallas_call(kernel, out_shape=[jax.ShapeDtypeStruct(s, d) for s, d in...  7.52 us
    ppermute x3, waiting for transfers between devices, send(): return lax.ppermute(x, 'ctx', moves)  4.73 us
    ppermute x2, starting transfers between devices, shift(): lax.ppermute(x, 'ctx', [(i, j) for i, j in moves if least <= i and least...  1.35 us
  transfers between devices with their start and end apart: 5, of which 1 were waited for; matrix products, arithmetic and copies ran while one was open for 0% of the time, Pallas kernels for 7%

profile of v7, /device:TPU:1, one launch (start us, length us, event | category | flops | bytes accessed | tf_op | source)
XLA Modules:
  0.0 42.2 jit_solution(7294847593562386167)
XLA Ops:
  0.6 1.2 %prep.1 = (bf16[528,256]{1,0:T(8,128)(2,1)S(1)}, bf16[256,256]{1,0:T(8,128)(2,1)S(1)}) custom-call(bf16[256,256]{1,0:T(8,128)(2,1)} %q_ref.1, bf16[256,256]{1,0:T(8,128)(2,1)} %go_ref.1, bf16[256,256]{1,0:T(8,128)(2,1)} %out_ref.1, f32[2,256]{1,0:T(2,128)} %norm_ref.1, bf16[256,128]{1,0:T(8,128)(2,1)} %k_ref.1, bf16[256,128]{1,0:T(8,128)(2,1)} %v_ref.1), custom_call_target="tpu_custom_call" | custom-call | bytes 526336 | tf_op jit(solution)/shard_map/prep/pallas_call | solution.py:233
  1.8 0.7 %collective-permute-start = (bf16[528,256]{1,0:T(8,128)(2,1)S(1)}, bf16[528,256]{1,0:T(8,128)(2,1)S(1)}, u32[]{:S(2)}, u32[]{:S(2)}) collective-permute-start(bf16[528,256]{1,0:T(8,128)(2,1)S(1)} %get-tuple-element.15), channel_id=1, source_target_pairs={{192,64},{224,96},{256,128},{288,160},{320,192},{352,224},{384,256... | collective-permute-start | bytes 811016 | tf_op jit(solution)/shard_map/ppermute | solution.py:269
  2.5 0.0 copy-start
  2.5 6.2 %collective-permute-start.2 = (bf16[256,256]{1,0:T(8,128)(2,1)S(1)}, bf16[256,256]{1,0:T(8,128)(2,1)S(1)}, u32[]{:S(2)}, u32[]{:S(2)}) collective-permute-start(bf16[256,256]{1,0:T(8,128)(2,1)S(1)} %get-tuple-element.16.kv_ref), channel_id=1, source_target_pairs={{0,64},{32,128},{64,160},{96,224},{128,192},{160,256},{192,288},{2... | collective-permute-start | bytes 393224 | tf_op jit(solution)/shard_map/ppermute | solution.py:259
  8.8 1.9 %collective-permute-start.1 = (bf16[256,256]{1,0:T(8,128)(2,1)S(1)}, bf16[256,256]{1,0:T(8,128)(2,1)S(1)}, u32[]{:S(2)}, u32[]{:S(2)}) collective-permute-start(bf16[256,256]{1,0:T(8,128)(2,1)S(1)} %get-tuple-element.16.kv_ref), channel_id=1, source_target_pairs={{0,128},{32,64},{64,224},{96,160},{128,256},{160,192},{192,352},{2... | collective-permute-start | bytes 393224 | tf_op jit(solution)/shard_map/ppermute | solution.py:259
  10.7 4.7 %all_gather.12.pay_ref.own_ref = bf16[1056,256]{1,0:T(8,128)(2,1)S(1)} all-gather(bf16[528,256]{1,0:T(8,128)(2,1)S(1)} %get-tuple-element.15), channel_id=1, replica_groups={{0,32},{64,96},{128,160},{192,224},{256,288},{320,352},{384,416},{448,4..., dimensions={0}, use_global_device_ids=true | all-gather | bytes 811008 | tf_op jit(solution)/shard_map/all_gather | solution.py:272
  15.4 0.0 copy-done
  15.4 1.4 %own.1 = (f32[512,256]{1,0:T(8,128)S(1)}, f32[256,256]{1,0:T(8,128)S(1)}) custom-call(s32[4]{0:T(128)S(1)} %copy-done, bf16[1056,256]{1,0:T(8,128)(2,1)S(1)} %all_gather.12.pay_ref.own_ref, bf16[256,256]{1,0:T(8,128)(2,1)S(1)} %get-tuple-element.16.kv_ref), custom_call_target="tpu_custom_call" | custom-call | flops 335544320 | bytes 671760 | tf_op jit(solution)/shard_map/own/pallas_call | solution.py:233
  16.8 0.0 collective-permute-done.2.same_ref
  16.9 1.4 %near.1 = (f32[512,256]{1,0:T(8,128)S(1)}, f32[256,256]{1,0:T(8,128)S(1)}) custom-call(s32[4]{0:T(128)S(1)} %copy-done, bf16[1056,256]{1,0:T(8,128)(2,1)S(1)} %all_gather.12.pay_ref.own_ref, bf16[256,256]{1,0:T(8,128)(2,1)S(1)} %collective-permute-done.2.same_ref, f32[512,256]{1,0:T(8,128)S(1)} %get-tuple-element.19.dqt_in_ref), custom_call_target="tpu_custom_call" | custom-call | flops 335544320 | bytes 1196048 | tf_op jit(solution)/shard_map/near/pallas_call | solution.py:233
  18.2 0.0 collective-permute-done.1.other_ref
  18.2 0.0 collective-permute-done
  18.3 2.2 %all_gather.13.far_ref = bf16[1056,256]{1,0:T(8,128)(2,1)S(1)} all-gather(bf16[528,256]{1,0:T(8,128)(2,1)S(1)} %collective-permute-done), channel_id=1, replica_groups={{0,32},{64,96},{128,160},{192,224},{256,288},{320,352},{384,416},{448,4..., dimensions={0}, use_global_device_ids=true | all-gather | bytes 811008 | tf_op jit(solution)/shard_map/all_gather | solution.py:272
  20.5 2.7 %cross.1 = (bf16[512,256]{1,0:T(8,128)(2,1)S(1)}, bf16[512,256]{1,0:T(8,128)(2,1)S(1)}, f32[256,256]{1,0:T(8,128)S(1)}, f32[256,256]{1,0:T(8,128)S(1)}) custom-call(s32[4]{0:T(128)S(1)} %copy-done, bf16[1056,256]{1,0:T(8,128)(2,1)S(1)} %all_gather.12.pay_ref.own_ref, bf16[1056,256]{1,0:T(8,128)(2,1)S(1)} %all_gather.13.far_ref, ...), custom_call_target="tpu_custom_call" | custom-call | flops 1006632960 | bytes 2129936 | tf_op jit(solution)/shard_map/cross/pallas_call | solution.py:233
  23.2 1.3 %collective-permute-start.3 = (bf16[512,256]{1,0:T(8,128)(2,1)S(1)}, bf16[512,256]{1,0:T(8,128)(2,1)S(1)}, u32[]{:S(2)}, u32[]{:S(2)}) collective-permute-start(bf16[512,256]{1,0:T(8,128)(2,1)S(1)} %get-tuple-element.25), channel_id=1, source_target_pairs={{64,32},{128,0},{160,64},{192,160},{224,96},{256,128},{288,192},{3... | collective-permute-start | bytes 786440 | tf_op jit(solution)/shard_map/ppermute | solution.py:259
  24.5 2.2 %all_gather.14.both_ref = bf16[1024,256]{1,0:T(8,128)(2,1)S(1)} all-gather(bf16[512,256]{1,0:T(8,128)(2,1)S(1)} %get-tuple-element.23), channel_id=1, replica_groups={{0,32},{64,96},{128,160},{192,224},{256,288},{320,352},{384,416},{448,4..., dimensions={0}, use_global_device_ids=true | all-gather | bytes 786432 | tf_op jit(solution)/shard_map/all_gather | solution.py:272
  26.7 0.7 %collective-permute-start.4 = (bf16[256,256]{1,0:T(8,128)(2,1)S(1)}, bf16[256,256]{1,0:T(8,128)(2,1)S(1)}, u32[]{:S(2)}, u32[]{:S(2)}) collective-permute-start(bf16[256,256]{1,0:T(8,128)(2,1)S(1)} %pair.1), channel_id=1, source_target_pairs={{64,192},{96,224},{128,256},{160,288},{192,320},{224,352},{256,384... | collective-permute-start | bytes 393224 | tf_op jit(solution)/shard_map/ppermute | solution.py:269
  27.4 4.7 %collective-permute-done.3 = bf16[512,256]{1,0:T(8,128)(2,1)S(1)} collective-permute-done((bf16[512,256]{1,0:T(8,128)(2,1)S(1)}, bf16[512,256]{1,0:T(8,128)(2,1)S(1)}, u32[]{:S(2)}, u32[]{:S(2)}) %collective-permute-start.3) | collective-permute-done | bytes 262176 | tf_op jit(solution)/shard_map/ppermute | solution.py:259
  32.1 9.3 %all_gather.15.back_ref = bf16[1024,256]{1,0:T(8,128)(2,1)S(1)} all-gather(bf16[512,256]{1,0:T(8,128)(2,1)S(1)} %collective-permute-done.3), channel_id=1, replica_groups={{0,32},{64,96},{128,160},{192,224},{256,288},{320,352},{384,416},{448,4..., dimensions={0}, use_global_device_ids=true | all-gather | bytes 786432 | tf_op jit(solution)/shard_map/all_gather | solution.py:272
  41.4 0.0 collective-permute-done.4.dqt_back_ref
  41.4 0.8 %final.1 = (bf16[256,256]{1,0:T(8,128)(2,1)}, bf16[256,128]{1,0:T(8,128)(2,1)}, bf16[256,128]{1,0:T(8,128)(2,1)}) custom-call(f32[256,256]{1,0:T(8,128)S(1)} %get-tuple-element.22.keep_ref, bf16[1024,256]{1,0:T(8,128)(2,1)S(1)} %all_gather.14.both_ref, f32[256,256]{1,0:T(8,128)S(1)} %get-tuple-element.24.dkv_ref, bf16[1024,256]{1,0:T(8,128)(2,1)S(1)} %all_gather.15.back_ref, ...), custom_call_target="tpu_custom_call" | custom-call | bytes 1703936 | tf_op jit(solution)/shard_map/final/pallas_call | solution.py:233
  (1 shorter events, 0.0 us)
Async XLA Ops:
  1.8 16.4 %collective-permute-start = (bf16[528,256]{1,0:T(8,128)(2,1)S(1)}, bf16[528,256]{1,0:T(8,128)(2,1)S(1)}, u32[]{:S(2)}, u32[]{:S(2)}) collective-permute-start(bf16[528,256]{1,0:T(8,128)(2,1)S(1)} %get-tuple-element.15), channel_id=1, source_target_pairs={{192,64},{224,96},{256,128},{288,160},{320,192},{352,224},{384,256... | collective-permute-start | bytes 811016 | tf_op jit(solution)/shard_map/ppermute | solution.py:269
  2.5 12.9 %copy-start = (s32[4]{0:T(128)S(1)}, s32[4]{0:T(128)}, u32[]{:S(2)}) copy-start(s32[4]{0:T(128)} %lens_ref.5) | copy-start | bytes 52
  2.5 14.3 %collective-permute-start.2 = (bf16[256,256]{1,0:T(8,128)(2,1)S(1)}, bf16[256,256]{1,0:T(8,128)(2,1)S(1)}, u32[]{:S(2)}, u32[]{:S(2)}) collective-permute-start(bf16[256,256]{1,0:T(8,128)(2,1)S(1)} %get-tuple-element.16.kv_ref), channel_id=1, source_target_pairs={{0,64},{32,128},{64,160},{96,224},{128,192},{160,256},{192,288},{2... | collective-permute-start | bytes 393224 | tf_op jit(solution)/shard_map/ppermute | solution.py:259
  8.8 9.5 %collective-permute-start.1 = (bf16[256,256]{1,0:T(8,128)(2,1)S(1)}, bf16[256,256]{1,0:T(8,128)(2,1)S(1)}, u32[]{:S(2)}, u32[]{:S(2)}) collective-permute-start(bf16[256,256]{1,0:T(8,128)(2,1)S(1)} %get-tuple-element.16.kv_ref), channel_id=1, source_target_pairs={{0,128},{32,64},{64,224},{96,160},{128,256},{160,192},{192,352},{2... | collective-permute-start | bytes 393224 | tf_op jit(solution)/shard_map/ppermute | solution.py:259
  23.2 8.9 %collective-permute-start.3 = (bf16[512,256]{1,0:T(8,128)(2,1)S(1)}, bf16[512,256]{1,0:T(8,128)(2,1)S(1)}, u32[]{:S(2)}, u32[]{:S(2)}) collective-permute-start(bf16[512,256]{1,0:T(8,128)(2,1)S(1)} %get-tuple-element.25), channel_id=1, source_target_pairs={{64,32},{128,0},{160,64},{192,160},{224,96},{256,128},{288,192},{3... | collective-permute-start | bytes 786440 | tf_op jit(solution)/shard_map/ppermute | solution.py:259
  26.7 14.7 %collective-permute-start.4 = (bf16[256,256]{1,0:T(8,128)(2,1)S(1)}, bf16[256,256]{1,0:T(8,128)(2,1)S(1)}, u32[]{:S(2)}, u32[]{:S(2)}) collective-permute-start(bf16[256,256]{1,0:T(8,128)(2,1)S(1)} %pair.1), channel_id=1, source_target_pairs={{64,192},{96,224},{128,256},{160,288},{192,320},{224,352},{256,384... | collective-permute-start | bytes 393224 | tf_op jit(solution)/shard_map/ppermute | solution.py:269

commit v8 on v7

--- a/solution.py
+++ b/solution.py
@@ -158,7 +158,7 @@
     index, chip, core = place()
     own = both_halves(own_ref, heads, chip, core, rows, lens_ref)
     back = behind(chip, core)
-    first = block_start(chip, back, chips, rows) + (back - 1) * rows
+    first = block_start(chip, back, chips, rows) + (2 - back) * rows
     fill(own, [same_ref[...]], [first], False, prob_ref, dscore_ref)
     dkv_ref[...] = key_terms(own, pl.ds(0, rows), prob_ref, dscore_ref)
     dqt = query_terms(same_ref[:, :e], dscore_ref[...])
@@ -182,14 +182,14 @@
     half = 2 * heads * rows
     far_prob, far_dscore = prob_ref.at[:, half:], dscore_ref.at[:, half:]
     own_prob, own_dscore = prob_ref.at[rows:, :half], dscore_ref.at[rows:, :half]
-    firsts = [first + (back - 1) * rows, first + (2 - back) * rows]
+    firsts = [first + (2 - back) * rows, first + (back - 1) * rows]
     fill(far, [same_ref[...], other_ref[...]], firsts, False, far_prob, far_dscore)
     fill(own, [other_ref[...]], firsts[1:], False, own_prob, own_dscore)
     terms = key_terms(far, pl.ds(0, 2 * rows), far_prob, far_dscore)
     same = terms[:rows] + dkv_in_ref[...]
     other = terms[rows:] + key_terms(own, pl.ds(0, rows), own_prob, own_dscore)
-    dkv_ref[pl.ds(pl.multiple_of((back - 1) * rows, rows), rows), :] = same.astype(jnp.bfloat16)
-    dkv_ref[pl.ds(pl.multiple_of((2 - back) * rows, rows), rows), :] = other.astype(jnp.bfloat16)
+    dkv_ref[pl.ds(pl.multiple_of((2 - back) * rows, rows), rows), :] = same.astype(jnp.bfloat16)
+    dkv_ref[pl.ds(pl.multiple_of((back - 1) * rows, rows), rows), :] = other.astype(jnp.bfloat16)
     keys = jnp.concatenate([same_ref[:, :e], other_ref[:, :e]], axis=0)
     dqt = query_terms(other_ref[:, :e], own_dscore[...])
     dqt_far = query_terms(keys, far_dscore[...])
@@ -288,8 +288,8 @@
         ]
     )
     pay_far = shift(pay, -4, -4, 2)
-    kv_same = send(kv, lambda m, c: near(m) if c == 0 else far(m))
-    kv_other = send(kv, lambda m, c: far(m) if c == 0 else near(m))
+    kv_same = send(kv, lambda m, c: near(m) if c == 1 else far(m))
+    kv_other = send(kv, lambda m, c: far(m) if c == 1 else near(m))
     pay_own = pair_gather(pay)
     unit = 5 * 2 * heads * rows * 2 * rows * e
     dqt, dkv_own = call(

time: 42.5 us -> 42.2 us (level)
  starting transfers between devices: 10.8 us -> 15.5 us
  blocking collectives: 18.4 us -> 13.8 us
  waiting for transfers between devices: 4.73 us -> 4.08 us
    ppermute x3, starting transfers between devices: 9.43 us -> 14.2 us  [send(): return lax.ppermute(x, 'ctx', moves)]
    all_gather x4, blocking collectives: 18.4 us -> 13.8 us  [pair_gather(): return lax.all_gather(x, 'ctx', axis=0, tiled=True, axis_index_groups=pairs)]
    ppermute x3, waiting for transfers between devices: 4.73 us -> 4.07 us  [send(): return lax.ppermute(x, 'ctx', moves)]
where the time goes in v8:
time: 42.2 us; the launch traced here: 41.6 us
  starting transfers between devices  15.5 us (37%)
  blocking collectives  13.8 us (33%)
  Pallas kernels  7.52 us (18%)
  waiting for transfers between devices  4.08 us (10%)
  between operations  0.74 us (2%)
    ppermute x3, starting transfers between devices, send(): return lax.ppermute(x, 'ctx', moves)  14.2 us
    all_gather x4, blocking collectives, pair_gather(): return lax.all_gather(x, 'ctx', axis=0, tiled=True, axis_index_groups=pairs)  13.8 us
    pallas_call x6, Pallas kernels, run(): pl.pallas_call(kernel, out_shape=[jax.ShapeDtypeStruct(s, d) for s, d in...  7.52 us
    ppermute x3, waiting for transfers between devices, send(): return lax.ppermute(x, 'ctx', moves)  4.07 us
    ppermute x2, starting transfers between devices, shift(): lax.ppermute(x, 'ctx', [(i, j) for i, j in moves if least <= i and least...  1.35 us
  transfers between devices with their start and end apart: 5, of which 1 were waited for; matrix products, arithmetic and copies ran while one was open for 0% of the time, Pallas kernels for 7%

profile of v8, /device:TPU:1, one launch (start us, length us, event | category | flops | bytes accessed | tf_op | source)
XLA Modules:
  0.0 41.6 jit_solution(9256718279873812834)
XLA Ops:
  0.6 1.2 %prep.1 = (bf16[528,256]{1,0:T(8,128)(2,1)S(1)}, bf16[256,256]{1,0:T(8,128)(2,1)S(1)}) custom-call(bf16[256,256]{1,0:T(8,128)(2,1)} %q_ref.1, bf16[256,256]{1,0:T(8,128)(2,1)} %go_ref.1, bf16[256,256]{1,0:T(8,128)(2,1)} %out_ref.1, f32[2,256]{1,0:T(2,128)} %norm_ref.1, bf16[256,128]{1,0:T(8,128)(2,1)} %k_ref.1, bf16[256,128]{1,0:T(8,128)(2,1)} %v_ref.1), custom_call_target="tpu_custom_call" | custom-call | bytes 526336 | tf_op jit(solution)/shard_map/prep/pallas_call | solution.py:233
  1.8 0.7 %collective-permute-start = (bf16[528,256]{1,0:T(8,128)(2,1)S(1)}, bf16[528,256]{1,0:T(8,128)(2,1)S(1)}, u32[]{:S(2)}, u32[]{:S(2)}) collective-permute-start(bf16[528,256]{1,0:T(8,128)(2,1)S(1)} %get-tuple-element.15), channel_id=1, source_target_pairs={{192,64},{224,96},{256,128},{288,160},{320,192},{352,224},{384,256... | collective-permute-start | bytes 811016 | tf_op jit(solution)/shard_map/ppermute | solution.py:269
  2.5 0.0 copy-start
  2.5 5.2 %collective-permute-start.2 = (bf16[256,256]{1,0:T(8,128)(2,1)S(1)}, bf16[256,256]{1,0:T(8,128)(2,1)S(1)}, u32[]{:S(2)}, u32[]{:S(2)}) collective-permute-start(bf16[256,256]{1,0:T(8,128)(2,1)S(1)} %get-tuple-element.16.kv_ref), channel_id=1, source_target_pairs={{0,128},{32,64},{64,224},{96,160},{128,256},{160,192},{192,352},{2... | collective-permute-start | bytes 393224 | tf_op jit(solution)/shard_map/ppermute | solution.py:259
  7.7 7.7 %collective-permute-start.1 = (bf16[256,256]{1,0:T(8,128)(2,1)S(1)}, bf16[256,256]{1,0:T(8,128)(2,1)S(1)}, u32[]{:S(2)}, u32[]{:S(2)}) collective-permute-start(bf16[256,256]{1,0:T(8,128)(2,1)S(1)} %get-tuple-element.16.kv_ref), channel_id=1, source_target_pairs={{0,64},{32,128},{64,160},{96,224},{128,192},{160,256},{192,288},{2... | collective-permute-start | bytes 393224 | tf_op jit(solution)/shard_map/ppermute | solution.py:259
  15.4 2.2 %all_gather.12.pay_ref.own_ref = bf16[1056,256]{1,0:T(8,128)(2,1)S(1)} all-gather(bf16[528,256]{1,0:T(8,128)(2,1)S(1)} %get-tuple-element.15), channel_id=1, replica_groups={{0,32},{64,96},{128,160},{192,224},{256,288},{320,352},{384,416},{448,4..., dimensions={0}, use_global_device_ids=true | all-gather | bytes 811008 | tf_op jit(solution)/shard_map/all_gather | solution.py:272
  17.6 0.0 copy-done
  17.6 1.4 %own.1 = (f32[512,256]{1,0:T(8,128)S(1)}, f32[256,256]{1,0:T(8,128)S(1)}) custom-call(s32[4]{0:T(128)S(1)} %copy-done, bf16[1056,256]{1,0:T(8,128)(2,1)S(1)} %all_gather.12.pay_ref.own_ref, bf16[256,256]{1,0:T(8,128)(2,1)S(1)} %get-tuple-element.16.kv_ref), custom_call_target="tpu_custom_call" | custom-call | flops 335544320 | bytes 671760 | tf_op jit(solution)/shard_map/own/pallas_call | solution.py:233
  19.1 0.0 collective-permute-done.2.same_ref
  19.1 1.4 %near.1 = (f32[512,256]{1,0:T(8,128)S(1)}, f32[256,256]{1,0:T(8,128)S(1)}) custom-call(s32[4]{0:T(128)S(1)} %copy-done, bf16[1056,256]{1,0:T(8,128)(2,1)S(1)} %all_gather.12.pay_ref.own_ref, bf16[256,256]{1,0:T(8,128)(2,1)S(1)} %collective-permute-done.2.same_ref, f32[512,256]{1,0:T(8,128)S(1)} %get-tuple-element.19.dqt_in_ref), custom_call_target="tpu_custom_call" | custom-call | flops 335544320 | bytes 1196048 | tf_op jit(solution)/shard_map/near/pallas_call | solution.py:233
  20.4 0.0 collective-permute-done.1.other_ref
  20.4 0.0 collective-permute-done
  20.5 2.2 %all_gather.13.far_ref = bf16[1056,256]{1,0:T(8,128)(2,1)S(1)} all-gather(bf16[528,256]{1,0:T(8,128)(2,1)S(1)} %collective-permute-done), channel_id=1, replica_groups={{0,32},{64,96},{128,160},{192,224},{256,288},{320,352},{384,416},{448,4..., dimensions={0}, use_global_device_ids=true | all-gather | bytes 811008 | tf_op jit(solution)/shard_map/all_gather | solution.py:272
  22.7 2.7 %cross.1 = (bf16[512,256]{1,0:T(8,128)(2,1)S(1)}, bf16[512,256]{1,0:T(8,128)(2,1)S(1)}, f32[256,256]{1,0:T(8,128)S(1)}, f32[256,256]{1,0:T(8,128)S(1)}) custom-call(s32[4]{0:T(128)S(1)} %copy-done, bf16[1056,256]{1,0:T(8,128)(2,1)S(1)} %all_gather.12.pay_ref.own_ref, bf16[1056,256]{1,0:T(8,128)(2,1)S(1)} %all_gather.13.far_ref, ...), custom_call_target="tpu_custom_call" | custom-call | flops 1006632960 | bytes 2129936 | tf_op jit(solution)/shard_map/cross/pallas_call | solution.py:233
  25.4 1.3 %collective-permute-start.3 = (bf16[512,256]{1,0:T(8,128)(2,1)S(1)}, bf16[512,256]{1,0:T(8,128)(2,1)S(1)}, u32[]{:S(2)}, u32[]{:S(2)}) collective-permute-start(bf16[512,256]{1,0:T(8,128)(2,1)S(1)} %get-tuple-element.25), channel_id=1, source_target_pairs={{64,32},{128,0},{160,64},{192,160},{224,96},{256,128},{288,192},{3... | collective-permute-start | bytes 786440 | tf_op jit(solution)/shard_map/ppermute | solution.py:259
  26.7 2.2 %all_gather.14.both_ref = bf16[1024,256]{1,0:T(8,128)(2,1)S(1)} all-gather(bf16[512,256]{1,0:T(8,128)(2,1)S(1)} %get-tuple-element.23), channel_id=1, replica_groups={{0,32},{64,96},{128,160},{192,224},{256,288},{320,352},{384,416},{448,4..., dimensions={0}, use_global_device_ids=true | all-gather | bytes 786432 | tf_op jit(solution)/shard_map/all_gather | solution.py:272
  28.9 0.7 %collective-permute-start.4 = (bf16[256,256]{1,0:T(8,128)(2,1)S(1)}, bf16[256,256]{1,0:T(8,128)(2,1)S(1)}, u32[]{:S(2)}, u32[]{:S(2)}) collective-permute-start(bf16[256,256]{1,0:T(8,128)(2,1)S(1)} %pair.1), channel_id=1, source_target_pairs={{64,192},{96,224},{128,256},{160,288},{192,320},{224,352},{256,384... | collective-permute-start | bytes 393224 | tf_op jit(solution)/shard_map/ppermute | solution.py:269
  29.6 4.1 %collective-permute-done.3 = bf16[512,256]{1,0:T(8,128)(2,1)S(1)} collective-permute-done((bf16[512,256]{1,0:T(8,128)(2,1)S(1)}, bf16[512,256]{1,0:T(8,128)(2,1)S(1)}, u32[]{:S(2)}, u32[]{:S(2)}) %collective-permute-start.3) | collective-permute-done | bytes 262176 | tf_op jit(solution)/shard_map/ppermute | solution.py:259
  33.6 7.2 %all_gather.15.back_ref = bf16[1024,256]{1,0:T(8,128)(2,1)S(1)} all-gather(bf16[512,256]{1,0:T(8,128)(2,1)S(1)} %collective-permute-done.3), channel_id=1, replica_groups={{0,32},{64,96},{128,160},{192,224},{256,288},{320,352},{384,416},{448,4..., dimensions={0}, use_global_device_ids=true | all-gather | bytes 786432 | tf_op jit(solution)/shard_map/all_gather | solution.py:272
  40.8 0.0 collective-permute-done.4.dqt_back_ref
  40.8 0.8 %final.1 = (bf16[256,256]{1,0:T(8,128)(2,1)}, bf16[256,128]{1,0:T(8,128)(2,1)}, bf16[256,128]{1,0:T(8,128)(2,1)}) custom-call(f32[256,256]{1,0:T(8,128)S(1)} %get-tuple-element.22.keep_ref, bf16[1024,256]{1,0:T(8,128)(2,1)S(1)} %all_gather.14.both_ref, f32[256,256]{1,0:T(8,128)S(1)} %get-tuple-element.24.dkv_ref, bf16[1024,256]{1,0:T(8,128)(2,1)S(1)} %all_gather.15.back_ref, ...), custom_call_target="tpu_custom_call" | custom-call | bytes 1703936 | tf_op jit(solution)/shard_map/final/pallas_call | solution.py:233
  (1 shorter events, 0.0 us)
Async XLA Ops:
  1.8 18.6 %collective-permute-start = (bf16[528,256]{1,0:T(8,128)(2,1)S(1)}, bf16[528,256]{1,0:T(8,128)(2,1)S(1)}, u32[]{:S(2)}, u32[]{:S(2)}) collective-permute-start(bf16[528,256]{1,0:T(8,128)(2,1)S(1)} %get-tuple-element.15), channel_id=1, source_target_pairs={{192,64},{224,96},{256,128},{288,160},{320,192},{352,224},{384,256... | collective-permute-start | bytes 811016 | tf_op jit(solution)/shard_map/ppermute | solution.py:269
  2.5 15.1 %copy-start = (s32[4]{0:T(128)S(1)}, s32[4]{0:T(128)}, u32[]{:S(2)}) copy-start(s32[4]{0:T(128)} %lens_ref.5) | copy-start | bytes 52
  2.5 16.5 %collective-permute-start.2 = (bf16[256,256]{1,0:T(8,128)(2,1)S(1)}, bf16[256,256]{1,0:T(8,128)(2,1)S(1)}, u32[]{:S(2)}, u32[]{:S(2)}) collective-permute-start(bf16[256,256]{1,0:T(8,128)(2,1)S(1)} %get-tuple-element.16.kv_ref), channel_id=1, source_target_pairs={{0,128},{32,64},{64,224},{96,160},{128,256},{160,192},{192,352},{2... | collective-permute-start | bytes 393224 | tf_op jit(solution)/shard_map/ppermute | solution.py:259
  7.7 12.7 %collective-permute-start.1 = (bf16[256,256]{1,0:T(8,128)(2,1)S(1)}, bf16[256,256]{1,0:T(8,128)(2,1)S(1)}, u32[]{:S(2)}, u32[]{:S(2)}) collective-permute-start(bf16[256,256]{1,0:T(8,128)(2,1)S(1)} %get-tuple-element.16.kv_ref), channel_id=1, source_target_pairs={{0,64},{32,128},{64,160},{96,224},{128,192},{160,256},{192,288},{2... | collective-permute-start | bytes 393224 | tf_op jit(solution)/shard_map/ppermute | solution.py:259
  25.4 8.3 %collective-permute-start.3 = (bf16[512,256]{1,0:T(8,128)(2,1)S(1)}, bf16[512,256]{1,0:T(8,128)(2,1)S(1)}, u32[]{:S(2)}, u32[]{:S(2)}) collective-permute-start(bf16[512,256]{1,0:T(8,128)(2,1)S(1)} %get-tuple-element.25), channel_id=1, source_target_pairs={{64,32},{128,0},{160,64},{192,160},{224,96},{256,128},{288,192},{3... | collective-permute-start | bytes 786440 | tf_op jit(solution)/shard_map/ppermute | solution.py:259
  28.9 11.9 %collective-permute-start.4 = (bf16[256,256]{1,0:T(8,128)(2,1)S(1)}, bf16[256,256]{1,0:T(8,128)(2,1)S(1)}, u32[]{:S(2)}, u32[]{:S(2)}) collective-permute-start(bf16[256,256]{1,0:T(8,128)(2,1)S(1)} %pair.1), channel_id=1, source_target_pairs={{64,192},{96,224},{128,256},{160,288},{192,320},{224,352},{256,384... | collective-permute-start | bytes 393224 | tf_op jit(solution)/shard_map/ppermute | solution.py:269

commit v9 on v8

--- a/solution.py
+++ b/solution.py
@@ -183,11 +183,12 @@
     far_prob, far_dscore = prob_ref.at[:, half:], dscore_ref.at[:, half:]
     own_prob, own_dscore = prob_ref.at[rows:, :half], dscore_ref.at[rows:, :half]
     firsts = [first + (2 - back) * rows, first + (back - 1) * rows]
+    fill(own, [other_ref[...]], firsts[1:], False, own_prob, own_dscore)
     fill(far, [same_ref[...], other_ref[...]], firsts, False, far_prob, far_dscore)
-    fill(own, [other_ref[...]], firsts[1:], False, own_prob, own_dscore)
+    own_terms = key_terms(own, pl.ds(0, rows), own_prob, own_dscore)
     terms = key_terms(far, pl.ds(0, 2 * rows), far_prob, far_dscore)
     same = terms[:rows] + dkv_in_ref[...]
-    other = terms[rows:] + key_terms(own, pl.ds(0, rows), own_prob, own_dscore)
+    other = terms[rows:] + own_terms
     dkv_ref[pl.ds(pl.multiple_of((2 - back) * rows, rows), rows), :] = same.astype(jnp.bfloat16)
     dkv_ref[pl.ds(pl.multiple_of((back - 1) * rows, rows), rows), :] = other.astype(jnp.bfloat16)
     keys = jnp.concatenate([same_ref[:, :e], other_ref[:, :e]], axis=0)

time: 42.2 us -> 42.2 us (level)
  no operation moved by 1% of the time
where the time goes in v9:
time: 42.2 us; the launch traced here: 41.6 us
  starting transfers between devices  15.5 us (37%)
  blocking collectives  13.8 us (33%)
  Pallas kernels  7.53 us (18%)
  waiting for transfers between devices  4.07 us (10%)
  between operations  0.74 us (2%)
    ppermute x3, starting transfers between devices, send(): return lax.ppermute(x, 'ctx', moves)  14.2 us
    all_gather x4, blocking collectives, pair_gather(): return lax.all_gather(x, 'ctx', axis=0, tiled=True, axis_index_groups=pairs)  13.8 us
    pallas_call x6, Pallas kernels, run(): pl.pallas_call(kernel, out_shape=[jax.ShapeDtypeStruct(s, d) for s, d in...  7.53 us
    ppermute x3, waiting for transfers between devices, send(): return lax.ppermute(x, 'ctx', moves)  4.07 us
    ppermute x2, starting transfers between devices, shift(): lax.ppermute(x, 'ctx', [(i, j) for i, j in moves if least <= i and least...  1.35 us
  transfers between devices with their start and end apart: 5, of which 1 were waited for; matrix products, arithmetic and copies ran while one was open for 0% of the time, Pallas kernels for 7%

profile of v9, /device:TPU:1, one launch (start us, length us, event | category | flops | bytes accessed | tf_op | source)
XLA Modules:
  0.0 41.6 jit_solution(4501164458972819331)
XLA Ops:
  0.6 1.2 %prep.1 = (bf16[528,256]{1,0:T(8,128)(2,1)S(1)}, bf16[256,256]{1,0:T(8,128)(2,1)S(1)}) custom-call(bf16[256,256]{1,0:T(8,128)(2,1)} %q_ref.1, bf16[256,256]{1,0:T(8,128)(2,1)} %go_ref.1, bf16[256,256]{1,0:T(8,128)(2,1)} %out_ref.1, f32[2,256]{1,0:T(2,128)} %norm_ref.1, bf16[256,128]{1,0:T(8,128)(2,1)} %k_ref.1, bf16[256,128]{1,0:T(8,128)(2,1)} %v_ref.1), custom_call_target="tpu_custom_call" | custom-call | bytes 526336 | tf_op jit(solution)/shard_map/prep/pallas_call | solution.py:234
  1.8 0.7 %collective-permute-start = (bf16[528,256]{1,0:T(8,128)(2,1)S(1)}, bf16[528,256]{1,0:T(8,128)(2,1)S(1)}, u32[]{:S(2)}, u32[]{:S(2)}) collective-permute-start(bf16[528,256]{1,0:T(8,128)(2,1)S(1)} %get-tuple-element.15), channel_id=1, source_target_pairs={{192,64},{224,96},{256,128},{288,160},{320,192},{352,224},{384,256... | collective-permute-start | bytes 811016 | tf_op jit(solution)/shard_map/ppermute | solution.py:270
  2.5 0.0 copy-start
  2.5 5.2 %collective-permute-start.2 = (bf16[256,256]{1,0:T(8,128)(2,1)S(1)}, bf16[256,256]{1,0:T(8,128)(2,1)S(1)}, u32[]{:S(2)}, u32[]{:S(2)}) collective-permute-start(bf16[256,256]{1,0:T(8,128)(2,1)S(1)} %get-tuple-element.16.kv_ref), channel_id=1, source_target_pairs={{0,128},{32,64},{64,224},{96,160},{128,256},{160,192},{192,352},{2... | collective-permute-start | bytes 393224 | tf_op jit(solution)/shard_map/ppermute | solution.py:260
  7.7 7.7 %collective-permute-start.1 = (bf16[256,256]{1,0:T(8,128)(2,1)S(1)}, bf16[256,256]{1,0:T(8,128)(2,1)S(1)}, u32[]{:S(2)}, u32[]{:S(2)}) collective-permute-start(bf16[256,256]{1,0:T(8,128)(2,1)S(1)} %get-tuple-element.16.kv_ref), channel_id=1, source_target_pairs={{0,64},{32,128},{64,160},{96,224},{128,192},{160,256},{192,288},{2... | collective-permute-start | bytes 393224 | tf_op jit(solution)/shard_map/ppermute | solution.py:260
  15.4 2.2 %all_gather.12.pay_ref.own_ref = bf16[1056,256]{1,0:T(8,128)(2,1)S(1)} all-gather(bf16[528,256]{1,0:T(8,128)(2,1)S(1)} %get-tuple-element.15), channel_id=1, replica_groups={{0,32},{64,96},{128,160},{192,224},{256,288},{320,352},{384,416},{448,4..., dimensions={0}, use_global_device_ids=true | all-gather | bytes 811008 | tf_op jit(solution)/shard_map/all_gather | solution.py:273
  17.6 0.0 copy-done
  17.6 1.4 %own.1 = (f32[512,256]{1,0:T(8,128)S(1)}, f32[256,256]{1,0:T(8,128)S(1)}) custom-call(s32[4]{0:T(128)S(1)} %copy-done, bf16[1056,256]{1,0:T(8,128)(2,1)S(1)} %all_gather.12.pay_ref.own_ref, bf16[256,256]{1,0:T(8,128)(2,1)S(1)} %get-tuple-element.16.kv_ref), custom_call_target="tpu_custom_call" | custom-call | flops 335544320 | bytes 671760 | tf_op jit(solution)/shard_map/own/pallas_call | solution.py:234
  19.1 0.0 collective-permute-done.2.same_ref
  19.1 1.4 %near.1 = (f32[512,256]{1,0:T(8,128)S(1)}, f32[256,256]{1,0:T(8,128)S(1)}) custom-call(s32[4]{0:T(128)S(1)} %copy-done, bf16[1056,256]{1,0:T(8,128)(2,1)S(1)} %all_gather.12.pay_ref.own_ref, bf16[256,256]{1,0:T(8,128)(2,1)S(1)} %collective-permute-done.2.same_ref, f32[512,256]{1,0:T(8,128)S(1)} %get-tuple-element.19.dqt_in_ref), custom_call_target="tpu_custom_call" | custom-call | flops 335544320 | bytes 1196048 | tf_op jit(solution)/shard_map/near/pallas_call | solution.py:234
  20.4 0.0 collective-permute-done.1.other_ref
  20.4 0.0 collective-permute-done
  20.5 2.2 %all_gather.13.far_ref = bf16[1056,256]{1,0:T(8,128)(2,1)S(1)} all-gather(bf16[528,256]{1,0:T(8,128)(2,1)S(1)} %collective-permute-done), channel_id=1, replica_groups={{0,32},{64,96},{128,160},{192,224},{256,288},{320,352},{384,416},{448,4..., dimensions={0}, use_global_device_ids=true | all-gather | bytes 811008 | tf_op jit(solution)/shard_map/all_gather | solution.py:273
  22.7 2.7 %cross.1 = (bf16[512,256]{1,0:T(8,128)(2,1)S(1)}, bf16[512,256]{1,0:T(8,128)(2,1)S(1)}, f32[256,256]{1,0:T(8,128)S(1)}, f32[256,256]{1,0:T(8,128)S(1)}) custom-call(s32[4]{0:T(128)S(1)} %copy-done, bf16[1056,256]{1,0:T(8,128)(2,1)S(1)} %all_gather.12.pay_ref.own_ref, bf16[1056,256]{1,0:T(8,128)(2,1)S(1)} %all_gather.13.far_ref, ...), custom_call_target="tpu_custom_call" | custom-call | flops 1006632960 | bytes 2129936 | tf_op jit(solution)/shard_map/cross/pallas_call | solution.py:234
  25.4 1.3 %collective-permute-start.3 = (bf16[512,256]{1,0:T(8,128)(2,1)S(1)}, bf16[512,256]{1,0:T(8,128)(2,1)S(1)}, u32[]{:S(2)}, u32[]{:S(2)}) collective-permute-start(bf16[512,256]{1,0:T(8,128)(2,1)S(1)} %get-tuple-element.25), channel_id=1, source_target_pairs={{64,32},{128,0},{160,64},{192,160},{224,96},{256,128},{288,192},{3... | collective-permute-start | bytes 786440 | tf_op jit(solution)/shard_map/ppermute | solution.py:260
  26.7 2.2 %all_gather.14.both_ref = bf16[1024,256]{1,0:T(8,128)(2,1)S(1)} all-gather(bf16[512,256]{1,0:T(8,128)(2,1)S(1)} %get-tuple-element.23), channel_id=1, replica_groups={{0,32},{64,96},{128,160},{192,224},{256,288},{320,352},{384,416},{448,4..., dimensions={0}, use_global_device_ids=true | all-gather | bytes 786432 | tf_op jit(solution)/shard_map/all_gather | solution.py:273
  28.9 0.7 %collective-permute-start.4 = (bf16[256,256]{1,0:T(8,128)(2,1)S(1)}, bf16[256,256]{1,0:T(8,128)(2,1)S(1)}, u32[]{:S(2)}, u32[]{:S(2)}) collective-permute-start(bf16[256,256]{1,0:T(8,128)(2,1)S(1)} %pair.1), channel_id=1, source_target_pairs={{64,192},{96,224},{128,256},{160,288},{192,320},{224,352},{256,384... | collective-permute-start | bytes 393224 | tf_op jit(solution)/shard_map/ppermute | solution.py:270
  29.6 4.1 %collective-permute-done.3 = bf16[512,256]{1,0:T(8,128)(2,1)S(1)} collective-permute-done((bf16[512,256]{1,0:T(8,128)(2,1)S(1)}, bf16[512,256]{1,0:T(8,128)(2,1)S(1)}, u32[]{:S(2)}, u32[]{:S(2)}) %collective-permute-start.3) | collective-permute-done | bytes 262176 | tf_op jit(solution)/shard_map/ppermute | solution.py:260
  33.6 7.2 %all_gather.15.back_ref = bf16[1024,256]{1,0:T(8,128)(2,1)S(1)} all-gather(bf16[512,256]{1,0:T(8,128)(2,1)S(1)} %collective-permute-done.3), channel_id=1, replica_groups={{0,32},{64,96},{128,160},{192,224},{256,288},{320,352},{384,416},{448,4..., dimensions={0}, use_global_device_ids=true | all-gather | bytes 786432 | tf_op jit(solution)/shard_map/all_gather | solution.py:273
  40.8 0.0 collective-permute-done.4.dqt_back_ref
  40.8 0.8 %final.1 = (bf16[256,256]{1,0:T(8,128)(2,1)}, bf16[256,128]{1,0:T(8,128)(2,1)}, bf16[256,128]{1,0:T(8,128)(2,1)}) custom-call(f32[256,256]{1,0:T(8,128)S(1)} %get-tuple-element.22.keep_ref, bf16[1024,256]{1,0:T(8,128)(2,1)S(1)} %all_gather.14.both_ref, f32[256,256]{1,0:T(8,128)S(1)} %get-tuple-element.24.dkv_ref, bf16[1024,256]{1,0:T(8,128)(2,1)S(1)} %all_gather.15.back_ref, ...), custom_call_target="tpu_custom_call" | custom-call | bytes 1703936 | tf_op jit(solution)/shard_map/final/pallas_call | solution.py:234
  (1 shorter events, 0.0 us)
Async XLA Ops:
  1.8 18.6 %collective-permute-start = (bf16[528,256]{1,0:T(8,128)(2,1)S(1)}, bf16[528,256]{1,0:T(8,128)(2,1)S(1)}, u32[]{:S(2)}, u32[]{:S(2)}) collective-permute-start(bf16[528,256]{1,0:T(8,128)(2,1)S(1)} %get-tuple-element.15), channel_id=1, source_target_pairs={{192,64},{224,96},{256,128},{288,160},{320,192},{352,224},{384,256... | collective-permute-start | bytes 811016 | tf_op jit(solution)/shard_map/ppermute | solution.py:270
  2.5 15.1 %copy-start = (s32[4]{0:T(128)S(1)}, s32[4]{0:T(128)}, u32[]{:S(2)}) copy-start(s32[4]{0:T(128)} %lens_ref.5) | copy-start | bytes 52
  2.5 16.5 %collective-permute-start.2 = (bf16[256,256]{1,0:T(8,128)(2,1)S(1)}, bf16[256,256]{1,0:T(8,128)(2,1)S(1)}, u32[]{:S(2)}, u32[]{:S(2)}) collective-permute-start(bf16[256,256]{1,0:T(8,128)(2,1)S(1)} %get-tuple-element.16.kv_ref), channel_id=1, source_target_pairs={{0,128},{32,64},{64,224},{96,160},{128,256},{160,192},{192,352},{2... | collective-permute-start | bytes 393224 | tf_op jit(solution)/shard_map/ppermute | solution.py:260
  7.7 12.7 %collective-permute-start.1 = (bf16[256,256]{1,0:T(8,128)(2,1)S(1)}, bf16[256,256]{1,0:T(8,128)(2,1)S(1)}, u32[]{:S(2)}, u32[]{:S(2)}) collective-permute-start(bf16[256,256]{1,0:T(8,128)(2,1)S(1)} %get-tuple-element.16.kv_ref), channel_id=1, source_target_pairs={{0,64},{32,128},{64,160},{96,224},{128,192},{160,256},{192,288},{2... | collective-permute-start | bytes 393224 | tf_op jit(solution)/shard_map/ppermute | solution.py:260
  25.4 8.3 %collective-permute-start.3 = (bf16[512,256]{1,0:T(8,128)(2,1)S(1)}, bf16[512,256]{1,0:T(8,128)(2,1)S(1)}, u32[]{:S(2)}, u32[]{:S(2)}) collective-permute-start(bf16[512,256]{1,0:T(8,128)(2,1)S(1)} %get-tuple-element.25), channel_id=1, source_target_pairs={{64,32},{128,0},{160,64},{192,160},{224,96},{256,128},{288,192},{3... | collective-permute-start | bytes 786440 | tf_op jit(solution)/shard_map/ppermute | solution.py:260
  28.9 11.9 %collective-permute-start.4 = (bf16[256,256]{1,0:T(8,128)(2,1)S(1)}, bf16[256,256]{1,0:T(8,128)(2,1)S(1)}, u32[]{:S(2)}, u32[]{:S(2)}) collective-permute-start(bf16[256,256]{1,0:T(8,128)(2,1)S(1)} %pair.1), channel_id=1, source_target_pairs={{64,192},{96,224},{128,256},{160,288},{192,320},{224,352},{256,384... | collective-permute-start | bytes 393224 | tf_op jit(solution)/shard_map/ppermute | solution.py:270
